TPU v7x, 256 devices: a whole 4x4x8 slice. The times are simulated.
256 devices in a mesh: group: 8 (over x, core), tensor: 8 (over z), rep: 4 (over y).
Axes of the slice: x: 4, y: 4, z: 8, core: 2. Of those that a mesh axis runs over, the one named last changes fastest.
Arguments:
- probe_vectors: bfloat16 [512, 64, 128], P(('group', 'rep'), 'tensor'), may hold values from -500 to 500
- stored_lookup_vectors: bfloat16 [512, 8, 512, 128], P(('group', 'rep'), 'tensor'), may hold values from -6 to 6
- stored_content_vectors: bfloat16 [512, 8, 512, 128], P(('group', 'rep'), 'tensor'), may hold values from -6 to 6
- fresh_lookup_vector: bfloat16 [512, 8, 128], P(('group', 'rep'), 'tensor'), may hold values from -6 to 6
- fresh_content_vector: bfloat16 [512, 8, 128], P(('group', 'rep'), 'tensor'), may hold values from -6 to 6
- history_counts: int32 [512], P(('group', 'rep')), may hold values from 1 to 512, as said below
- mixing_matrix: bfloat16 [8192, 8192], P('tensor', ('group', 'rep')), may hold values from -0.25 to 0.25
- skip_stream: bfloat16 [512, 8192], P(('group', 'rep'), 'tensor'), may hold values from -8 to 8
- closing_multiplier: bfloat16 [8192], P('tensor'), may hold values from 0.25 to 1.75
- lexicon_matrix: bfloat16 [8192, 131072], P(None, ('group', 'tensor', 'rep')), may hold values from -0.088388348 to 0.088388348
- sharpening_factor: float32 [512], replicated, may hold values from 0.5 to 20
- desired_perplexity: float32 [512], replicated, may hold values from 6 to 12
- chosen_symbols: int32 [512], replicated, may hold values from 0 to 131071
Outputs:
- hidden: bfloat16 [512, 8192], P(('group', 'rep'), 'tensor')
- next_targets: float32 [512], replicated
- surprise: float32 [512], replicated
Inputs may be any that keep to these rules, and one draw needn't show every extreme that they name: `history_counts`: each row holds at least one cached position; some row holds 512.
All inputs are finite; a program needn't handle non-finite values.
Results may differ from a plain program's by a relative error of at most 0.0063.
Values may be sent and summed in bfloat16 or wider, within the bound.
No kernel may reach another device: no remote copies, remote signals or barrier semaphores. Data moves between devices by JAX's collectives and lax.ppermute only.
A program may use at most 128 MiB of HBM per device.

v0:
```python
import math

import jax
import jax.numpy as jnp
from jax import lax
from jax.sharding import PartitionSpec as P

cut_slope = 4.0


def attend(
    probe_vectors,
    stored_lookup_vectors,
    stored_content_vectors,
    fresh_lookup_vector,
    fresh_content_vector,
    history_counts,
):
    rows, kv_local, cache_len, head_dim = stored_lookup_vectors.shape
    heads_local = probe_vectors.shape[1]
    grouped_query_rows = probe_vectors.reshape(rows, kv_local, heads_local // kv_local, head_dim)
    score_scale = 1.0 / math.sqrt(head_dim)
    self_entry = (
        jnp.einsum(
            "mjqo,mjo->mjq",
            grouped_query_rows,
            fresh_lookup_vector,
            preferred_element_type=jnp.float32,
        )
        * score_scale
    )
    scores = (
        jnp.einsum(
            "bkgd,bkld->bkgl",
            grouped_query_rows,
            stored_lookup_vectors,
            preferred_element_type=jnp.float32,
        )
        * score_scale
    )
    position = lax.broadcasted_iota(jnp.int32, (1, 1, 1, cache_len), 3)
    live = position < history_counts[:, None, None, None]
    top = jnp.maximum(jnp.max(jnp.where(live, scores, -1e30), axis=3), self_entry)
    expo = jnp.where(live, jnp.exp(scores - top[..., None]), 0.0)
    total = jnp.sum(expo, axis=3)
    accum = jnp.einsum(
        "bkgl,bkld->bkgd",
        expo.astype(jnp.bfloat16),
        stored_content_vectors,
        preferred_element_type=jnp.float32,
    )
    own_expo = jnp.exp(self_entry - top)
    total = total + own_expo
    accum = accum + jnp.einsum(
        "vct,vcn->vctn",
        own_expo.astype(jnp.bfloat16),
        fresh_content_vector,
        preferred_element_type=jnp.float32,
    )
    return (accum / total[..., None]).reshape(rows, heads_local * head_dim).astype(jnp.bfloat16)


def shards(
    probe_vectors,
    stored_lookup_vectors,
    stored_content_vectors,
    fresh_lookup_vector,
    fresh_content_vector,
    history_counts,
    mixing_matrix,
    skip_stream,
    closing_multiplier,
    lexicon_matrix,
    sharpening_factor,
    desired_perplexity,
    chosen_symbols,
):
    attn = attend(
        probe_vectors,
        stored_lookup_vectors,
        stored_content_vectors,
        fresh_lookup_vector,
        fresh_content_vector,
        history_counts,
    )
    every_attn = lax.all_gather(attn, ("group", "rep"), axis=0, tiled=True)
    partial_cols = jnp.dot(every_attn, mixing_matrix, preferred_element_type=jnp.float32)
    terms = lax.all_to_all(partial_cols, ("group", "rep"), split_axis=0, concat_axis=1, tiled=True)
    summed = lax.psum_scatter(terms, "tensor", scatter_dimension=1, tiled=True)
    hidden = (skip_stream.astype(jnp.float32) + summed).astype(jnp.bfloat16)
    wide = hidden.astype(jnp.float32)
    squares = lax.psum(jnp.sum(wide * wide, axis=1), "tensor")
    width = wide.shape[1] * lax.axis_size("tensor")
    rescaled_stream = (
        wide * lax.rsqrt(squares / width + 1e-05)[:, None] * closing_multiplier.astype(jnp.float32)
    ).astype(jnp.bfloat16)
    features = lax.all_gather(rescaled_stream, "tensor", axis=1, tiled=True)
    unnormalized_odds = (
        jnp.dot(
            lax.all_gather(features, ("group", "rep"), axis=0, tiled=True),
            lexicon_matrix,
            preferred_element_type=jnp.float32,
        )
        * sharpening_factor[:, None]
    )
    vocab_local = lexicon_matrix.shape[1]
    offset = lax.axis_index(("group", "tensor", "rep")) * vocab_local
    entry_ids = offset + lax.broadcasted_iota(jnp.int32, (1, vocab_local), 1)
    token_part = jnp.sum(
        jnp.where(entry_ids == chosen_symbols[:, None], unnormalized_odds, 0.0), axis=1
    )
    top = lax.pmax(jnp.max(unnormalized_odds, axis=1), ("group", "tensor", "rep"))
    local_total = jnp.sum(jnp.exp(unnormalized_odds - top[:, None]), axis=1)
    total, token_logit = lax.psum((local_total, token_part), ("group", "tensor", "rep"))
    lognorm = top + jnp.log(total)
    logp = unnormalized_odds - lognorm[:, None]
    bits = -logp / math.log(2.0)
    logw = logp + jax.nn.log_sigmoid(cut_slope * (desired_perplexity[:, None] - bits))
    kept = lax.psum(jnp.sum(jnp.exp(logw), axis=1), ("group", "tensor", "rep"))
    token_logp = token_logit - lognorm
    token_logw = token_logp + jax.nn.log_sigmoid(
        cut_slope * (desired_perplexity + token_logp / math.log(2.0))
    )
    surprise = -(token_logw - jnp.log(kept)) / math.log(2.0)
    next_targets = desired_perplexity - 0.1 * (surprise - 5.0)
    return (hidden, next_targets, surprise)


def solution(mesh):
    placed = (
        P(("group", "rep"), "tensor", None),
        P(("group", "rep"), "tensor", None, None),
        P(("group", "rep"), "tensor", None, None),
        P(("group", "rep"), "tensor", None),
        P(("group", "rep"), "tensor", None),
        P(("group", "rep")),
        P("tensor", ("group", "rep")),
        P(("group", "rep"), "tensor"),
        P("tensor"),
        P(None, ("group", "tensor", "rep")),
        P(),
        P(),
        P(),
    )
    return jax.shard_map(
        shards,
        mesh=mesh,
        in_specs=placed,
        out_specs=(P(("group", "rep"), "tensor"), P(), P()),
        check_vma=False,
    )
```

profile of v0, /device:TPU:1, one launch (start us, length us, event | category | flops | bytes accessed | tf_op | source)
XLA Modules:
  0.0 465.4 jit_solution(7517380844080763561)
XLA Ops:
  7.2 0.0 copy-start
  7.2 0.0 copy-start.3
  7.2 0.0 copy-start.2
  7.2 0.0 copy-start.5
  7.2 0.0 all-gather.3.cloned.1.call-start
  7.3 0.9 iota_compare_fusion
  8.1 0.9 fusion.29
  9.0 0.0 copy-done
  9.0 1.5 select_reduce_fusion.1
  10.5 0.2 fusion.20
  10.7 0.7 bitcast_convert_fusion
  11.4 2.0 fusion.13
  13.5 0.6 copy.24
  14.1 0.0 all-gather.3.cloned.1.call-update
  14.1 0.0 reduce-scatter.2.cloned.1.call-start
  14.2 52.2 %all-gather.3.cloned.1.call-done = bf16[512,1024]{1,0:T(8,128)(2,1)} async-done(((bf16[16,1024]{1,0:T(8,128)(2,1)}), bf16[512,1024]{1,0:T(8,128)(2,1)}) %all-gather.3.cloned.1.call-update) | async-done | bytes 1048592 | tf_op jit(solution)/shard_map/all_gather | solution.py:86
  66.3 1.8 fusion.40
  68.1 16.0 %all_to_all.19 = f32[32,16,256]{2,1,0:T(8,128)S(1)} all-to-all(f32[32,16,256]{2,1,0:T(8,128)S(1)} %bitcast.39), channel_id=1, replica_groups=mesh['group'=8,'tensor'=8,'rep'=4] {'group','rep'}, dimensions={0} | all-to-all | bytes 1048576 | tf_op jit(solution)/shard_map/all_to_all | solution.py:88
  84.2 0.8 copy.19
  85.0 0.0 reduce-scatter.2.cloned.1.call-update
  85.0 0.0 all-gather.5.cloned.1.call-start
  85.1 0.0 copy-done.3
  85.1 30.9 %reduce-scatter.2.cloned.1.call-done = f32[16,1024]{1,0:T(8,128)} async-done(((f32[16,8192]{1,0:T(8,128)}), f32[16,1024]{1,0:T(8,128)}) %reduce-scatter.2.cloned.1.call-update) | async-done | bytes 65552 | tf_op jit(solution)/shard_map/reduce_scatter | solution.py:89
  116.0 0.0 copy-done.2
  116.0 1.0 fusion.26
  117.0 0.0 copy-start.1
  117.0 12.0 %psum.28 = f32[16]{0:T(128)S(1)} all-reduce(f32[16]{0:T(128)S(1)} %get-tuple-element.9), channel_id=1, replica_groups=mesh['group'=8,'tensor'=8,'rep'=4] {'tensor'}, use_global_device_ids=true, to_apply=%region_4.5 | all-reduce | flops 16 | bytes 128 | tf_op jit(solution)/shard_map/psum | solution.py:92
  128.9 0.1 fusion.28
  129.0 20.6 %all_gather.10 = bf16[16,8192]{1,0:T(8,128)(2,1)} all-gather(bf16[16,1024]{1,0:T(8,128)(2,1)S(1)} %fusion.28), channel_id=1, replica_groups=mesh['group'=8,'tensor'=8,'rep'=4] {'tensor'}, dimensions={1}, use_global_device_ids=true | all-gather | bytes 294912 | tf_op jit(solution)/shard_map/all_gather | solution.py:97
  149.6 0.0 all-gather.5.cloned.1.call-update
  149.7 0.0 copy-start.4
  149.7 0.0 copy-start.6
  149.7 72.8 %all-gather.5.cloned.1.call-done = bf16[512,8192]{1,0:T(8,128)(2,1)} async-done(((bf16[16,8192]{1,0:T(8,128)(2,1)}), bf16[512,8192]{1,0:T(8,128)(2,1)}) %all-gather.5.cloned.1.call-update) | async-done | bytes 8388624 | tf_op jit(solution)/shard_map/all_gather | solution.py:100
  222.5 0.0 copy-done.5
  222.5 10.9 %fusion.39 = (f32[512]{0:T(512)S(1)}, f32[512,512]{0,1:T(8,128)S(1)}) fusion(f32[512]{0:T(512)S(1)} %copy-done.5, bf16[512,8192]{1,0:T(8,128)(2,1)} %all-gather.5.cloned.1.call-done, bf16[8192,512]{1,0:T(8,128)(2,1)} %param.22), kind=kOutput, calls=%fused_computation.49 | convolution fusion | flops 4295491072 | bytes 17829888 | tf_op jit(solution)/shard_map/dot_general | solution.py:99
  233.4 0.0 copy-done.1
  233.4 75.8 %pmax.7 = f32[512]{0:T(512)S(1)} all-reduce(f32[512]{0:T(512)S(1)} %get-tuple-element.15), channel_id=1, replica_groups=mesh['group'=8,'tensor'=8,'rep'=4] {'group','tensor','rep'}, use_global_device_ids=true, to_apply=%region_8.9 | all-reduce | flops 512 | bytes 4096 | tf_op jit(solution)/shard_map/pmax | solution.py:112
  309.2 0.2 exponential_reduce_fusion
  309.4 74.3 %psum.30 = f32[512]{0:T(512)S(1)} all-reduce(f32[512]{0:T(512)S(1)} %exponential_reduce_fusion), channel_id=1, replica_groups=mesh['group'=8,'tensor'=8,'rep'=4] {'group','tensor','rep'}, use_global_device_ids=true, to_apply=%region_10.11 | all-reduce | flops 512 | bytes 4096 | tf_op jit(solution)/shard_map/psum | solution.py:114
  383.7 0.0 copy-done.4
  383.7 0.0 copy-done.6
  383.7 1.1 select_reduce_fusion
  384.8 73.4 %all-reduce = (f32[512]{0:T(512)S(1)}, f32[512]{0:T(512)S(1)}) all-reduce(f32[512]{0:T(512)S(1)} %get-tuple-element.4, f32[512]{0:T(512)S(1)} %get-tuple-element.3), channel_id=1, replica_groups=mesh['group'=8,'tensor'=8,'rep'=4] {'group','tensor','rep'}, use_global_device_ids=true, to_apply=%region_12.13 | all-reduce | flops 1024 | bytes 8192 | tf_op jit(solution)/shard_map/psum | solution.py:119
  458.3 0.6 multiply_subtract_fusion
  (6 shorter events, 0.0 us)
Async XLA Ops:
  7.2 1.8 copy-start
  7.2 77.9 %copy-start.3 = (bf16[1024]{0:T(1024)(128)(2,1)S(1)}, bf16[1024]{0:T(1024)(128)(2,1)}, u32[]{:S(2)}) copy-start(bf16[1024]{0:T(1024)(128)(2,1)} %param.21) | copy-start | bytes 6148
  7.2 108.8 %copy-start.2 = (bf16[16,1024]{1,0:T(8,128)(2,1)S(1)}, bf16[16,1024]{1,0:T(8,128)(2,1)}, u32[]{:S(2)}) copy-start(bf16[16,1024]{1,0:T(8,128)(2,1)} %param.20) | copy-start | bytes 98308
  7.2 215.3 %copy-start.5 = (f32[512]{0:T(512)S(1)}, f32[512]{0:T(512)}, u32[]{:S(2)}) copy-start(f32[512]{0:T(512)} %param.23) | copy-start | bytes 6148
  7.2 59.1 %all-gather.3.cloned.1.call-start = ((), (), s32[]{:S(2)}) async-start(), calls=%async_computation.2 | async-start | bytes 1081344 | tf_op jit(solution)/shard_map/all_gather | solution.py:86
  14.1 101.9 %reduce-scatter.2.cloned.1.call-start = ((), (), s32[]{:S(2)}) async-start(), calls=%async_computation.3 | async-start | bytes 589824 | tf_op jit(solution)/shard_map/reduce_scatter | solution.py:89
  85.0 137.5 %all-gather.5.cloned.1.call-start = ((), (), s32[]{:S(2)}) async-start(), calls=%async_computation.4 | async-start | bytes 8650752 | tf_op jit(solution)/shard_map/all_gather | solution.py:100
  117.0 116.4 %copy-start.1 = (bf16[16,1024]{1,0:T(8,128)(2,1)}, bf16[16,1024]{1,0:T(8,128)(2,1)S(1)}, u32[]{:S(2)}) copy-start(bf16[16,1024]{1,0:T(8,128)(2,1)S(1)} %get-tuple-element.10) | copy-start | bytes 98308
  149.7 234.1 %copy-start.4 = (f32[512]{0:T(512)S(1)}, f32[512]{0:T(512)}, u32[]{:S(2)}) copy-start(f32[512]{0:T(512)} %param.24) | copy-start | bytes 6148
  149.7 234.1 %copy-start.6 = (s32[512]{0:T(512)S(1)}, s32[512]{0:T(512)}, u32[]{:S(2)}) copy-start(s32[512]{0:T(512)} %param.25) | copy-start | bytes 6148
Sparse Core Ops, SparseCore 0:
  14.3 52.0 all-gather.2
  85.1 30.8 reduce-scatter.1
  149.8 72.7 all-gather.4
where the time goes:
time: 466 us; the launch traced here: 465 us
  blocking collectives  272 us (58%)
  waiting for transfers between devices  156 us (33%)
  matrix products  17.1 us (4%)
  between operations  13.9 us (3%)
  other arithmetic  4.74 us (1%)
    pmax x1, blocking collectives, shards(): lax.pmax(jnp.max(unnormalized_odds, axis=1), ('group', 'tensor', 'rep'))  75.8 us
    psum x1, blocking collectives, shards(): lax.psum((local_total, token_part), ('group', 'tensor', 'rep'))  74.3 us
    psum x1, blocking collectives, shards(): kept = lax.psum(jnp.sum(jnp.exp(logw), axis=1), ('group', 'tensor', 'rep'))  73.4 us
    all_gather x1, waiting for transfers between devices, shards(): lax.all_gather(features, ('group', 'rep'), axis=0, tiled=True)  72.8 us
    all_gather x1, waiting for transfers between devices, shards(): every_attn = lax.all_gather(attn, ('group', 'rep'), axis=0, tiled=True)  52.2 us
    reduce_scatter x1, waiting for transfers between devices, shards(): summed = lax.psum_scatter(terms, 'tensor', scatter_dimension=1, tiled=True)  30.9 us
    all_gather x1, blocking collectives, shards(): features = lax.all_gather(rescaled_stream, 'tensor', axis=1, tiled=True)  20.6 us
    all_to_all x1, blocking collectives, shards(): lax.all_to_all(partial_cols, ('group', 'rep'), split_axis=0, concat_axis=...  16 us
  transfers between devices with their start and end apart: 3, of which 3 were waited for; matrix products, arithmetic and copies ran while one was open for 0% of the time, Pallas kernels for 0%

commit v1 on v0

v1 whole, which is shorter than its diff:
```python
import functools
import math

import jax
import jax.numpy as jnp
from jax import lax
from jax.experimental import pallas as pl
from jax.experimental.pallas import tpu as pltpu
from jax.sharding import Mesh
from jax.sharding import PartitionSpec as P

cut_slope = 4.0
LN2 = math.log(2.0)
F32 = jnp.float32
BF16 = jnp.bfloat16
PLANE = ("x", "core", "rep")
SAME_CORE = ("x", "tensor", "rep")


def attend(
    probe_vectors,
    stored_lookup_vectors,
    stored_content_vectors,
    fresh_lookup_vector,
    fresh_content_vector,
    history_counts,
):
    rows, kv_local, cache_len, head_dim = stored_lookup_vectors.shape
    heads_local = probe_vectors.shape[1]
    grouped_query_rows = probe_vectors.reshape(rows, kv_local, heads_local // kv_local, head_dim)
    score_scale = 1.0 / math.sqrt(head_dim)
    self_entry = (
        jnp.einsum(
            "mjqo,mjo->mjq",
            grouped_query_rows,
            fresh_lookup_vector,
            preferred_element_type=jnp.float32,
        )
        * score_scale
    )
    scores = (
        jnp.einsum(
            "bkgd,bkld->bkgl",
            grouped_query_rows,
            stored_lookup_vectors,
            preferred_element_type=jnp.float32,
        )
        * score_scale
    )
    position = lax.broadcasted_iota(jnp.int32, (1, 1, 1, cache_len), 3)
    live = position < history_counts[:, None, None, None]
    top = jnp.maximum(jnp.max(jnp.where(live, scores, -1e30), axis=3), self_entry)
    expo = jnp.where(live, jnp.exp(scores - top[..., None]), 0.0)
    total = jnp.sum(expo, axis=3)
    accum = jnp.einsum(
        "bkgl,bkld->bkgd",
        expo.astype(jnp.bfloat16),
        stored_content_vectors,
        preferred_element_type=jnp.float32,
    )
    own_expo = jnp.exp(self_entry - top)
    total = total + own_expo
    accum = accum + jnp.einsum(
        "vct,vcn->vctn",
        own_expo.astype(jnp.bfloat16),
        fresh_content_vector,
        preferred_element_type=jnp.float32,
    )
    return (accum / total[..., None]).reshape(rows, heads_local * head_dim).astype(jnp.bfloat16)


def turn(shift):
    pairs = []
    for x in range(4):
        for c in range(2):
            for y in range(4):
                here = (x * 2 + c) * 4 + y
                if c == 0:
                    there = (((x + shift) % 4) * 2 + c) * 4 + y
                else:
                    there = (x * 2 + c) * 4 + (y + shift) % 4
                pairs.append((here, there))
    return pairs


def turn_other(shift):
    pairs = []
    for x in range(4):
        for c in range(2):
            for y in range(4):
                here = (x * 2 + c) * 4 + y
                if c == 1:
                    there = (((x + shift) % 4) * 2 + c) * 4 + y
                else:
                    there = (x * 2 + c) * 4 + (y + shift) % 4
                pairs.append((here, there))
    return pairs


def swap_core(value):
    return lax.ppermute(value, "core", [(0, 1), (1, 0)])


def head_body(
    steps,
    first,
    last,
    table,
    h_ref,
    lo_a,
    lo_b,
    lp_a,
    lp_b,
    m_a,
    m_b,
    *rest,
):
    rest = list(rest)
    if not first:
        z_in, sq_in = rest[:2]
        rest = rest[2:]
    if last:
        sharp, chosen, z_out, lse_out, tok_out, sq_acc = rest
        sq_ref = sq_acc
    else:
        z_out, sq_ref = rest
    step = pl.program_id(0)

    @pl.when(step == 0)
    def _():
        if first:
            z_out[...] = jnp.zeros_like(z_out)
            sq_ref[...] = jnp.zeros_like(sq_ref)
        else:
            z_out[...] = z_in[...]
            sq_ref[...] = sq_in[...]

    wide = h_ref[0].astype(F32)
    half = wide.shape[1] // 2
    squares = wide * wide
    sq_ref[...] += (
        squares[:, 0:128] + squares[:, 128:256] + squares[:, 256:384] + squares[:, 384:512]
    )
    xa = (wide[:, :half] * m_a[0].astype(F32)).astype(BF16)
    xb = (wide[:, half:] * m_b[0].astype(F32)).astype(BF16)
    cols = lo_a.shape[1]
    z_out[:, :cols] += jnp.dot(xa, lo_a[...], preferred_element_type=F32) + jnp.dot(
        xb, lo_b[...], preferred_element_type=F32
    )
    z_out[:, cols:] += jnp.dot(xa, lp_a[...], preferred_element_type=F32) + jnp.dot(
        xb, lp_b[...], preferred_element_type=F32
    )

    if last:

        @pl.when(step == steps - 1)
        def _():
            total = jnp.sum(sq_ref[...], axis=1, keepdims=True)
            scale = lax.rsqrt(total / 8192.0 + 1e-05) * sharp[...]
            z = z_out[...] * scale
            z_out[...] = z
            top = jnp.max(z, axis=1, keepdims=True)
            mass = jnp.sum(jnp.exp(z - top), axis=1, keepdims=True)
            lse_out[...] = jnp.transpose(jnp.broadcast_to(top + jnp.log(mass), (z.shape[0], 128)))
            spot = lax.broadcasted_iota(jnp.int32, z.shape, 1)
            token = jnp.sum(jnp.where(spot == chosen[...], z, 0.0), axis=1, keepdims=True)
            tok_out[...] = jnp.transpose(jnp.broadcast_to(token, (z.shape[0], 128)))


def head_call(blocks, table, lex_own, lex_peer, gain, state, closing):
    steps, rows, width = blocks.shape
    half = width // 2
    cols = lex_own.shape[1]
    first, last = state is None, closing is not None
    whole = lambda *shape: pl.BlockSpec(shape, lambda i, t: (0,) * len(shape))
    in_specs = [
        pl.BlockSpec((1, rows, width), lambda i, t: (i, 0, 0)),
        pl.BlockSpec((half, cols), lambda i, t: (t[2 * i], 0)),
        pl.BlockSpec((half, cols), lambda i, t: (t[2 * i + 1], 0)),
        pl.BlockSpec((half, cols), lambda i, t: (t[2 * i], 0)),
        pl.BlockSpec((half, cols), lambda i, t: (t[2 * i + 1], 0)),
        pl.BlockSpec((1, 1, half), lambda i, t: (t[2 * i], 0, 0)),
        pl.BlockSpec((1, 1, half), lambda i, t: (t[2 * i + 1], 0, 0)),
    ]
    operands = [blocks, lex_own, lex_own, lex_peer, lex_peer, gain, gain]
    scratch = []
    if not first:
        in_specs += [whole(rows, 2 * cols), whole(rows, 128)]
        operands += list(state)
    out_shape = [jax.ShapeDtypeStruct((rows, 2 * cols), F32)]
    out_specs = [whole(rows, 2 * cols)]
    if last:
        in_specs += [whole(rows, 1), whole(rows, 1)]
        operands += list(closing)
        out_shape += [jax.ShapeDtypeStruct((128, rows), F32)] * 2
        out_specs += [whole(128, rows)] * 2
        scratch = [pltpu.VMEM((rows, 128), F32)]
    else:
        out_shape += [jax.ShapeDtypeStruct((rows, 128), F32)]
        out_specs += [whole(rows, 128)]
    return pl.pallas_call(
        functools.partial(head_body, steps, first, last),
        grid_spec=pltpu.PrefetchScalarGridSpec(
            num_scalar_prefetch=1,
            grid=(steps,),
            in_specs=in_specs,
            out_specs=out_specs,
            scratch_shapes=scratch,
        ),
        out_shape=out_shape,
        compiler_params=pltpu.CompilerParams(vmem_limit_bytes=24 * 1024 * 1024),
        cost_estimate=pl.CostEstimate(
            flops=4 * rows * steps * width * cols,
            bytes_accessed=steps * (rows * width * 2 + width * cols * 4) + rows * cols * 8,
            transcendentals=0,
        ),
    )(table, *operands)


def mass_body(z_ref, lse_ref, level_ref, kept_out, norm_out):
    parts = lse_ref[...]
    top = jnp.max(parts, axis=0, keepdims=True)
    norm = top + jnp.log(jnp.sum(jnp.exp(parts - top), axis=0, keepdims=True))
    norm_out[...] = norm
    column = jnp.transpose(jnp.broadcast_to(norm, parts.shape))[:, :1]
    logp = z_ref[...] - column
    gate = cut_slope * (level_ref[...] + logp * (1.0 / LN2))
    kept = jnp.sum(jnp.exp(logp) / (1.0 + jnp.exp(-gate)), axis=1, keepdims=True)
    kept_out[...] = jnp.transpose(jnp.broadcast_to(kept, (kept.shape[0], 128)))


def mass_call(z, lse, level):
    rows = z.shape[0]
    return pl.pallas_call(
        mass_body,
        out_shape=[
            jax.ShapeDtypeStruct((128, rows), F32),
            jax.ShapeDtypeStruct((1, rows), F32),
        ],
        compiler_params=pltpu.CompilerParams(vmem_limit_bytes=24 * 1024 * 1024),
    )(z, lse, level)


def shards(
    probe_vectors,
    stored_lookup_vectors,
    stored_content_vectors,
    fresh_lookup_vector,
    fresh_content_vector,
    history_counts,
    mixing_matrix,
    skip_stream,
    closing_multiplier,
    lexicon_matrix,
    sharpening_factor,
    desired_perplexity,
    chosen_symbols,
):
    x, c, t, y = (lax.axis_index(name) for name in ("x", "core", "tensor", "rep"))
    mix_peer = swap_core(mixing_matrix)
    lex_peer = swap_core(lexicon_matrix)

    attn = attend(
        probe_vectors,
        stored_lookup_vectors,
        stored_content_vectors,
        fresh_lookup_vector,
        fresh_content_vector,
        history_counts,
    )

    skip_blocks = skip_stream.reshape(16, 4, 256).transpose(1, 0, 2)
    skip_sent = jnp.broadcast_to(skip_blocks[None], (4, 4, 16, 256)).reshape(16, 16, 256)
    sent = jnp.concatenate([jnp.broadcast_to(attn[None], (16, 16, 1024)), skip_sent], axis=2)
    got = lax.all_to_all(sent, ("x", "rep"), 0, 0, tiled=True).reshape(256, 1280)
    every_attn = got[:, :1024]
    skip_got = got[:, 1024:]

    part_own = jnp.dot(every_attn, mixing_matrix, preferred_element_type=F32).astype(BF16)
    part_peer = jnp.dot(every_attn, mix_peer, preferred_element_type=F32).astype(BF16)
    gain_row = jnp.broadcast_to(closing_multiplier.reshape(1, 8, 128), (8, 8, 128))
    gain_sent = jnp.concatenate([gain_row, jnp.zeros((8, 24, 128), BF16)], axis=1)
    sent = jnp.concatenate(
        [
            part_own.reshape(8, 32, 256),
            part_peer.reshape(8, 32, 256),
            skip_got.reshape(8, 32, 256),
            gain_sent,
        ],
        axis=2,
    )
    got = lax.all_to_all(sent, "tensor", 0, 0, tiled=True)
    gain = got[:, :8, 768:].reshape(32, 1, 256)
    sums = jnp.sum(got[:, :, :512].astype(F32), axis=0)
    skip_own = lax.dynamic_index_in_dim(got[:, :, 512:768], 2 * x + c, 0, keepdims=False)
    skip_peer = lax.dynamic_index_in_dim(got[:, :, 512:768], 2 * x + 1 - c, 0, keepdims=False)
    skip = jnp.concatenate([skip_own, skip_peer], axis=1).astype(F32)
    piece = (skip + sums).astype(BF16)

    sent = jnp.broadcast_to(piece[None], (8, 32, 512))
    block = lax.all_to_all(sent, "tensor", 0, 0, tiled=True).reshape(256, 512)
    near = [block] + [lax.ppermute(block, PLANE, turn_other(s)) for s in (1, -1, 2)]
    stack = jnp.stack(near)
    from_left = lax.ppermute(stack, PLANE, turn(1))
    from_right = lax.ppermute(stack, PLANE, turn(-1))
    far_a = lax.ppermute(from_left[:2], PLANE, turn(1))
    far_b = lax.ppermute(from_right[2:], PLANE, turn(-1))

    order = []
    for far in (0, -1, 1, 2):
        for side in (0, -1, 1, 2):
            bx = jnp.where(c == 0, x + far, x + side) % 4
            by = jnp.where(c == 0, y + side, y + far) % 4
            order += [(bx * 2 + c) * 4 + by, (bx * 2 + 1 - c) * 4 + by]
    table = jnp.stack(order).astype(jnp.int32)

    mine = lambda v: lax.dynamic_index_in_dim(v.reshape(4, 2, 64), c, 1, keepdims=False).reshape(256)
    sharp = mine(sharpening_factor)
    level = mine(desired_perplexity)
    picks = mine(chosen_symbols)
    base_own = (((x * 2 + c) * 8 + t) * 4 + y) * 512
    base_peer = (((x * 2 + 1 - c) * 8 + t) * 4 + y) * 512
    in_own = (picks >= base_own) & (picks < base_own + 512)
    in_peer = (picks >= base_peer) & (picks < base_peer + 512)
    spot = jnp.where(in_own, picks - base_own, jnp.where(in_peer, picks - base_peer + 512, -1))

    near_blocks = jnp.concatenate([stack, from_left, from_right])
    far_blocks = jnp.concatenate([far_a, far_b])
    state = head_call(near_blocks, table[:24], lexicon_matrix, lex_peer, gain, None, None)
    z, lse, tok = head_call(
        far_blocks,
        table[24:],
        lexicon_matrix,
        lex_peer,
        gain,
        state,
        (sharp[:, None], spot[:, None]),
    )
    every_lse = lax.all_to_all(
        lse.reshape(128, 2, 128), SAME_CORE, 0, 0, tiled=True
    ).reshape(128, 256)
    kept, norm = mass_call(z, every_lse, level[:, None])
    sent = jnp.concatenate([kept, tok], axis=1).reshape(128, 4, 128)
    got = lax.all_to_all(sent, SAME_CORE, 0, 0, tiled=True)
    kept, tok = jnp.sum(got, axis=0).reshape(2, 256)
    token_logp = tok - norm.reshape(256)
    token_logw = token_logp + jax.nn.log_sigmoid(cut_slope * (level + token_logp / LN2))
    mine_out = -(token_logw - jnp.log(kept)) / LN2
    peer_out = swap_core(mine_out)
    even = jnp.where(c == 0, mine_out, peer_out).reshape(4, 64)
    odd = jnp.where(c == 0, peer_out, mine_out).reshape(4, 64)
    surprise = jnp.stack([even, odd], axis=1).reshape(512)
    next_targets = desired_perplexity - 0.1 * (surprise - 5.0)

    every_block = jnp.concatenate([near_blocks, far_blocks])
    rows = lax.dynamic_slice_in_dim(every_block, (x * 4 + y) * 16, 16, 1)
    half = lax.dynamic_slice_in_dim(rows, jnp.where(t % 2 == c, 0, 256), 256, 2)
    place = lambda delta: jnp.array([0, 2, 3, 1], jnp.int32)[delta % 4]
    pieces = []
    for yb in range(4):
        dx, dy = t // 2 - x, yb - y
        far = jnp.where(c == 0, dx, dy)
        side = jnp.where(c == 0, dy, dx)
        pieces.append(
            lax.dynamic_index_in_dim(half, place(far) * 4 + place(side), 0, keepdims=False)
        )
    hidden = jnp.concatenate(pieces, axis=1)
    return (hidden, next_targets, surprise)


def solution(mesh):
    fine = Mesh(mesh.devices.reshape(4, 2, 8, 4), ("x", "core", "tensor", "rep"))
    rows = ("x", "core", "rep")
    placed = (
        P(rows, "tensor", None),
        P(rows, "tensor", None, None),
        P(rows, "tensor", None, None),
        P(rows, "tensor", None),
        P(rows, "tensor", None),
        P(rows),
        P("tensor", rows),
        P(rows, "tensor"),
        P("tensor"),
        P(None, ("x", "core", "tensor", "rep")),
        P(),
        P(),
        P(),
    )
    return jax.shard_map(
        shards,
        mesh=fine,
        in_specs=placed,
        out_specs=(P(rows, "tensor"), P(), P()),
        check_vma=False,
    )
```

time: 466 us -> 181 us (0.39)
  blocking collectives: 272 us -> 12 us
  waiting for transfers between devices: 156 us -> 54.9 us
  starting transfers between devices: 0.12 us -> 53.3 us
  local copies, waits for them, and re-layouts: 1.5 us -> 24 us
  Pallas kernels: 0 us -> 16.1 us
  matrix products: 17.1 us -> 6.08 us
  between operations: 13.9 us -> 6.37 us
    psum x3 -> x0, blocking collectives: 160 us -> none  [the longest x1 74.3 us: shards(): lax.psum((local_total, token_part), ('group', 'tensor', 'rep'))]
    all_gather x2 -> x0, waiting for transfers between devices: 125 us -> none  [the longest x1 72.8 us: shards(): lax.all_gather(features, ('group', 'rep'), axis=0, tiled=True)]
    pmax x1 -> x0, blocking collectives: 75.8 us -> none  [shards(): lax.pmax(jnp.max(unnormalized_odds, axis=1), ('group', 'tensor', 'rep'))]
    all_to_all x0 -> x4, waiting for transfers between devices: none -> 35.4 us  [the longest x1 12.8 us: shards(): got = lax.all_to_all(sent, 'tensor', 0, 0, tiled=True)]
    reduce_scatter x1 -> x0, waiting for transfers between devices: 30.9 us -> none  [shards(): summed = lax.psum_scatter(terms, 'tensor', scatter_dimension=1, tiled=True)]
    all_to_all x0 -> x4, starting transfers between devices: none -> 29.4 us  [the longest x1 10 us: shards(): lax.all_to_all(lse.reshape(128, 2, 128), SAME_CORE, 0, 0, tiled=True)]
    ppermute x0 -> x10, starting transfers between devices: none -> 23.9 us  [the longest x3 14 us: swap_core(): return lax.ppermute(value, 'core', [(0, 1), (1, 0)])]
    all_gather x1 -> x0, blocking collectives: 20.6 us -> none  [shards(): features = lax.all_gather(rescaled_stream, 'tensor', axis=1, tiled=True)]
  transfers between devices with their start and end apart: 3 -> 14, of which waited for: 3 -> 11; matrix products, arithmetic and copies ran while one was open for 0% -> 14% of each run, Pallas kernels for 0% -> 0%
where the time goes in v1:
time: 181 us; the launch traced here: 180 us
  waiting for transfers between devices  54.9 us (30%)
  starting transfers between devices  53.3 us (29%)
  local copies, waits for them, and re-layouts  24 us (13%)
  Pallas kernels  16.1 us (9%)
  blocking collectives  12 us (7%)
  other arithmetic  7.17 us (4%)
  between operations  6.37 us (4%)
  matrix products  6.08 us (3%)
    pallas_call x2, Pallas kernels, head_call(): pl.pallas_call(functools.partial(head_body, steps, first, last), grid_spe...  15.4 us
    ppermute x3, starting transfers between devices, swap_core(): return lax.ppermute(value, 'core', [(0, 1), (1, 0)])  14 us
    all_to_all x1, waiting for transfers between devices, shards(): got = lax.all_to_all(sent, 'tensor', 0, 0, tiled=True)  12.8 us
    unnamed x48, local copies, waits for them, and re-layouts  12.4 us
    all_to_all x1, blocking collectives, shards(): block = lax.all_to_all(sent, 'tensor', 0, 0, tiled=True).reshape(256, 512)  12 us
    all_to_all x1, waiting for transfers between devices, shards(): lax.all_to_all(sent, ('x', 'rep'), 0, 0, tiled=True).reshape(256, 1280)  10.8 us
    ppermute x1, waiting for transfers between devices, shards(): from_left = lax.ppermute(stack, PLANE, turn(1))  10 us
    all_to_all x1, starting transfers between devices, shards(): lax.all_to_all(lse.reshape(128, 2, 128), SAME_CORE, 0, 0, tiled=True)  10 us
  transfers between devices with their start and end apart: 14, of which 11 were waited for; matrix products, arithmetic and copies ran while one was open for 14% of the time, Pallas kernels for 0%

profile of v1, /device:TPU:1, one launch (start us, length us, event | category | flops | bytes accessed | tf_op | source)
XLA Modules:
  0.0 179.9 jit_solution(918246949604049007)
XLA Ops:
  0.6 3.3 %collective-permute-start.8 = (bf16[8192,512]{1,0:T(8,128)(2,1)}, bf16[8192,512]{1,0:T(8,128)(2,1)}, u32[]{:S(2)}, u32[]{:S(2)}) collective-permute-start(bf16[8192,512]{1,0:T(8,128)(2,1)} %lo_b.3), channel_id=1, source_target_pairs={{0,32},{32,0},{1,33},{33,1},{2,34},{34,2},{3,35},{35,3},{4,36},{36... | collective-permute-start | bytes 25165832 | tf_op jit(solution)/shard_map/ppermute | solution.py:101
  4.0 0.8 reshape.281
  4.8 0.7 iota_compare_fusion.1
  5.5 0.9 fusion.26
  6.4 1.5 select_reduce_fusion
  7.9 0.2 fusion.20
  8.1 0.7 bitcast_convert_fusion
  8.8 2.0 %fusion.13 = bf16[16,8,128]{2,1,0:T(8,128)(2,1)S(1)} fusion(bf16[16,1,512,128]{3,2,1,0:T(8,128)(2,1)} %param.23, f32[16,8,512]{2,1,0:T(8,128)S(1)} %get-tuple-element.50, f32[16,8]{1,0:T(8,128)S(1)} %multiply_maximum_fusion, pred[16,512]{1,0:T(8,128)(4,1)S(1)} %iota_compare_fusion.1, f32[16,8]{1,0:T(8,128)S(1)} %get-tuple-element.38, ...), kind=kOutput, calls=%fused_computation.9 | convolution fusion | flops 17039360 | bytes 2409984 | tf_op jit(solution)/shard_map/bkgl,bkld->bkgd/dot_general | solution.py:55
  11.0 1.0 pad_maximum_fusion.2
  11.9 5.0 %all-to-all-start = ((bf16[16,16,1280]{2,1,0:T(8,128)(2,1)}), bf16[16,16,1280]{2,1,0:T(8,128)(2,1)S(1)}, u32[]{:S(2)}, u32[]{:S(2)}) async-start(bf16[16,16,1280]{2,1,0:T(8,128)(2,1)} %pad_maximum_fusion.2), calls=%async_computation | async-start | bytes 1310720 | tf_op jit(solution)/shard_map/all_to_all | solution.py:275
  17.0 0.5 collective-permute-start
  17.5 10.8 %all-to-all-done = bf16[16,16,1280]{2,1,0:T(8,128)(2,1)S(1)} async-done(((bf16[16,16,1280]{2,1,0:T(8,128)(2,1)}), bf16[16,16,1280]{2,1,0:T(8,128)(2,1)S(1)}, u32[]{:S(2)}, u32[]{:S(2)}) %all-to-all-start) | async-done | bytes 655392 | tf_op jit(solution)/shard_map/all_to_all | solution.py:275
  28.3 0.3 convolution_convert_fusion.1
  28.6 1.3 convolution_convert_fusion
  30.0 0.9 fusion.19
  30.9 8.2 %all-to-all-start.1 = ((bf16[8,32,896]{2,1,0:T(8,128)(2,1)}), bf16[8,32,896]{2,1,0:T(8,128)(2,1)S(1)}, u32[]{:S(2)}, u32[]{:S(2)}) async-start(bf16[8,32,896]{2,1,0:T(8,128)(2,1)} %fusion.19), calls=%async_computation.1 | async-start | bytes 917504 | tf_op jit(solution)/shard_map/all_to_all | solution.py:292
  39.1 12.8 %all-to-all-done.1 = bf16[8,32,896]{2,1,0:T(8,128)(2,1)S(1)} async-done(((bf16[8,32,896]{2,1,0:T(8,128)(2,1)}), bf16[8,32,896]{2,1,0:T(8,128)(2,1)S(1)}, u32[]{:S(2)}, u32[]{:S(2)}) %all-to-all-start.1) | async-done | bytes 458784 | tf_op jit(solution)/shard_map/all_to_all | solution.py:292
  52.0 12.0 %all_to_all.25 = bf16[8,32,512]{2,1,0:T(8,128)(2,1)S(1)} all-to-all(bf16[8,32,512]{2,1,0:T(8,128)(2,1)S(1)} %broadcast_in_dim.59), channel_id=1, replica_groups=mesh['x'=4,'core'=2,'tensor'=8,'rep'=4] {'tensor'}, dimensions={0} | all-to-all | bytes 524288 | tf_op jit(solution)/shard_map/all_to_all | solution.py:301
  64.0 1.8 collective-permute-start.1
  65.8 1.1 collective-permute-start.2
  66.8 1.6 collective-permute-start.3
  68.4 2.2 %collective-permute-done.1 = bf16[256,512]{1,0:T(8,128)(2,1)S(1)} collective-permute-done((bf16[256,512]{1,0:T(8,128)(2,1)S(1)}, bf16[256,512]{1,0:T(8,128)(2,1)S(1)}, u32[]{:S(2)}, u32[]{:S(2)}) %collective-permute-start.1) | collective-permute-done | bytes 262176 | tf_op jit(solution)/shard_map/ppermute | solution.py:302
  70.6 0.4 collective-permute-done.2
  71.0 3.6 %collective-permute-done.3 = bf16[256,512]{1,0:T(8,128)(2,1)S(1)} collective-permute-done((bf16[256,512]{1,0:T(8,128)(2,1)S(1)}, bf16[256,512]{1,0:T(8,128)(2,1)S(1)}, u32[]{:S(2)}, u32[]{:S(2)}) %collective-permute-start.3) | collective-permute-done | bytes 262176 | tf_op jit(solution)/shard_map/ppermute | solution.py:302
  74.6 1.2 pad_maximum_fusion
  75.7 0.6 collective-permute-start.4
  76.4 2.1 %collective-permute-start.5 = (bf16[4,256,512]{2,1,0:T(8,128)(2,1)}, bf16[4,256,512]{2,1,0:T(8,128)(2,1)}, u32[]{:S(2)}, u32[]{:S(2)}) collective-permute-start(bf16[4,256,512]{2,1,0:T(8,128)(2,1)} %pad_maximum_fusion), channel_id=1, source_target_pairs={{0,192},{1,193},{2,194},{3,195},{32,35},{33,32},{34,33},{35,34},{6... | collective-permute-start | bytes 3145736 | tf_op jit(solution)/shard_map/ppermute | solution.py:305
  79.2 1.0 constant_dynamic-update-slice_fusion.12
  80.2 1.0 constant_dynamic-update-slice_fusion.11
  81.2 10.0 %collective-permute-done.4 = bf16[4,256,512]{2,1,0:T(8,128)(2,1)} collective-permute-done((bf16[4,256,512]{2,1,0:T(8,128)(2,1)}, bf16[4,256,512]{2,1,0:T(8,128)(2,1)}, u32[]{:S(2)}, u32[]{:S(2)}) %collective-permute-start.4) | collective-permute-done | bytes 1048608 | tf_op jit(solution)/shard_map/ppermute | solution.py:304
  91.2 1.1 slice.39
  92.4 1.1 slice.40
  93.5 2.7 %collective-permute-start.7 = (bf16[2,256,512]{2,1,0:T(8,128)(2,1)S(1)}, bf16[2,256,512]{2,1,0:T(8,128)(2,1)S(1)}, u32[]{:S(2)}, u32[]{:S(2)}) collective-permute-start(bf16[2,256,512]{2,1,0:T(8,128)(2,1)S(1)} %slice.40), channel_id=1, source_target_pairs={{0,192},{1,193},{2,194},{3,195},{32,35},{33,32},{34,33},{35,34},{6... | collective-permute-start | bytes 1572872 | tf_op jit(solution)/shard_map/ppermute | solution.py:307
  96.3 1.5 constant_dynamic-update-slice_fusion.9
  97.8 1.4 constant_dynamic-update-slice_fusion.8
  99.2 2.4 %collective-permute-done.6 = bf16[2,256,512]{2,1,0:T(8,128)(2,1)S(1)} collective-permute-done((bf16[2,256,512]{2,1,0:T(8,128)(2,1)S(1)}, bf16[2,256,512]{2,1,0:T(8,128)(2,1)S(1)}, u32[]{:S(2)}, u32[]{:S(2)}) %collective-permute-start.6) | collective-permute-done | bytes 524320 | tf_op jit(solution)/shard_map/ppermute | solution.py:306
  101.6 0.7 collective-permute-done.7
  102.5 0.7 copy-done.5
  103.1 3.4 %copy-done.1 = bf16[8192,512]{1,0:T(8,128)(2,1)S(1)} copy-done((bf16[8192,512]{1,0:T(8,128)(2,1)S(1)}, bf16[8192,512]{1,0:T(8,128)(2,1)}, u32[]{:S(2)}) %copy-start.1) | copy-done | bytes 8388632
  106.5 10.5 %shard_map.220 = (f32[256,1024]{1,0:T(8,128)S(1)}, f32[256,128]{1,0:T(8,128)S(1)}) custom-call(s32[24]{0:T(128)S(1)} %stack.154.table, bf16[12,256,512]{2,1,0:T(8,128)(2,1)S(1)} %get-tuple-element.23.h_ref, bf16[8192,512]{1,0:T(8,128)(2,1)S(1)} %copy-done.1, bf16[8192,512]{1,0:T(8,128)(2,1)S(1)} %copy-done.1, ...), custom_call_target="tpu_custom_call" | custom-call | flops 3221225472 | bytes 16777216 | tf_op jit(solution)/shard_map/pallas_call | solution.py:201
  117.1 4.8 %shard_map.221 = (f32[256,1024]{1,0:T(8,128)S(1)}, f32[128,256]{1,0:T(8,128)S(1)}, f32[128,256]{1,0:T(8,128)S(1)}) custom-call(s32[8]{0:T(128)S(1)} %stack.129.table, bf16[4,256,512]{2,1,0:T(8,128)(2,1)S(1)} %pad_maximum_fusion.1.h_ref, bf16[8192,512]{1,0:T(8,128)(2,1)S(1)} %bitcast.117, bf16[8192,512]{1,0:T(8,128)(2,1)S(1)} %bitcast.117, ...), custom_call_target="tpu_custom_call" | custom-call | flops 1073741824 | bytes 6291456 | tf_op jit(solution)/shard_map/pallas_call | solution.py:201
  121.9 0.6 copy-done.2
  122.6 0.6 copy-done.3
  123.2 1.6 reshape.291
  124.8 10.0 %all-to-all-start.3 = ((f32[128,2,128]{2,1,0:T(2,128)}), f32[128,2,128]{2,1,0:T(2,128)S(1)}, u32[]{:S(2)}, u32[]{:S(2)}) async-start(f32[128,2,128]{2,1,0:T(2,128)} %reshape.291), calls=%async_computation.3 | async-start | bytes 262144 | tf_op jit(solution)/shard_map/all_to_all | solution.py:339
  134.9 0.5 broadcast.170
  135.4 0.7 fusion.34
  136.3 9.5 %all-to-all-done.3 = f32[128,2,128]{2,1,0:T(2,128)S(1)} async-done(((f32[128,2,128]{2,1,0:T(2,128)}), f32[128,2,128]{2,1,0:T(2,128)S(1)}, u32[]{:S(2)}, u32[]{:S(2)}) %all-to-all-start.3) | async-done | bytes 131104 | tf_op jit(solution)/shard_map/all_to_all | solution.py:339
  145.8 0.6 copy-done.9
  146.4 0.9 copy.41
  147.3 0.8 shard_map.222
  148.1 1.0 pad_maximum_fusion.3
  149.1 0.8 reshape.294
  149.9 6.2 %all-to-all-start.4 = ((f32[128,4,128]{2,1,0:T(4,128)}), f32[128,4,128]{2,1,0:T(4,128)S(1)}, u32[]{:S(2)}, u32[]{:S(2)}) async-start(f32[128,4,128]{2,1,0:T(4,128)} %reshape.294), calls=%async_computation.4 | async-start | bytes 524288 | tf_op jit(solution)/shard_map/all_to_all | solution.py:344
  156.3 0.7 fusion.35
  162.1 1.9 %constant_dynamic-update-slice_fusion.1 = bf16[16,256,512]{2,1,0:T(8,128)(2,1)} fusion(bf16[16,256,512]{2,1,0:T(8,128)(2,1)} %copy-done.11, bf16[2,256,512]{2,1,0:T(8,128)(2,1)} %copy-done.4), kind=kLoop, calls=%fused_computation.33 | loop fusion | bytes 1048576
  164.0 0.8 constant_dynamic-update-slice_fusion
  164.8 0.8 dynamic-slice_bitcast_fusion.5
  165.7 2.3 %all-to-all-done.4 = f32[128,4,128]{2,1,0:T(4,128)S(1)} async-done(((f32[128,4,128]{2,1,0:T(4,128)}), f32[128,4,128]{2,1,0:T(4,128)S(1)}, u32[]{:S(2)}, u32[]{:S(2)}) %all-to-all-start.4) | async-done | bytes 262176 | tf_op jit(solution)/shard_map/all_to_all | solution.py:344
  168.0 0.1 reduce_sum.29
  168.1 10.1 %collective-permute-start.9 = (f32[256]{0:T(256)S(1)}, f32[256]{0:T(256)S(1)}, u32[]{:S(2)}, u32[]{:S(2)}) collective-permute-start(f32[256]{0:T(256)S(1)} %negate_multiply_fusion), channel_id=1, source_target_pairs={{0,32},{32,0},{1,33},{33,1},{2,34},{34,2},{3,35},{35,3},{4,36},{36... | collective-permute-start | bytes 3080 | tf_op jit(solution)/shard_map/ppermute | solution.py:101
  178.2 0.6 pad_maximum_fusion.4
  178.9 0.2 collective-permute-done.9
  179.3 0.6 multiply_subtract_fusion
  (75 shorter events, 1.8 us)
Async XLA Ops:
  0.6 5.8 %copy-start = (bf16[16,1,512,128]{3,2,1,0:T(8,128)(2,1)S(1)}, bf16[16,1,512,128]{3,2,1,0:T(8,128)(2,1)}, u32[]{:S(2)}) copy-start(bf16[16,1,512,128]{3,2,1,0:T(8,128)(2,1)} %param.22) | copy-start | bytes 6291460
  0.6 101.8 %collective-permute-start.8 = (bf16[8192,512]{1,0:T(8,128)(2,1)}, bf16[8192,512]{1,0:T(8,128)(2,1)}, u32[]{:S(2)}, u32[]{:S(2)}) collective-permute-start(bf16[8192,512]{1,0:T(8,128)(2,1)} %lo_b.3), channel_id=1, source_target_pairs={{0,32},{32,0},{1,33},{33,1},{2,34},{34,2},{3,35},{35,3},{4,36},{36... | collective-permute-start | bytes 25165832 | tf_op jit(solution)/shard_map/ppermute | solution.py:101
  7.9 9.1 %copy-start.17 = (bf16[1024,256]{1,0:T(8,128)(2,1)S(1)}, bf16[1024,256]{1,0:T(8,128)(2,1)}, u32[]{:S(2)}) copy-start(bf16[1024,256]{1,0:T(8,128)(2,1)} %param.27) | copy-start | bytes 1572868
  10.9 19.1 %copy-start.14 = (bf16[1024]{0:T(1024)(128)(2,1)S(1)}, bf16[1024]{0:T(1024)(128)(2,1)}, u32[]{:S(2)}) copy-start(bf16[1024]{0:T(1024)(128)(2,1)} %param.29) | copy-start | bytes 6148
  11.9 16.4 %all-to-all-start = ((bf16[16,16,1280]{2,1,0:T(8,128)(2,1)}), bf16[16,16,1280]{2,1,0:T(8,128)(2,1)S(1)}, u32[]{:S(2)}, u32[]{:S(2)}) async-start(bf16[16,16,1280]{2,1,0:T(8,128)(2,1)} %pad_maximum_fusion.2), calls=%async_computation | async-start | bytes 1310720 | tf_op jit(solution)/shard_map/all_to_all | solution.py:275
  17.0 11.7 %collective-permute-start = (bf16[1024,256]{1,0:T(8,128)(2,1)S(1)}, bf16[1024,256]{1,0:T(8,128)(2,1)}, u32[]{:S(2)}, u32[]{:S(2)}) collective-permute-start(bf16[1024,256]{1,0:T(8,128)(2,1)S(1)} %copy-done.17), channel_id=1, source_target_pairs={{0,32},{32,0},{1,33},{33,1},{2,34},{34,2},{3,35},{35,3},{4,36},{36... | collective-permute-start | bytes 1572872 | tf_op jit(solution)/shard_map/ppermute | solution.py:101
  30.0 48.4 %copy-start.15 = (f32[512]{0:T(512)S(1)}, f32[512]{0:T(512)}, u32[]{:S(2)}) copy-start(f32[512]{0:T(512)} %param.31) | copy-start | bytes 6148
  30.0 48.7 %copy-start.16 = (s32[512]{0:T(512)S(1)}, s32[512]{0:T(512)}, u32[]{:S(2)}) copy-start(s32[512]{0:T(512)} %param.33) | copy-start | bytes 6148
  30.9 21.0 %all-to-all-start.1 = ((bf16[8,32,896]{2,1,0:T(8,128)(2,1)}), bf16[8,32,896]{2,1,0:T(8,128)(2,1)S(1)}, u32[]{:S(2)}, u32[]{:S(2)}) async-start(bf16[8,32,896]{2,1,0:T(8,128)(2,1)} %fusion.19), calls=%async_computation.1 | async-start | bytes 917504 | tf_op jit(solution)/shard_map/all_to_all | solution.py:292
  64.0 6.6 %collective-permute-start.1 = (bf16[256,512]{1,0:T(8,128)(2,1)S(1)}, bf16[256,512]{1,0:T(8,128)(2,1)S(1)}, u32[]{:S(2)}, u32[]{:S(2)}) collective-permute-start(bf16[256,512]{1,0:T(8,128)(2,1)S(1)} %bitcast.120), channel_id=1, source_target_pairs={{0,1},{1,2},{2,3},{3,0},{32,96},{33,97},{34,98},{35,99},{64,65},{6... | collective-permute-start | bytes 786440 | tf_op jit(solution)/shard_map/ppermute | solution.py:302
  65.8 5.2 %collective-permute-start.2 = (bf16[256,512]{1,0:T(8,128)(2,1)S(1)}, bf16[256,512]{1,0:T(8,128)(2,1)S(1)}, u32[]{:S(2)}, u32[]{:S(2)}) collective-permute-start(bf16[256,512]{1,0:T(8,128)(2,1)S(1)} %bitcast.121), channel_id=1, source_target_pairs={{0,3},{1,0},{2,1},{3,2},{32,224},{33,225},{34,226},{35,227},{64,67... | collective-permute-start | bytes 786440 | tf_op jit(solution)/shard_map/ppermute | solution.py:302
  66.8 7.7 %collective-permute-start.3 = (bf16[256,512]{1,0:T(8,128)(2,1)S(1)}, bf16[256,512]{1,0:T(8,128)(2,1)S(1)}, u32[]{:S(2)}, u32[]{:S(2)}) collective-permute-start(bf16[256,512]{1,0:T(8,128)(2,1)S(1)} %bitcast.122), channel_id=1, source_target_pairs={{0,2},{1,3},{2,0},{3,1},{32,160},{33,161},{34,162},{35,163},{64,66... | collective-permute-start | bytes 786440 | tf_op jit(solution)/shard_map/ppermute | solution.py:302
  70.6 5.2 %copy-start.8 = (bf16[256,512]{1,0:T(8,128)(2,1)}, bf16[256,512]{1,0:T(8,128)(2,1)S(1)}, u32[]{:S(2)}) copy-start(bf16[256,512]{1,0:T(8,128)(2,1)S(1)} %collective-permute-done.1) | copy-start | bytes 786436
  71.0 3.6 %copy-start.7 = (bf16[256,512]{1,0:T(8,128)(2,1)}, bf16[256,512]{1,0:T(8,128)(2,1)S(1)}, u32[]{:S(2)}) copy-start(bf16[256,512]{1,0:T(8,128)(2,1)S(1)} %collective-permute-done.2) | copy-start | bytes 786436
  75.7 15.5 %collective-permute-start.4 = (bf16[4,256,512]{2,1,0:T(8,128)(2,1)}, bf16[4,256,512]{2,1,0:T(8,128)(2,1)}, u32[]{:S(2)}, u32[]{:S(2)}) collective-permute-start(bf16[4,256,512]{2,1,0:T(8,128)(2,1)} %pad_maximum_fusion), channel_id=1, source_target_pairs={{0,64},{1,65},{2,66},{3,67},{32,33},{33,34},{34,35},{35,32},{64,12... | collective-permute-start | bytes 3145736 | tf_op jit(solution)/shard_map/ppermute | solution.py:304
  76.4 16.0 %collective-permute-start.5 = (bf16[4,256,512]{2,1,0:T(8,128)(2,1)}, bf16[4,256,512]{2,1,0:T(8,128)(2,1)}, u32[]{:S(2)}, u32[]{:S(2)}) collective-permute-start(bf16[4,256,512]{2,1,0:T(8,128)(2,1)} %pad_maximum_fusion), channel_id=1, source_target_pairs={{0,192},{1,193},{2,194},{3,195},{32,35},{33,32},{34,33},{35,34},{6... | collective-permute-start | bytes 3145736 | tf_op jit(solution)/shard_map/ppermute | solution.py:305
  92.3 9.3 %collective-permute-start.6 = (bf16[2,256,512]{2,1,0:T(8,128)(2,1)S(1)}, bf16[2,256,512]{2,1,0:T(8,128)(2,1)S(1)}, u32[]{:S(2)}, u32[]{:S(2)}) collective-permute-start(bf16[2,256,512]{2,1,0:T(8,128)(2,1)S(1)} %slice.39), channel_id=1, source_target_pairs={{0,64},{1,65},{2,66},{3,67},{32,33},{33,34},{34,35},{35,32},{64,12... | collective-permute-start | bytes 1572872 | tf_op jit(solution)/shard_map/ppermute | solution.py:306
  93.5 8.9 %collective-permute-start.7 = (bf16[2,256,512]{2,1,0:T(8,128)(2,1)S(1)}, bf16[2,256,512]{2,1,0:T(8,128)(2,1)S(1)}, u32[]{:S(2)}, u32[]{:S(2)}) collective-permute-start(bf16[2,256,512]{2,1,0:T(8,128)(2,1)S(1)} %slice.40), channel_id=1, source_target_pairs={{0,192},{1,193},{2,194},{3,195},{32,35},{33,32},{34,33},{35,34},{6... | collective-permute-start | bytes 1572872 | tf_op jit(solution)/shard_map/ppermute | solution.py:307
  96.2 20.8 %slice-start = ((s8[8388608]{0:T(1024)(128)(4,1)}), s8[4194304]{0:T(1024)(128)(4,1)S(1)}, s32[]{:S(2)}) async-start(s8[8388608]{0:T(1024)(128)(4,1)} %bitcast.116), calls=%async_computation.5 | async-start | bytes 8388608
  99.2 3.3 %copy-start.11 = (bf16[16,256,512]{2,1,0:T(8,128)(2,1)}, bf16[16,256,512]{2,1,0:T(8,128)(2,1)S(1)}, u32[]{:S(2)}) copy-start(bf16[16,256,512]{2,1,0:T(8,128)(2,1)S(1)} %get-tuple-element.24) | copy-start | bytes 12582916
  101.6 15.4 %copy-start.4 = (bf16[2,256,512]{2,1,0:T(8,128)(2,1)}, bf16[2,256,512]{2,1,0:T(8,128)(2,1)S(1)}, u32[]{:S(2)}) copy-start(bf16[2,256,512]{2,1,0:T(8,128)(2,1)S(1)} %collective-permute-done.6) | copy-start | bytes 1572868
  102.3 0.8 copy-start.5
  103.1 3.4 %copy-start.1 = (bf16[8192,512]{1,0:T(8,128)(2,1)S(1)}, bf16[8192,512]{1,0:T(8,128)(2,1)}, u32[]{:S(2)}) copy-start(bf16[8192,512]{1,0:T(8,128)(2,1)} %lo_b.3) | copy-start | bytes 25165828
  106.5 10.5 %slice-start.1 = ((s8[8388608]{0:T(1024)(128)(4,1)}), s8[4194304]{0:T(1024)(128)(4,1)S(1)}, s32[]{:S(2)}) async-start(s8[8388608]{0:T(1024)(128)(4,1)} %bitcast.116), calls=%async_computation.6 | async-start | bytes 8388608
  117.1 17.8 %copy-start.12 = (f32[512]{0:T(512)S(1)}, f32[512]{0:T(512)}, u32[]{:S(2)}) copy-start(f32[512]{0:T(512)} %param.32) | copy-start | bytes 6148
  121.9 0.6 copy-start.2
  122.6 0.6 copy-start.3
  123.2 33.1 %copy-start.10 = (s32[4]{0:T(128)S(1)}, s32[4]{0:T(128)}, u32[]{:S(2)}) copy-start(s32[4]{0:T(128)} %constant.366.clone) | copy-start | bytes 52
  124.8 20.9 %all-to-all-start.3 = ((f32[128,2,128]{2,1,0:T(2,128)}), f32[128,2,128]{2,1,0:T(2,128)S(1)}, u32[]{:S(2)}, u32[]{:S(2)}) async-start(f32[128,2,128]{2,1,0:T(2,128)} %reshape.291), calls=%async_computation.3 | async-start | bytes 262144 | tf_op jit(solution)/shard_map/all_to_all | solution.py:339
  145.8 0.6 copy-start.9
  148.1 15.9 %copy-start.6 = (bf16[2,256,512]{2,1,0:T(8,128)(2,1)S(1)}, bf16[2,256,512]{2,1,0:T(8,128)(2,1)}, u32[]{:S(2)}) copy-start(bf16[2,256,512]{2,1,0:T(8,128)(2,1)} %copy-done.5) | copy-start | bytes 1572868
  149.9 18.1 %all-to-all-start.4 = ((f32[128,4,128]{2,1,0:T(4,128)}), f32[128,4,128]{2,1,0:T(4,128)S(1)}, u32[]{:S(2)}, u32[]{:S(2)}) async-start(f32[128,4,128]{2,1,0:T(4,128)} %reshape.294), calls=%async_computation.4 | async-start | bytes 524288 | tf_op jit(solution)/shard_map/all_to_all | solution.py:344
  168.1 10.9 %collective-permute-start.9 = (f32[256]{0:T(256)S(1)}, f32[256]{0:T(256)S(1)}, u32[]{:S(2)}, u32[]{:S(2)}) collective-permute-start(f32[256]{0:T(256)S(1)} %negate_multiply_fusion), channel_id=1, source_target_pairs={{0,32},{32,0},{1,33},{33,1},{2,34},{34,2},{3,35},{35,3},{4,36},{36... | collective-permute-start | bytes 3080 | tf_op jit(solution)/shard_map/ppermute | solution.py:101
  179.3 0.6 copy-start.13

commit v2 on v0

v2 whole, which is shorter than its diff:
```python
import functools
import math

import jax
import jax.numpy as jnp
from jax import lax
from jax.experimental import pallas as pl
from jax.experimental.pallas import tpu as pltpu
from jax.sharding import Mesh
from jax.sharding import PartitionSpec as P

cut_slope = 4.0
LN2 = math.log(2.0)
F32 = jnp.float32
BF16 = jnp.bfloat16
PLANE = ("x", "core", "rep")
EVERY = ("x", "core", "tensor", "rep")
SAME_CORE = ("x", "tensor", "rep")
LIMIT = 16 * 1024 * 1024


def place():
    return tuple(lax.axis_index(name) for name in ("x", "core", "tensor", "rep"))


def number(far, side, half):
    x, c, _, y = place()
    even = c == 0
    bx = jnp.where(even, x + (far % 4), x + (side % 4)) % 4
    by = jnp.where(even, y + (side % 4), y + (far % 4)) % 4
    return (bx * 2 + (c if half == 0 else 1 - c)) * 4 + by


def column_of(table, held):
    c = lax.axis_index("core")
    held[...] = jnp.transpose(jnp.concatenate([table, jnp.zeros((124, 128), F32)]))
    start = pl.multiple_of(c * 64, 64)
    return jnp.concatenate([held[pl.ds(start, 64), i : i + 1] for i in range(4)])


LOWS, HIGHS = (0, -1), (1, 2)
BLOCKS = [
    (far, side)
    for far, sides in (
        (0, LOWS),
        (0, HIGHS),
        (-1, LOWS),
        (1, HIGHS),
        (-1, HIGHS),
        (1, LOWS),
        (2, LOWS),
        (2, HIGHS),
    )
    for side in sides
]


def in_hbm(value):
    return pltpu.with_memory_space_constraint(value, pltpu.HBM)


def in_vmem(value):
    return pltpu.with_memory_space_constraint(value, pltpu.VMEM)


def attend_body(
    counts, q_ref, k_hbm, v_hbm, own_k_ref, own_v_ref, skip_ref, mix, out_ref, mix_out, *scratch
):
    k_ref, v_ref, own_k, own_v, held, sems, mix_sem = scratch
    rows = 4
    groups = k_ref.shape[0] // rows
    score_scale = 1.0 / math.sqrt(k_ref.shape[3])
    copies = []
    for group in range(groups):
        span = pl.ds(group * rows, rows)
        pair = [
            pltpu.make_async_copy(k_hbm.at[span], k_ref.at[span], sems.at[2 * group]),
            pltpu.make_async_copy(v_hbm.at[span], v_ref.at[span], sems.at[2 * group + 1]),
        ]
        for copy in pair:
            copy.start()
        copies.append(pair)
    mix_copy = pltpu.make_async_copy(mix, mix_out, mix_sem)
    mix_copy.start()
    own_k[...] = own_k_ref[...].astype(F32)
    own_v[...] = own_v_ref[...].astype(F32)
    for there in range(16):
        block = there % 4
        out_ref[there, :, 1024:] = skip_ref[:, block * 256 : (block + 1) * 256]

    for group in range(groups):
        first = group * rows
        spread = lambda ref: jnp.concatenate(
            [jnp.broadcast_to(ref[first + row : first + row + 1], (8, 128)) for row in range(rows)]
        )
        q = q_ref[first : first + rows].reshape(rows * 8, 128)
        own = score_scale * jnp.sum(q.astype(F32) * spread(own_k), axis=1, keepdims=True)
        copies[group][0].wait()
        scores = score_scale * jnp.concatenate(
            [
                lax.dot_general(
                    q_ref[first + row],
                    k_ref[first + row, 0],
                    (((1,), (1,)), ((), ())),
                    preferred_element_type=F32,
                )
                for row in range(rows)
            ]
        )
        position = lax.broadcasted_iota(jnp.int32, (8, scores.shape[1]), 1)
        live = jnp.concatenate([position < counts[first + row] for row in range(rows)])
        top = jnp.maximum(jnp.max(jnp.where(live, scores, -1e30), axis=1, keepdims=True), own)
        expo = jnp.where(live, jnp.exp(scores - top), 0.0)
        own_expo = jnp.exp(own - top)
        total = jnp.sum(expo, axis=1, keepdims=True) + own_expo
        weights = expo.astype(BF16)
        copies[group][1].wait()
        accum = jnp.concatenate(
            [
                jnp.dot(
                    weights[row * 8 : (row + 1) * 8],
                    v_ref[first + row, 0],
                    preferred_element_type=F32,
                )
                for row in range(rows)
            ]
        )
        accum = accum + own_expo.astype(BF16).astype(F32) * spread(own_v)
        held[first * 8 : (first + rows) * 8, :] = accum / total

    for h in range(8):
        piece = held[pl.ds(h, 16, stride=8), :].astype(BF16)
        for there in range(16):
            out_ref[there, :, h * 128 : (h + 1) * 128] = piece
    mix_copy.wait()


def attend(q, k, v, own_k, own_v, counts, skip, mix):
    vmem, anywhere = pl.BlockSpec(), pl.BlockSpec(memory_space=pl.ANY)
    own_k, own_v = own_k.reshape(16, 128), own_v.reshape(16, 128)
    return pl.pallas_call(
        attend_body,
        in_specs=[
            pl.BlockSpec(memory_space=pltpu.SMEM),
            vmem,
            anywhere,
            anywhere,
            vmem,
            vmem,
            vmem,
            anywhere,
        ],
        out_shape=[
            jax.ShapeDtypeStruct((16, 16, 1280), BF16),
            pltpu.VMEM((1024, 256), BF16),
        ],
        scratch_shapes=[
            pltpu.VMEM((16, 1, 512, 128), BF16),
            pltpu.VMEM((16, 1, 512, 128), BF16),
            pltpu.VMEM((16, 128), F32),
            pltpu.VMEM((16, 128), F32),
            pltpu.VMEM((128, 128), F32),
            pltpu.SemaphoreType.DMA((8,)),
            pltpu.SemaphoreType.DMA,
        ],
        compiler_params=pltpu.CompilerParams(vmem_limit_bytes=LIMIT),
    )(counts, *[in_hbm(value) for value in (q, k, v, own_k, own_v, skip, mix)])


def project_body(got_ref, own_ref, peer_ref, gain_ref, out_ref):
    attn = got_ref[:, :1024]
    skip = got_ref[:, 1024:].astype(F32)
    x, c, t, _ = place()
    for side, mix_ref in enumerate((own_ref, peer_ref)):
        part = jnp.dot(attn, mix_ref[...], preferred_element_type=F32)
        holds = t == 2 * x + (c if side == 0 else 1 - c)
        part = jnp.where(holds, part + skip, part).astype(BF16)
        for j in range(2):
            cols = part[:, j * 128 : (j + 1) * 128].reshape(8, 32, 128)
            out_ref[:, (2 * side + j) * 32 : (2 * side + j + 1) * 32, :] = cols
    gain = gain_ref[...]
    for there in range(8):
        out_ref[there, 128:, :] = gain


def project(got, mix_own, mix_peer, gain):
    return pl.pallas_call(
        project_body,
        out_shape=jax.ShapeDtypeStruct((8, 136, 128), BF16),
        compiler_params=pltpu.CompilerParams(vmem_limit_bytes=LIMIT),
    )(got, mix_own, mix_peer, gain)


def total_body(got_ref, out_ref, gain_ref):
    total = got_ref[0, :128, :].astype(F32)
    for source in range(1, 8):
        total += got_ref[source, :128, :].astype(F32)
    total = total.astype(BF16)
    for there in range(8):
        out_ref[there] = total
    for there in range(8):
        gain_ref[there * 8 : (there + 1) * 8, :] = got_ref[there, 128:, :].astype(F32)


def total_call(got):
    return pl.pallas_call(
        total_body,
        out_shape=[
            jax.ShapeDtypeStruct((8, 128, 128), BF16),
            jax.ShapeDtypeStruct((64, 128), F32),
        ],
        compiler_params=pltpu.CompilerParams(vmem_limit_bytes=LIMIT),
    )(got)


def turn(shift):
    pairs = []
    for x in range(4):
        for c in range(2):
            for y in range(4):
                here = (x * 2 + c) * 4 + y
                if c == 0:
                    there = (((x + shift) % 4) * 2 + c) * 4 + y
                else:
                    there = (x * 2 + c) * 4 + (y + shift) % 4
                pairs.append((here, there))
    return pairs


def turn_other(shift):
    pairs = []
    for x in range(4):
        for c in range(2):
            for y in range(4):
                here = (x * 2 + c) * 4 + y
                if c == 1:
                    there = (((x + shift) % 4) * 2 + c) * 4 + y
                else:
                    there = (x * 2 + c) * 4 + (y + shift) % 4
                pairs.append((here, there))
    return pairs


def swap_core(value):
    return lax.ppermute(value, "core", [(0, 1), (1, 0)])


def rows_of(column, copies):
    wide = jnp.broadcast_to(column, (256, 128))
    return [jnp.transpose(wide[h * 128 : (h + 1) * 128])[:1] for h in range(2)]


def fetch(lexicons, at, count, target, sems):
    copies = []
    for i in range(count):
        group = []
        for half in range(2):
            row = pl.multiple_of(number(*BLOCKS[at + i], half) * 256, 256)
            for side, lex in enumerate(lexicons):
                copy = pltpu.make_async_copy(
                    lex.at[pl.ds(row, 256), :],
                    target.at[side, pl.ds(i * 512 + half * 256, 256), :],
                    sems.at[4 * i + 2 * half + side],
                )
                copy.start()
                group.append(copy)
        copies.append(group)
    return copies


def head_body(plan, *refs):
    sides, at, ready, following, first, last = plan
    refs = list(refs)
    take = lambda n: [refs.pop(0) for _ in range(n)]
    total = sum(sides)
    sources = take(len(sides))
    gain, *lexicons = take(3)
    if not first:
        z_in, sq_in = take(2)
    if ready:
        (lexs,) = take(1)
    if last:
        sharp_ref, chosen_ref = take(2)
        z_out, pick_out, lse_out, tok_out = take(4)
    else:
        z_out, pick_out, sq_out = take(3)
    if following:
        (lex_next,) = take(1)
    if first:
        for source, copy_out in zip(sources, take(len(sources))):
            copy_out[...] = source[...]
    copies = None
    if not ready:
        lexs, sems = take(2)
        copies = fetch(lexicons, at, total, lexs, sems)
    if following:
        next_copies = fetch(lexicons, at + total, following, lex_next, *take(1))
    xs, held = take(2)
    x, c, t, y = place()
    mine = x * 4 + y
    squares = None if first else sq_in[...]
    own_piece, own_part = mine // 2, pl.multiple_of((mine % 2) * 16, 16)
    places = [(source, side) for source, some in zip(sources, sides) for side in range(some)]
    for start in range(0, total, 2):
        pair = range(start, min(start + 2, total))
        for i in pair:
            source, side = places[i]
            pick_out[i] = source[side, own_piece, :, pl.ds(own_part, 16), :]
            for j in range(4):
                wide = source[side, :, j].astype(F32).reshape(256, 128)
                squares = wide * wide if squares is None else squares + wide * wide
                row = gain[pl.ds(number(*BLOCKS[at + i], j // 2) * 2 + j % 2, 1), :]
                xs[:, i * 512 + j * 128 : i * 512 + (j + 1) * 128] = (wide * row).astype(BF16)
        if copies is not None:
            for i in pair:
                for copy in copies[i]:
                    copy.wait()
        span = slice(start * 512, (pair[-1] + 1) * 512)
        for side in range(2):
            cols = slice(side * 512, (side + 1) * 512)
            part = jnp.dot(xs[:, span], lexs[side, span, :], preferred_element_type=F32)
            if start:
                z_out[:, cols] += part
            elif first:
                z_out[:, cols] = part
            else:
                z_out[:, cols] = z_in[:, cols] + part
    if not last:
        sq_out[...] = squares
    if following:
        for group in next_copies:
            for copy in group:
                copy.wait()
    if last:
        sharp = column_of(sharp_ref[...], held)
        chosen = column_of(chosen_ref[...].astype(F32), held).astype(jnp.int32)
        scale = lax.rsqrt(jnp.sum(squares, axis=1, keepdims=True) / 8192.0 + 1e-05) * sharp
        z = z_out[...] * scale
        z_out[...] = z
        top = jnp.max(z, axis=1, keepdims=True)
        lse = top + jnp.log(jnp.sum(jnp.exp(z - top), axis=1, keepdims=True))
        token = jnp.zeros((256, 1), F32)
        for side in range(2):
            base = (((x * 2 + (c if side == 0 else 1 - c)) * 8 + t) * 4 + y) * 512
            here = lax.broadcasted_iota(jnp.int32, (256, 512), 1) == chosen - base
            part = jnp.where(here, z[:, side * 512 : (side + 1) * 512], 0.0)
            token += jnp.sum(part, axis=1, keepdims=True)
        odd = lax.broadcasted_iota(jnp.int32, (256, 128), 0) % 2
        low, high = rows_of(lse, 256)
        lse_out[...] = jnp.where(odd == 0, low, high)
        low, high = rows_of(token, 256)
        tok_out[0:1, :] = low
        tok_out[1:2, :] = high


def head_call(sources, at, following, gain, lex_own, lex_peer, state, lexs, closing):
    sides = [source.shape[0] for source in sources]
    total = sum(sides)
    first, ready, last = state is None, lexs is not None, closing is not None
    vmem, anywhere = pl.BlockSpec(), pl.BlockSpec(memory_space=pl.ANY)
    in_specs = [vmem] * (len(sources) + 1) + [anywhere] * 2
    operands = [*sources, gain, in_hbm(lex_own), in_hbm(lex_peer)]
    for extra in (state, lexs, closing):
        if extra is not None:
            operands += list(extra)
            in_specs += [vmem] * len(extra)
    out_shape = [
        jax.ShapeDtypeStruct((256, 1024), F32),
        jax.ShapeDtypeStruct((total, 4, 16, 128), BF16),
    ]
    scratch = []
    if last:
        out_shape += [
            jax.ShapeDtypeStruct((256, 128), F32),
            jax.ShapeDtypeStruct((2, 128), F32),
        ]
    else:
        out_shape += [jax.ShapeDtypeStruct((256, 128), F32)]
    if following:
        out_shape += [pltpu.VMEM((2, 512 * following, 512), BF16)]
    if first:
        out_shape += [jax.ShapeDtypeStruct(source.shape, source.dtype) for source in sources]
    if not ready:
        scratch += [pltpu.VMEM((2, 512 * total, 512), BF16), pltpu.SemaphoreType.DMA((4 * total,))]
    if following:
        scratch += [pltpu.SemaphoreType.DMA((4 * following,))]
    scratch += [pltpu.VMEM((256, 512 * total), BF16), pltpu.VMEM((128, 128), F32)]
    return pl.pallas_call(
        functools.partial(head_body, (sides, at, ready, following, first, last)),
        in_specs=in_specs,
        out_shape=out_shape,
        scratch_shapes=scratch,
        compiler_params=pltpu.CompilerParams(vmem_limit_bytes=LIMIT),
        cost_estimate=pl.CostEstimate(
            flops=2 * 256 * 512 * 1024 * total,
            bytes_accessed=total * (2**20 + 2**18) + 2**21,
            transcendentals=0,
        ),
    )(*operands)


def pile_body(first_ref, second_ref, out_ref):
    out_ref[0] = first_ref[...]
    out_ref[1] = second_ref[...]


def pile(first, second):
    return pl.pallas_call(
        pile_body,
        out_shape=jax.ShapeDtypeStruct((2, 8, 4, 32, 128), BF16),
        compiler_params=pltpu.CompilerParams(vmem_limit_bytes=LIMIT),
        cost_estimate=pl.CostEstimate(flops=0, bytes_accessed=2**20, transcendentals=0),
    )(first, second)


def mass_body(z_ref, lse_ref, tok_ref, level_ref, *refs):
    picks, (out_ref, norm_out, hidden_out, heap, held) = refs[:-5], refs[-5:]
    at = 0
    for pick in picks:
        heap[at : at + pick.shape[0]] = pick[...]
        at += pick.shape[0]
    x, c, t, y = place()
    spots = [(far % 4, side % 4) for far, side in BLOCKS]
    for yb in range(4):
        dx, dy = (t // 2 - x + 4) % 4, (yb - y + 4) % 4
        far, side = jnp.where(c == 0, dx, dy), jnp.where(c == 0, dy, dx)
        spot = jnp.int32(0)
        for i, (f, s) in enumerate(spots):
            spot = jnp.where((far == f) & (side == s), i, spot)
        piece = heap[spot]
        for j in range(2):
            cols = slice(yb * 256 + j * 128, yb * 256 + (j + 1) * 128)
            hidden_out[:, cols] = jnp.where(t % 2 == c, piece[j], piece[2 + j])
    level = column_of(level_ref[...], held)
    parts = lse_ref[...]
    odd = lax.broadcasted_iota(jnp.int32, parts.shape, 0) % 2
    columns = []
    for h in range(2):
        top = jnp.max(jnp.where(odd == h, parts, -jnp.inf), axis=0, keepdims=True)
        total = jnp.sum(jnp.where(odd == h, jnp.exp(parts - top), 0.0), axis=0, keepdims=True)
        norm = top + jnp.log(total)
        norm_out[h : h + 1, :] = norm
        columns.append(jnp.transpose(jnp.broadcast_to(norm, (128, 128)))[:, :1])
    logp = z_ref[...] - jnp.concatenate(columns, axis=0)
    gate = cut_slope * (level + logp * (1.0 / LN2))
    kept = jnp.sum(jnp.exp(logp) / (1.0 + jnp.exp(-gate)), axis=1, keepdims=True)
    low, high = rows_of(kept, 512)
    which = lax.broadcasted_iota(jnp.int32, (512, 128), 0) % 4
    out_ref[...] = jnp.where(
        which == 0,
        low,
        jnp.where(which == 1, high, jnp.where(which == 2, tok_ref[0:1, :], tok_ref[1:2, :])),
    )


def mass_call(z, lse, tok, level, picks):
    return pl.pallas_call(
        mass_body,
        out_shape=[
            jax.ShapeDtypeStruct((512, 128), F32),
            jax.ShapeDtypeStruct((2, 128), F32),
            jax.ShapeDtypeStruct((16, 1024), BF16),
        ],
        scratch_shapes=[pltpu.VMEM((16, 4, 16, 128), BF16), pltpu.VMEM((128, 128), F32)],
        compiler_params=pltpu.CompilerParams(vmem_limit_bytes=LIMIT),
    )(z, lse, tok, level, *picks)


def shards(
    probe_vectors,
    stored_lookup_vectors,
    stored_content_vectors,
    fresh_lookup_vector,
    fresh_content_vector,
    history_counts,
    mixing_matrix,
    skip_stream,
    closing_multiplier,
    lexicon_matrix,
    sharpening_factor,
    desired_perplexity,
    chosen_symbols,
):
    mix_peer = swap_core(mixing_matrix)
    lex_peer = swap_core(lexicon_matrix)

    sent, mix_own = attend(
        probe_vectors,
        stored_lookup_vectors,
        stored_content_vectors,
        fresh_lookup_vector,
        fresh_content_vector,
        history_counts,
        skip_stream,
        mixing_matrix,
    )
    got = lax.all_to_all(sent, ("x", "rep"), 0, 0, tiled=True).reshape(256, 1280)
    gain_rows = closing_multiplier.reshape(8, 128)
    sent = project(got, mix_own, mix_peer, gain_rows)
    got = lax.all_to_all(sent, "tensor", 0, 0, tiled=True)
    sent, gain = total_call(got)

    own = lax.all_to_all(sent, "tensor", 0, 0, tiled=True).reshape(8, 4, 32, 128)
    side = lambda v, s: lax.ppermute(v, PLANE, turn_other(s))
    far = lambda v, s: lax.ppermute(v, PLANE, turn(s))
    low = pile(own, side(own, 1))
    high = pile(side(own, -1), side(own, 2))
    left_low, right_high = far(low, 1), far(high, -1)
    past_low, past_high = far(left_low, 1), far(right_high, -1)

    fixed = (gain, lexicon_matrix, lex_peer)
    z, pick_0, sq, low, high = head_call([low, high], 0, 0, *fixed, None, None, None)
    left_high, right_low = far(high, 1), far(low, -1)
    z, pick_1, sq = head_call([left_low, right_high], 4, 0, *fixed, (z, sq), None, None)
    z, pick_2, sq, lexs = head_call([left_high, right_low], 8, 4, *fixed, (z, sq), None, None)
    closing = (sharpening_factor.reshape(4, 128), chosen_symbols.reshape(4, 128))
    z, pick_3, lse, tok = head_call(
        [past_low, past_high], 12, 0, *fixed, (z, sq), (lexs,), closing
    )
    picked = [pick_0, pick_1, pick_2, pick_3]
    every_lse = lax.all_to_all(lse.reshape(128, 2, 128), SAME_CORE, 0, 0, tiled=True)
    levels = desired_perplexity.reshape(4, 128)
    sent, norm, hidden = mass_call(z, every_lse.reshape(256, 128), tok, levels, picked)
    got = lax.all_to_all(sent.reshape(128, 4, 128), SAME_CORE, 0, 0, tiled=True)
    kept, tok = jnp.sum(got, axis=0).reshape(2, 256)
    token_logp = tok - norm.reshape(256)
    c = lax.axis_index("core")
    level = lax.dynamic_index_in_dim(desired_perplexity.reshape(4, 2, 64), c, 1, keepdims=False)
    level = level.reshape(256)
    token_logw = token_logp + jax.nn.log_sigmoid(cut_slope * (level + token_logp / LN2))
    mine_out = -(token_logw - jnp.log(kept)) / LN2
    peer_out = swap_core(mine_out)
    even = jnp.where(c == 0, mine_out, peer_out).reshape(4, 64)
    odd = jnp.where(c == 0, peer_out, mine_out).reshape(4, 64)
    surprise = jnp.stack([even, odd], axis=1).reshape(512)
    next_targets = desired_perplexity - 0.1 * (surprise - 5.0)
    return (hidden, next_targets, surprise)


def solution(mesh):
    fine = Mesh(mesh.devices.reshape(4, 2, 8, 4), ("x", "core", "tensor", "rep"))
    rows = ("x", "core", "rep")
    placed = (
        P(rows, "tensor", None),
        P(rows, "tensor", None, None),
        P(rows, "tensor", None, None),
        P(rows, "tensor", None),
        P(rows, "tensor", None),
        P(rows),
        P("tensor", rows),
        P(rows, "tensor"),
        P("tensor"),
        P(None, ("x", "core", "tensor", "rep")),
        P(),
        P(),
        P(),
    )
    return jax.shard_map(
        shards,
        mesh=fine,
        in_specs=placed,
        out_specs=(P(rows, "tensor"), P(), P()),
        check_vma=False,
    )
```

time: 466 us -> 140 us (0.30)
  blocking collectives: 272 us -> 45.9 us
  waiting for transfers between devices: 156 us -> 37.1 us
  starting transfers between devices: 0.12 us -> 34 us
  Pallas kernels: 0 us -> 20.3 us
  matrix products: 17.1 us -> 0 us
  between operations: 13.9 us -> 0.78 us
    psum x3 -> x0, blocking collectives: 160 us -> none  [the longest x1 74.3 us: shards(): lax.psum((local_total, token_part), ('group', 'tensor', 'rep'))]
    all_gather x2 -> x0, waiting for transfers between devices: 125 us -> none  [the longest x1 72.8 us: shards(): lax.all_gather(features, ('group', 'rep'), axis=0, tiled=True)]
    pmax x1 -> x0, blocking collectives: 75.8 us -> none  [shards(): lax.pmax(jnp.max(unnormalized_odds, axis=1), ('group', 'tensor', 'rep'))]
    reduce_scatter x1 -> x0, waiting for transfers between devices: 30.9 us -> none  [shards(): summed = lax.psum_scatter(terms, 'tensor', scatter_dimension=1, tiled=True)]
    all_to_all x1 -> x3, blocking collectives: 16 us -> 45.9 us  [the longest x1 17.5 us: shards(): got = lax.all_to_all(sent, 'tensor', 0, 0, tiled=True)]
    ppermute x0 -> x12, starting transfers between devices: none -> 22.8 us  [the longest x3 13.5 us: swap_core(): return lax.ppermute(value, 'core', [(0, 1), (1, 0)])]
    all_to_all x0 -> x2, waiting for transfers between devices: none -> 20.9 us  [the longest x1 11.7 us: shards(): got = lax.all_to_all(sent.reshape(128, 4, 128), SAME_CORE, 0, 0, tiled=True)]
    all_gather x1 -> x0, blocking collectives: 20.6 us -> none  [shards(): features = lax.all_gather(rescaled_stream, 'tensor', axis=1, tiled=True)]
  transfers between devices with their start and end apart: 3 -> 14, of which waited for: 3 -> 11; matrix products, arithmetic and copies ran while one was open for 0% -> 0% of each run, Pallas kernels for 0% -> 12%
where the time goes in v2:
time: 140 us
  blocking collectives  45.9 us (33%)
  waiting for transfers between devices  37.1 us (26%)
  starting transfers between devices  34 us (24%)
  Pallas kernels  20.3 us (14%)
    all_to_all x1, blocking collectives, shards(): got = lax.all_to_all(sent, 'tensor', 0, 0, tiled=True)  17.5 us
    all_to_all x1, blocking collectives, shards(): lax.all_to_all(lse.reshape(128, 2, 128), SAME_CORE, 0, 0, tiled=True)  16.5 us
    ppermute x3, starting transfers between devices, swap_core(): return lax.ppermute(value, 'core', [(0, 1), (1, 0)])  13.5 us
    pallas_call x4, Pallas kernels, head_call(): pl.pallas_call(functools.partial(head_body, (sides, at, ready, following,...  12.7 us
    all_to_all x1, blocking collectives, shards(): lax.all_to_all(sent, 'tensor', 0, 0, tiled=True).reshape(8, 4, 32, 128)  11.9 us
    all_to_all x1, waiting for transfers between devices, shards(): got = lax.all_to_all(sent.reshape(128, 4, 128), SAME_CORE, 0, 0, tiled=True)  11.7 us
    all_to_all x1, waiting for transfers between devices, shards(): lax.all_to_all(sent, ('x', 'rep'), 0, 0, tiled=True).reshape(256, 1280)  9.14 us
    ppermute x3, waiting for transfers between devices, shards(): side = lambda v, s: lax.ppermute(v, PLANE, turn_other(s))  8.05 us
  transfers between devices with their start and end apart: 14, of which 11 were waited for; matrix products, arithmetic and copies ran while one was open for 0% of the time, Pallas kernels for 12%

profile of v2, /device:TPU:1, one launch (start us, length us, event | category | flops | bytes accessed | tf_op | source)
XLA Modules:
  0.0 139.9 jit_solution(9638223395194364396)
XLA Ops:
  0.6 0.0 copy-start.1
  0.6 3.3 %collective-permute-start.8 = (bf16[8192,512]{1,0:T(8,128)(2,1)}, bf16[8192,512]{1,0:T(8,128)(2,1)}, u32[]{:S(2)}, u32[]{:S(2)}) collective-permute-start(bf16[8192,512]{1,0:T(8,128)(2,1)} %refs_3_.7), channel_id=1, source_target_pairs={{0,32},{32,0},{1,33},{33,1},{2,34},{34,2},{3,35},{35,3},{4,36},{36... | collective-permute-start | bytes 25165832 | tf_op jit(solution)/shard_map/ppermute | solution.py:245
  4.0 0.0 copy-start.4
  4.0 0.7 copy-done.4
  4.6 0.0 copy-start.5
  4.6 5.4 %shard_map.148 = (bf16[16,16,1280]{2,1,0:T(8,128)(2,1)}, bf16[1024,256]{1,0:T(8,128)(2,1)S(1)}) custom-call(s32[16]{0:T(128)S(1)} %copy-done.4, bf16[16,8,128]{2,1,0:T(8,128)(2,1)} %q_ref.1, bf16[16,1,512,128]{3,2,1,0:T(8,128)(2,1)} %k_hbm.1, bf16[16,1,512,128]{3,2,1,0:T(8,128)(2,1)} %v_hbm.1, bf16[16,128]{1,0:T(8,128)(2,1)} %bitcast.39, ...), custom_call_target="tpu_custom_call" | custom-call | tf_op jit(solution)/shard_map/pallas_call | solution.py:141
  10.0 5.0 %all-to-all-start = ((bf16[16,16,1280]{2,1,0:T(8,128)(2,1)}), bf16[16,16,1280]{2,1,0:T(8,128)(2,1)S(1)}, u32[]{:S(2)}, u32[]{:S(2)}) async-start(bf16[16,16,1280]{2,1,0:T(8,128)(2,1)} %get-tuple-element.26), calls=%async_computation | async-start | bytes 1310720 | tf_op jit(solution)/shard_map/all_to_all | solution.py:497
  15.1 0.0 copy-done.5
  15.1 0.4 collective-permute-start
  15.5 2.0 %collective-permute-done.peer_ref = bf16[1024,256]{1,0:T(8,128)(2,1)S(1)} collective-permute-done((bf16[1024,256]{1,0:T(8,128)(2,1)S(1)}, bf16[1024,256]{1,0:T(8,128)(2,1)S(1)}, u32[]{:S(2)}, u32[]{:S(2)}) %collective-permute-start) | collective-permute-done | bytes 524320 | tf_op jit(solution)/shard_map/ppermute | solution.py:245
  17.5 9.1 %all-to-all-done = bf16[16,16,1280]{2,1,0:T(8,128)(2,1)S(1)} async-done(((bf16[16,16,1280]{2,1,0:T(8,128)(2,1)}), bf16[16,16,1280]{2,1,0:T(8,128)(2,1)S(1)}, u32[]{:S(2)}, u32[]{:S(2)}) %all-to-all-start) | async-done | bytes 655392 | tf_op jit(solution)/shard_map/all_to_all | solution.py:497
  26.7 0.0 copy-done.1
  26.7 0.4 shard_map.149
  27.1 17.5 %all_to_all.25.got_ref = bf16[8,136,128]{2,1,0:T(8,128)(2,1)S(1)} all-to-all(bf16[8,136,128]{2,1,0:T(8,128)(2,1)S(1)} %shard_map.149), channel_id=1, replica_groups=mesh['x'=4,'core'=2,'tensor'=8,'rep'=4] {'tensor'}, dimensions={0} | all-to-all | bytes 557056 | tf_op jit(solution)/shard_map/all_to_all | solution.py:500
  44.6 11.9 %all_to_all.26 = bf16[8,128,128]{2,1,0:T(8,128)(2,1)S(1)} all-to-all(bf16[8,128,128]{2,1,0:T(8,128)(2,1)S(1)} %get-tuple-element.28), channel_id=1, replica_groups=mesh['x'=4,'core'=2,'tensor'=8,'rep'=4] {'tensor'}, dimensions={0} | all-to-all | bytes 524288 | tf_op jit(solution)/shard_map/all_to_all | solution.py:503
  56.5 2.6 %collective-permute-start.4 = (bf16[8,4,32,128]{3,2,1,0:T(8,128)(2,1)S(1)}, bf16[8,4,32,128]{3,2,1,0:T(8,128)(2,1)S(1)}, u32[]{:S(2)}, u32[]{:S(2)}) collective-permute-start(bf16[8,4,32,128]{3,2,1,0:T(8,128)(2,1)S(1)} %bitcast.29), channel_id=1, source_target_pairs={{0,3},{1,0},{2,1},{3,2},{32,224},{33,225},{34,226},{35,227},{64,67... | collective-permute-start | bytes 786440 | tf_op jit(solution)/shard_map/ppermute | solution.py:504
  59.1 0.6 collective-permute-start.5
  59.7 0.0 collective-permute-start.1
  59.7 5.5 %collective-permute-done.4.first_ref = bf16[8,4,32,128]{3,2,1,0:T(8,128)(2,1)S(1)} collective-permute-done((bf16[8,4,32,128]{3,2,1,0:T(8,128)(2,1)S(1)}, bf16[8,4,32,128]{3,2,1,0:T(8,128)(2,1)S(1)}, u32[]{:S(2)}, u32[]{:S(2)}) %collective-permute-start.4) | collective-permute-done | bytes 262176 | tf_op jit(solution)/shard_map/ppermute | solution.py:504
  65.2 0.7 collective-permute-done.5.second_ref
  66.0 1.1 collective-permute-start.6
  67.1 1.8 %collective-permute-done.1.second_ref = bf16[8,4,32,128]{3,2,1,0:T(8,128)(2,1)S(1)} collective-permute-done((bf16[8,4,32,128]{3,2,1,0:T(8,128)(2,1)S(1)}, bf16[8,4,32,128]{3,2,1,0:T(8,128)(2,1)S(1)}, u32[]{:S(2)}, u32[]{:S(2)}) %collective-permute-start.1) | collective-permute-done | bytes 262176 | tf_op jit(solution)/shard_map/ppermute | solution.py:504
  69.0 0.1 collective-permute-start.2
  69.1 0.0 collective-permute-done.8.refs_4_
  69.1 3.2 %shard_map.153 = (f32[256,1024]{1,0:T(8,128)S(1)}, bf16[4,4,16,128]{3,2,1,0:T(8,128)(2,1)S(1)}, f32[256,128]{1,0:T(8,128)S(1)}, bf16[2,8,4,32,128]{4,3,2,1,0:T(8,128)(2,1)S(1)}, bf16[2,8,4,32,128]{4,3,2,1,0:T(8,128)(2,1)S(1)}) custom-call(bf16[2,8,4,32,128]{4,3,2,1,0:T(8,128)(2,1)S(1)} %shard_map.151.refs_0_, ...), custom_call_target="tpu_custom_call" | custom-call | flops 1073741824 | bytes 7340032 | tf_op jit(solution)/shard_map/pallas_call | solution.py:388
  72.2 2.7 %collective-permute-start.10 = (bf16[2,8,4,32,128]{4,3,2,1,0:T(8,128)(2,1)S(1)}, bf16[2,8,4,32,128]{4,3,2,1,0:T(8,128)(2,1)S(1)}, u32[]{:S(2)}, u32[]{:S(2)}) collective-permute-start(bf16[2,8,4,32,128]{4,3,2,1,0:T(8,128)(2,1)S(1)} %get-tuple-element.31), channel_id=1, source_target_pairs={{0,192},{1,193},{2,194},{3,195},{32,35},{33,32},{34,33},{35,34},{6... | collective-permute-start | bytes 1572872 | tf_op jit(solution)/shard_map/ppermute | solution.py:505
  75.0 0.0 collective-permute-start.9
  75.0 0.8 collective-permute-done.6.refs_1_
  75.8 2.2 %collective-permute-start.7 = (bf16[2,8,4,32,128]{4,3,2,1,0:T(8,128)(2,1)S(1)}, bf16[2,8,4,32,128]{4,3,2,1,0:T(8,128)(2,1)S(1)}, u32[]{:S(2)}, u32[]{:S(2)}) collective-permute-start(bf16[2,8,4,32,128]{4,3,2,1,0:T(8,128)(2,1)S(1)} %collective-permute-done.6.refs_1_), channel_id=1, source_target_pairs={{0,192},{1,193},{2,194},{3,195},{32,35},{33,32},{34,33},{35,34},{6... | collective-permute-start | bytes 1572872 | tf_op jit(solution)/shard_map/ppermute | solution.py:505
  77.9 0.9 collective-permute-done.2.refs_0_
  78.8 0.0 collective-permute-start.3
  78.8 3.3 %shard_map.154 = (f32[256,1024]{1,0:T(8,128)S(1)}, bf16[4,4,16,128]{3,2,1,0:T(8,128)(2,1)S(1)}, f32[256,128]{1,0:T(8,128)S(1)}) custom-call(bf16[2,8,4,32,128]{4,3,2,1,0:T(8,128)(2,1)S(1)} %collective-permute-done.2.refs_0_, bf16[2,8,4,32,128]{4,3,2,1,0:T(8,128)(2,1)S(1)} %collective-permute-done.6.refs_1_, f32[64,128]{1,0:T(8,128)S(1)} %get-tuple-element.29.refs_2_, ...), custom_call_target="tpu_custom_call" | custom-call | flops 1073741824 | bytes 7340032 | tf_op jit(solution)/shard_map/pallas_call | solution.py:388
  82.1 0.0 collective-permute-done.10.refs_1_
  82.1 2.1 %collective-permute-done.9.refs_0_ = bf16[2,8,4,32,128]{4,3,2,1,0:T(8,128)(2,1)S(1)} collective-permute-done((bf16[2,8,4,32,128]{4,3,2,1,0:T(8,128)(2,1)S(1)}, bf16[2,8,4,32,128]{4,3,2,1,0:T(8,128)(2,1)S(1)}, u32[]{:S(2)}, u32[]{:S(2)}) %collective-permute-start.9) | collective-permute-done | bytes 524320 | tf_op jit(solution)/shard_map/ppermute | solution.py:505
  84.2 0.0 copy-start.2
  84.2 0.0 copy-start.3
  84.2 4.3 %shard_map.155 = (f32[256,1024]{1,0:T(8,128)S(1)}, bf16[4,4,16,128]{3,2,1,0:T(8,128)(2,1)S(1)}, f32[256,128]{1,0:T(8,128)S(1)}, bf16[2,2048,512]{2,1,0:T(8,128)(2,1)S(1)}) custom-call(bf16[2,8,4,32,128]{4,3,2,1,0:T(8,128)(2,1)S(1)} %collective-permute-done.9.refs_0_, bf16[2,8,4,32,128]{4,3,2,1,0:T(8,128)(2,1)S(1)} %collective-permute-done.10.refs_1_, ...), custom_call_target="tpu_custom_call" | custom-call | flops 1073741824 | bytes 7340032 | tf_op jit(solution)/shard_map/pallas_call | solution.py:388
  88.6 0.0 collective-permute-done.7.refs_1_
  88.6 1.6 %collective-permute-done.3.refs_0_ = bf16[2,8,4,32,128]{4,3,2,1,0:T(8,128)(2,1)S(1)} collective-permute-done((bf16[2,8,4,32,128]{4,3,2,1,0:T(8,128)(2,1)S(1)}, bf16[2,8,4,32,128]{4,3,2,1,0:T(8,128)(2,1)S(1)}, u32[]{:S(2)}, u32[]{:S(2)}) %collective-permute-start.3) | collective-permute-done | bytes 524320 | tf_op jit(solution)/shard_map/ppermute | solution.py:505
  90.1 0.0 copy-done.2
  90.1 0.0 copy-done.3
  90.1 0.0 copy-start
  90.1 1.9 %shard_map.156 = (f32[256,1024]{1,0:T(8,128)S(1)}, bf16[4,4,16,128]{3,2,1,0:T(8,128)(2,1)S(1)}, f32[256,128]{1,0:T(8,128)S(1)}, f32[2,128]{1,0:T(2,128)S(1)}) custom-call(bf16[2,8,4,32,128]{4,3,2,1,0:T(8,128)(2,1)S(1)} %collective-permute-done.3.refs_0_, bf16[2,8,4,32,128]{4,3,2,1,0:T(8,128)(2,1)S(1)} %collective-permute-done.7.refs_1_, ...), custom_call_target="tpu_custom_call" | custom-call | flops 1073741824 | bytes 7340032 | tf_op jit(solution)/shard_map/pallas_call | solution.py:388
  92.1 16.5 %all_to_all.27 = f32[128,2,128]{2,1,0:T(2,128)S(1)} all-to-all(f32[128,2,128]{2,1,0:T(2,128)S(1)} %bitcast.34), channel_id=1, replica_groups=mesh['x'=4,'core'=2,'tensor'=8,'rep'=4] {'x','tensor','rep'}, dimensions={0} | all-to-all | bytes 262144 | tf_op jit(solution)/shard_map/all_to_all | solution.py:521
  108.6 0.0 copy-done
  108.6 1.6 %shard_map.157 = (f32[512,128]{1,0:T(8,128)}, f32[2,128]{1,0:T(2,128)S(1)}, bf16[16,1024]{1,0:T(8,128)(2,1)}) custom-call(f32[256,1024]{1,0:T(8,128)S(1)} %get-tuple-element.39.z_ref, f32[256,128]{1,0:T(8,128)S(1)} %bitcast.33, f32[2,128]{1,0:T(2,128)S(1)} %get-tuple-element.41.tok_ref, f32[4,128]{1,0:T(4,128)S(1)} %bitcast.35, ...), custom_call_target="tpu_custom_call" | custom-call | tf_op jit(solution)/shard_map/pallas_call | solution.py:457
  110.2 6.2 %all-to-all-start.4 = ((f32[128,4,128]{2,1,0:T(4,128)}), f32[128,4,128]{2,1,0:T(4,128)S(1)}, u32[]{:S(2)}, u32[]{:S(2)}) async-start(f32[128,4,128]{2,1,0:T(4,128)} %bitcast.10), calls=%async_computation.4 | async-start | bytes 524288 | tf_op jit(solution)/shard_map/all_to_all | solution.py:524
  116.4 0.1 reshape.68
  116.5 0.1 reshape.69
  116.6 11.7 %all-to-all-done.4 = f32[128,4,128]{2,1,0:T(4,128)S(1)} async-done(((f32[128,4,128]{2,1,0:T(4,128)}), f32[128,4,128]{2,1,0:T(4,128)S(1)}, u32[]{:S(2)}, u32[]{:S(2)}) %all-to-all-start.4) | async-done | bytes 262176 | tf_op jit(solution)/shard_map/all_to_all | solution.py:524
  128.3 0.1 reduce_sum.9
  128.5 9.8 %collective-permute-start.11 = (f32[256]{0:T(256)S(1)}, f32[256]{0:T(256)S(1)}, u32[]{:S(2)}, u32[]{:S(2)}) collective-permute-start(f32[256]{0:T(256)S(1)} %negate_multiply_fusion), channel_id=1, source_target_pairs={{0,32},{32,0},{1,33},{33,1},{2,34},{34,2},{3,35},{35,3},{4,36},{36... | collective-permute-start | bytes 3080 | tf_op jit(solution)/shard_map/ppermute | solution.py:245
  138.2 0.8 collective-permute-done.11
  139.1 0.1 stack_reshape.6
  139.1 0.1 stack_reshape.7
  139.2 0.1 reshape.70
  139.3 0.0 copy-start.6
  139.3 0.6 multiply_subtract_fusion
  139.9 0.0 copy-done.6
  (7 shorter events, 0.2 us)
Async XLA Ops:
  0.6 26.0 %copy-start.1 = (bf16[1024]{0:T(1024)(128)(2,1)S(1)}, bf16[1024]{0:T(1024)(128)(2,1)}, u32[]{:S(2)}) copy-start(bf16[1024]{0:T(1024)(128)(2,1)} %param.21) | copy-start | bytes 6148
  0.6 68.4 %collective-permute-start.8 = (bf16[8192,512]{1,0:T(8,128)(2,1)}, bf16[8192,512]{1,0:T(8,128)(2,1)}, u32[]{:S(2)}, u32[]{:S(2)}) collective-permute-start(bf16[8192,512]{1,0:T(8,128)(2,1)} %refs_3_.7), channel_id=1, source_target_pairs={{0,32},{32,0},{1,33},{33,1},{2,34},{34,2},{3,35},{35,3},{4,36},{36... | collective-permute-start | bytes 25165832 | tf_op jit(solution)/shard_map/ppermute | solution.py:245
  4.0 0.7 copy-start.4
  4.6 10.5 %copy-start.5 = (bf16[1024,256]{1,0:T(8,128)(2,1)S(1)}, bf16[1024,256]{1,0:T(8,128)(2,1)}, u32[]{:S(2)}) copy-start(bf16[1024,256]{1,0:T(8,128)(2,1)} %mix.1) | copy-start | bytes 1572868
  10.0 16.6 %all-to-all-start = ((bf16[16,16,1280]{2,1,0:T(8,128)(2,1)}), bf16[16,16,1280]{2,1,0:T(8,128)(2,1)S(1)}, u32[]{:S(2)}, u32[]{:S(2)}) async-start(bf16[16,16,1280]{2,1,0:T(8,128)(2,1)} %get-tuple-element.26), calls=%async_computation | async-start | bytes 1310720 | tf_op jit(solution)/shard_map/all_to_all | solution.py:497
  15.1 2.4 %collective-permute-start = (bf16[1024,256]{1,0:T(8,128)(2,1)S(1)}, bf16[1024,256]{1,0:T(8,128)(2,1)S(1)}, u32[]{:S(2)}, u32[]{:S(2)}) collective-permute-start(bf16[1024,256]{1,0:T(8,128)(2,1)S(1)} %copy-done.5), channel_id=1, source_target_pairs={{0,32},{32,0},{1,33},{33,1},{2,34},{34,2},{3,35},{35,3},{4,36},{36... | collective-permute-start | bytes 1572872 | tf_op jit(solution)/shard_map/ppermute | solution.py:245
  56.5 8.7 %collective-permute-start.4 = (bf16[8,4,32,128]{3,2,1,0:T(8,128)(2,1)S(1)}, bf16[8,4,32,128]{3,2,1,0:T(8,128)(2,1)S(1)}, u32[]{:S(2)}, u32[]{:S(2)}) collective-permute-start(bf16[8,4,32,128]{3,2,1,0:T(8,128)(2,1)S(1)} %bitcast.29), channel_id=1, source_target_pairs={{0,3},{1,0},{2,1},{3,2},{32,224},{33,225},{34,226},{35,227},{64,67... | collective-permute-start | bytes 786440 | tf_op jit(solution)/shard_map/ppermute | solution.py:504
  59.1 6.8 %collective-permute-start.5 = (bf16[8,4,32,128]{3,2,1,0:T(8,128)(2,1)S(1)}, bf16[8,4,32,128]{3,2,1,0:T(8,128)(2,1)S(1)}, u32[]{:S(2)}, u32[]{:S(2)}) collective-permute-start(bf16[8,4,32,128]{3,2,1,0:T(8,128)(2,1)S(1)} %bitcast.30), channel_id=1, source_target_pairs={{0,2},{1,3},{2,0},{3,1},{32,160},{33,161},{34,162},{35,163},{64,66... | collective-permute-start | bytes 786440 | tf_op jit(solution)/shard_map/ppermute | solution.py:504
  59.7 9.2 %collective-permute-start.1 = (bf16[8,4,32,128]{3,2,1,0:T(8,128)(2,1)S(1)}, bf16[8,4,32,128]{3,2,1,0:T(8,128)(2,1)S(1)}, u32[]{:S(2)}, u32[]{:S(2)}) collective-permute-start(bf16[8,4,32,128]{3,2,1,0:T(8,128)(2,1)S(1)} %bitcast.31), channel_id=1, source_target_pairs={{0,1},{1,2},{2,3},{3,0},{32,96},{33,97},{34,98},{35,99},{64,65},{6... | collective-permute-start | bytes 786440 | tf_op jit(solution)/shard_map/ppermute | solution.py:504
  66.0 9.8 %collective-permute-start.6 = (bf16[2,8,4,32,128]{4,3,2,1,0:T(8,128)(2,1)S(1)}, bf16[2,8,4,32,128]{4,3,2,1,0:T(8,128)(2,1)S(1)}, u32[]{:S(2)}, u32[]{:S(2)}) collective-permute-start(bf16[2,8,4,32,128]{4,3,2,1,0:T(8,128)(2,1)S(1)} %shard_map.152.refs_1_), channel_id=1, source_target_pairs={{0,192},{1,193},{2,194},{3,195},{32,35},{33,32},{34,33},{35,34},{6... | collective-permute-start | bytes 1572872 | tf_op jit(solution)/shard_map/ppermute | solution.py:505
  69.0 9.8 %collective-permute-start.2 = (bf16[2,8,4,32,128]{4,3,2,1,0:T(8,128)(2,1)S(1)}, bf16[2,8,4,32,128]{4,3,2,1,0:T(8,128)(2,1)S(1)}, u32[]{:S(2)}, u32[]{:S(2)}) collective-permute-start(bf16[2,8,4,32,128]{4,3,2,1,0:T(8,128)(2,1)S(1)} %shard_map.151.refs_0_), channel_id=1, source_target_pairs={{0,64},{1,65},{2,66},{3,67},{32,33},{33,34},{34,35},{35,32},{64,12... | collective-permute-start | bytes 1572872 | tf_op jit(solution)/shard_map/ppermute | solution.py:505
  72.2 9.9 %collective-permute-start.10 = (bf16[2,8,4,32,128]{4,3,2,1,0:T(8,128)(2,1)S(1)}, bf16[2,8,4,32,128]{4,3,2,1,0:T(8,128)(2,1)S(1)}, u32[]{:S(2)}, u32[]{:S(2)}) collective-permute-start(bf16[2,8,4,32,128]{4,3,2,1,0:T(8,128)(2,1)S(1)} %get-tuple-element.31), channel_id=1, source_target_pairs={{0,192},{1,193},{2,194},{3,195},{32,35},{33,32},{34,33},{35,34},{6... | collective-permute-start | bytes 1572872 | tf_op jit(solution)/shard_map/ppermute | solution.py:505
  75.0 9.2 %collective-permute-start.9 = (bf16[2,8,4,32,128]{4,3,2,1,0:T(8,128)(2,1)S(1)}, bf16[2,8,4,32,128]{4,3,2,1,0:T(8,128)(2,1)S(1)}, u32[]{:S(2)}, u32[]{:S(2)}) collective-permute-start(bf16[2,8,4,32,128]{4,3,2,1,0:T(8,128)(2,1)S(1)} %get-tuple-element.30), channel_id=1, source_target_pairs={{0,64},{1,65},{2,66},{3,67},{32,33},{33,34},{34,35},{35,32},{64,12... | collective-permute-start | bytes 1572872 | tf_op jit(solution)/shard_map/ppermute | solution.py:505
  75.8 12.8 %collective-permute-start.7 = (bf16[2,8,4,32,128]{4,3,2,1,0:T(8,128)(2,1)S(1)}, bf16[2,8,4,32,128]{4,3,2,1,0:T(8,128)(2,1)S(1)}, u32[]{:S(2)}, u32[]{:S(2)}) collective-permute-start(bf16[2,8,4,32,128]{4,3,2,1,0:T(8,128)(2,1)S(1)} %collective-permute-done.6.refs_1_), channel_id=1, source_target_pairs={{0,192},{1,193},{2,194},{3,195},{32,35},{33,32},{34,33},{35,34},{6... | collective-permute-start | bytes 1572872 | tf_op jit(solution)/shard_map/ppermute | solution.py:505
  78.8 11.3 %collective-permute-start.3 = (bf16[2,8,4,32,128]{4,3,2,1,0:T(8,128)(2,1)S(1)}, bf16[2,8,4,32,128]{4,3,2,1,0:T(8,128)(2,1)S(1)}, u32[]{:S(2)}, u32[]{:S(2)}) collective-permute-start(bf16[2,8,4,32,128]{4,3,2,1,0:T(8,128)(2,1)S(1)} %collective-permute-done.2.refs_0_), channel_id=1, source_target_pairs={{0,64},{1,65},{2,66},{3,67},{32,33},{33,34},{34,35},{35,32},{64,12... | collective-permute-start | bytes 1572872 | tf_op jit(solution)/shard_map/ppermute | solution.py:505
  84.2 5.9 %copy-start.2 = (f32[512]{0:T(512)S(1)}, f32[512]{0:T(512)}, u32[]{:S(2)}) copy-start(f32[512]{0:T(512)} %param.23) | copy-start | bytes 6148
  84.2 5.9 %copy-start.3 = (s32[512]{0:T(512)S(1)}, s32[512]{0:T(512)}, u32[]{:S(2)}) copy-start(s32[512]{0:T(512)} %param.25) | copy-start | bytes 6148
  90.1 18.5 %copy-start = (f32[512]{0:T(512)S(1)}, f32[512]{0:T(512)}, u32[]{:S(2)}) copy-start(f32[512]{0:T(512)} %param.24) | copy-start | bytes 6148
  110.2 18.1 %all-to-all-start.4 = ((f32[128,4,128]{2,1,0:T(4,128)}), f32[128,4,128]{2,1,0:T(4,128)S(1)}, u32[]{:S(2)}, u32[]{:S(2)}) async-start(f32[128,4,128]{2,1,0:T(4,128)} %bitcast.10), calls=%async_computation.4 | async-start | bytes 524288 | tf_op jit(solution)/shard_map/all_to_all | solution.py:524
  128.5 10.6 %collective-permute-start.11 = (f32[256]{0:T(256)S(1)}, f32[256]{0:T(256)S(1)}, u32[]{:S(2)}, u32[]{:S(2)}) collective-permute-start(f32[256]{0:T(256)S(1)} %negate_multiply_fusion), channel_id=1, source_target_pairs={{0,32},{32,0},{1,33},{33,1},{2,34},{34,2},{3,35},{35,3},{4,36},{36... | collective-permute-start | bytes 3080 | tf_op jit(solution)/shard_map/ppermute | solution.py:245
  139.3 0.6 copy-start.6

commit v3 on v2

--- a/solution.py
+++ b/solution.py
@@ -38,7 +38,7 @@
     return jnp.concatenate([held[pl.ds(start, 64), i : i + 1] for i in range(4)])
 
 
-LOWS, HIGHS = (0, -1), (1, 2)
+LOWS, HIGHS = (0, 1), (-1, 2)
 BLOCKS = [
     (far, side)
     for far, sides in (
@@ -164,7 +164,7 @@
             pltpu.SemaphoreType.DMA,
         ],
         compiler_params=pltpu.CompilerParams(vmem_limit_bytes=LIMIT),
-    )(counts, *[in_hbm(value) for value in (q, k, v, own_k, own_v, skip, mix)])
+    )(*[in_hbm(value) for value in (counts, q, k, v, own_k, own_v, skip, mix)])
 
 
 def project_body(got_ref, own_ref, peer_ref, gain_ref, out_ref):
@@ -250,20 +250,19 @@
     return [jnp.transpose(wide[h * 128 : (h + 1) * 128])[:1] for h in range(2)]
 
 
-def fetch(lexicons, at, count, target, sems):
+def fetch(lexicon, at, count, target, sems):
     copies = []
     for i in range(count):
         group = []
         for half in range(2):
             row = pl.multiple_of(number(*BLOCKS[at + i], half) * 256, 256)
-            for side, lex in enumerate(lexicons):
-                copy = pltpu.make_async_copy(
-                    lex.at[pl.ds(row, 256), :],
-                    target.at[side, pl.ds(i * 512 + half * 256, 256), :],
-                    sems.at[4 * i + 2 * half + side],
-                )
-                copy.start()
-                group.append(copy)
+            copy = pltpu.make_async_copy(
+                lexicon.at[pl.ds(row, 256), :],
+                target.at[pl.ds(i * 512 + half * 256, 256), :],
+                sems.at[2 * i + half],
+            )
+            copy.start()
+            group.append(copy)
         copies.append(group)
     return copies
 
@@ -274,7 +273,7 @@
     take = lambda n: [refs.pop(0) for _ in range(n)]
     total = sum(sides)
     sources = take(len(sides))
-    gain, *lexicons = take(3)
+    gain, lex_own, lex_peer = take(3)
     if not first:
         z_in, sq_in = take(2)
     if ready:
@@ -292,9 +291,9 @@
     copies = None
     if not ready:
         lexs, sems = take(2)
-        copies = fetch(lexicons, at, total, lexs, sems)
+        copies = fetch(lex_own, at, total, lexs, sems)
     if following:
-        next_copies = fetch(lexicons, at + total, following, lex_next, *take(1))
+        next_copies = fetch(lex_own, at + total, following, lex_next, *take(1))
     xs, held = take(2)
     x, c, t, y = place()
     mine = x * 4 + y
@@ -318,7 +317,17 @@
         span = slice(start * 512, (pair[-1] + 1) * 512)
         for side in range(2):
             cols = slice(side * 512, (side + 1) * 512)
-            part = jnp.dot(xs[:, span], lexs[side, span, :], preferred_element_type=F32)
+            if side == 0:
+                part = jnp.dot(xs[:, span], lexs[span, :], preferred_element_type=F32)
+            else:
+                part = 0.0
+                for i in pair:
+                    for half in range(2):
+                        row = pl.multiple_of(number(*BLOCKS[at + i], half) * 256, 256)
+                        x_cols = slice(i * 512 + half * 256, i * 512 + (half + 1) * 256)
+                        part += jnp.dot(
+                            xs[:, x_cols], lex_peer[pl.ds(row, 256), :], preferred_element_type=F32
+                        )
             if start:
                 z_out[:, cols] += part
             elif first:
@@ -358,8 +367,8 @@
     total = sum(sides)
     first, ready, last = state is None, lexs is not None, closing is not None
     vmem, anywhere = pl.BlockSpec(), pl.BlockSpec(memory_space=pl.ANY)
-    in_specs = [vmem] * (len(sources) + 1) + [anywhere] * 2
-    operands = [*sources, gain, in_hbm(lex_own), in_hbm(lex_peer)]
+    in_specs = [vmem] * (len(sources) + 1) + [anywhere, vmem]
+    operands = [*sources, gain, in_hbm(lex_own), in_vmem(lex_peer)]
     for extra in (state, lexs, closing):
         if extra is not None:
             operands += list(extra)
@@ -377,13 +386,13 @@
     else:
         out_shape += [jax.ShapeDtypeStruct((256, 128), F32)]
     if following:
-        out_shape += [pltpu.VMEM((2, 512 * following, 512), BF16)]
+        out_shape += [pltpu.VMEM((512 * following, 512), BF16)]
     if first:
         out_shape += [jax.ShapeDtypeStruct(source.shape, source.dtype) for source in sources]
     if not ready:
-        scratch += [pltpu.VMEM((2, 512 * total, 512), BF16), pltpu.SemaphoreType.DMA((4 * total,))]
+        scratch += [pltpu.VMEM((512 * total, 512), BF16), pltpu.SemaphoreType.DMA((2 * total,))]
     if following:
-        scratch += [pltpu.SemaphoreType.DMA((4 * following,))]
+        scratch += [pltpu.SemaphoreType.DMA((2 * following,))]
     scratch += [pltpu.VMEM((256, 512 * total), BF16), pltpu.VMEM((128, 128), F32)]
     return pl.pallas_call(
         functools.partial(head_body, (sides, at, ready, following, first, last)),
@@ -466,6 +475,56 @@
     )(z, lse, tok, level, *picks)
 
 
+def swap_halves(rows):
+    return jnp.concatenate([rows[:, 64:], rows[:, :64]], axis=1)
+
+
+def surprise_body(got_ref, norm_ref, level_ref, out_ref):
+    sums = jnp.sum(got_ref[...].reshape(64, 8, 128), axis=0)
+    sums = sums[:4] + sums[4:]
+    kept, token = sums[:2], sums[2:]
+    table = level_ref[...]
+    turned = swap_halves(table)
+    even = lax.axis_index("core") == 0
+    first, second = jnp.where(even, table, turned), jnp.where(even, turned, table)
+    low = lax.broadcasted_iota(jnp.int32, (1, 128), 1) < 64
+    level = jnp.concatenate(
+        [jnp.where(low, first[2 * h : 2 * h + 1], second[2 * h + 1 : 2 * h + 2]) for h in range(2)]
+    )
+    token_logp = token - norm_ref[...]
+    gate = cut_slope * (level + token_logp / LN2)
+    log_gate = jnp.minimum(gate, 0.0) - jnp.log1p(jnp.exp(-jnp.abs(gate)))
+    out_ref[...] = -(token_logp + log_gate - jnp.log(kept)) / LN2
+
+
+def surprise_call(got, norm, level):
+    return pl.pallas_call(
+        surprise_body,
+        out_shape=jax.ShapeDtypeStruct((2, 128), F32),
+        compiler_params=pltpu.CompilerParams(vmem_limit_bytes=LIMIT),
+    )(got, norm, level)
+
+
+def merge_body(own_ref, peer_ref, level_ref, surprise_out, next_out):
+    even = lax.axis_index("core") == 0
+    own, peer = own_ref[...], peer_ref[...]
+    evens, odds = jnp.where(even, own, peer), jnp.where(even, peer, own)
+    low = lax.broadcasted_iota(jnp.int32, (1, 128), 1) < 64
+    first = jnp.where(low, evens, swap_halves(odds))
+    second = jnp.where(low, swap_halves(evens), odds)
+    surprise = jnp.concatenate([first[:1], second[:1], first[1:], second[1:]])
+    surprise_out[...] = surprise
+    next_out[...] = level_ref[...] - 0.1 * (surprise - 5.0)
+
+
+def merge_call(own, peer, level):
+    return pl.pallas_call(
+        merge_body,
+        out_shape=[jax.ShapeDtypeStruct((4, 128), F32)] * 2,
+        compiler_params=pltpu.CompilerParams(vmem_limit_bytes=LIMIT),
+    )(own, peer, level)
+
+
 def shards(
     probe_vectors,
     stored_lookup_vectors,
@@ -482,7 +541,6 @@
     chosen_symbols,
 ):
     mix_peer = swap_core(mixing_matrix)
-    lex_peer = swap_core(lexicon_matrix)
 
     sent, mix_own = attend(
         probe_vectors,
@@ -494,6 +552,8 @@
         skip_stream,
         mixing_matrix,
     )
+    lexicon_matrix, mix_peer, sent = lax.optimization_barrier((lexicon_matrix, mix_peer, sent))
+    lex_peer = swap_core(lexicon_matrix)
     got = lax.all_to_all(sent, ("x", "rep"), 0, 0, tiled=True).reshape(256, 1280)
     gain_rows = closing_multiplier.reshape(8, 128)
     sent = project(got, mix_own, mix_peer, gain_rows)
@@ -503,8 +563,10 @@
     own = lax.all_to_all(sent, "tensor", 0, 0, tiled=True).reshape(8, 4, 32, 128)
     side = lambda v, s: lax.ppermute(v, PLANE, turn_other(s))
     far = lambda v, s: lax.ppermute(v, PLANE, turn(s))
-    low = pile(own, side(own, 1))
-    high = pile(side(own, -1), side(own, 2))
+    ahead, behind, across = side(own, 1), side(own, -1), side(own, 2)
+    low = pile(own, behind)
+    ahead, across, low = lax.optimization_barrier((ahead, across, low))
+    high = pile(ahead, across)
     left_low, right_high = far(low, 1), far(high, -1)
     past_low, past_high = far(left_low, 1), far(right_high, -1)
 
@@ -522,18 +584,9 @@
     levels = desired_perplexity.reshape(4, 128)
     sent, norm, hidden = mass_call(z, every_lse.reshape(256, 128), tok, levels, picked)
     got = lax.all_to_all(sent.reshape(128, 4, 128), SAME_CORE, 0, 0, tiled=True)
-    kept, tok = jnp.sum(got, axis=0).reshape(2, 256)
-    token_logp = tok - norm.reshape(256)
-    c = lax.axis_index("core")
-    level = lax.dynamic_index_in_dim(desired_perplexity.reshape(4, 2, 64), c, 1, keepdims=False)
-    level = level.reshape(256)
-    token_logw = token_logp + jax.nn.log_sigmoid(cut_slope * (level + token_logp / LN2))
-    mine_out = -(token_logw - jnp.log(kept)) / LN2
-    peer_out = swap_core(mine_out)
-    even = jnp.where(c == 0, mine_out, peer_out).reshape(4, 64)
-    odd = jnp.where(c == 0, peer_out, mine_out).reshape(4, 64)
-    surprise = jnp.stack([even, odd], axis=1).reshape(512)
-    next_targets = desired_perplexity - 0.1 * (surprise - 5.0)
+    mine = surprise_call(got.reshape(512, 128), norm, levels)
+    surprise, next_targets = merge_call(mine, swap_core(mine), levels)
+    surprise, next_targets = surprise.reshape(512), next_targets.reshape(512)
     return (hidden, next_targets, surprise)
 
 

time: 140 us -> 138 us (0.986)
  blocking collectives: 45.9 us -> 80.3 us
  waiting for transfers between devices: 37.1 us -> 15.3 us
  starting transfers between devices: 34 us -> 23.2 us
  Pallas kernels: 20.3 us -> 17.9 us
    all_to_all x0 -> x2, blocking collectives: none -> 34.1 us  [the longest x1 17.4 us: shards(): got = lax.all_to_all(sent.reshape(128, 4, 128), SAME_CORE, 0, 0, tiled=True)]
    all_to_all x2 -> x0, waiting for transfers between devices: 20.9 us -> none  [the longest x1 11.7 us: shards(): got = lax.all_to_all(sent.reshape(128, 4, 128), SAME_CORE, 0, 0, tiled=True)]
    all_to_all x2 -> x0, starting transfers between devices: 11.2 us -> none  [the longest x1 6.17 us: shards(): got = lax.all_to_all(sent.reshape(128, 4, 128), SAME_CORE, 0, 0, tiled=True)]
    ppermute x3, waiting for transfers between devices: 2.85 us -> 0.82 us  [swap_core(): return lax.ppermute(value, 'core', [(0, 1), (1, 0)])]
    pallas_call x4, Pallas kernels: 12.7 us -> 10.8 us  [head_call(): pl.pallas_call(functools.partial(head_body, (sides, at, ready, following,...]
  transfers between devices with their start and end apart: 14 -> 12, of which waited for: 11 -> 9; matrix products, arithmetic and copies ran while one was open for 0% -> 0% of each run, Pallas kernels for 12% -> 10%
where the time goes in v3:
time: 138 us; the launch traced here: 137 us
  blocking collectives  80.3 us (58%)
  starting transfers between devices  23.2 us (17%)
  Pallas kernels  17.9 us (13%)
  waiting for transfers between devices  15.3 us (11%)
    all_to_all x1, blocking collectives, shards(): got = lax.all_to_all(sent.reshape(128, 4, 128), SAME_CORE, 0, 0, tiled=True)  17.4 us
    all_to_all x1, blocking collectives, shards(): got = lax.all_to_all(sent, 'tensor', 0, 0, tiled=True)  17.2 us
    all_to_all x1, blocking collectives, shards(): lax.all_to_all(sent, ('x', 'rep'), 0, 0, tiled=True).reshape(256, 1280)  16.7 us
    all_to_all x1, blocking collectives, shards(): lax.all_to_all(lse.reshape(128, 2, 128), SAME_CORE, 0, 0, tiled=True)  16.6 us
    ppermute x3, starting transfers between devices, swap_core(): return lax.ppermute(value, 'core', [(0, 1), (1, 0)])  14.1 us
    all_to_all x1, blocking collectives, shards(): lax.all_to_all(sent, 'tensor', 0, 0, tiled=True).reshape(8, 4, 32, 128)  12.4 us
    pallas_call x4, Pallas kernels, head_call(): pl.pallas_call(functools.partial(head_body, (sides, at, ready, following,...  10.8 us
    ppermute x3, waiting for transfers between devices, shards(): side = lambda v, s: lax.ppermute(v, PLANE, turn_other(s))  7.94 us
  transfers between devices with their start and end apart: 12, of which 9 were waited for; matrix products, arithmetic and copies ran while one was open for 0% of the time, Pallas kernels for 10%

profile of v3, /device:TPU:1, one launch (start us, length us, event | category | flops | bytes accessed | tf_op | source)
XLA Modules:
  0.0 137.4 jit_solution(2105538393269008710)
XLA Ops:
  0.6 3.3 %collective-permute-start = (bf16[1024,256]{1,0:T(8,128)(2,1)}, bf16[1024,256]{1,0:T(8,128)(2,1)S(1)}, u32[]{:S(2)}, u32[]{:S(2)}) collective-permute-start(bf16[1024,256]{1,0:T(8,128)(2,1)} %mix.1), channel_id=1, source_target_pairs={{0,32},{32,0},{1,33},{33,1},{2,34},{34,2},{3,35},{35,3},{4,36},{36... | collective-permute-start | bytes 1572872 | tf_op jit(solution)/shard_map/ppermute | solution.py:245
  4.0 0.0 copy-start.1
  4.0 4.4 %shard_map.148 = (bf16[16,16,1280]{2,1,0:T(8,128)(2,1)S(1)}, bf16[1024,256]{1,0:T(8,128)(2,1)S(1)}) custom-call(s32[16]{0:T(128)} %counts.1, bf16[16,8,128]{2,1,0:T(8,128)(2,1)} %q_ref.1, bf16[16,1,512,128]{3,2,1,0:T(8,128)(2,1)} %k_hbm.1, bf16[16,1,512,128]{3,2,1,0:T(8,128)(2,1)} %v_hbm.1, bf16[16,128]{1,0:T(8,128)(2,1)} %bitcast.29, ...), custom_call_target="tpu_custom_call" | custom-call | tf_op jit(solution)/shard_map/pallas_call | solution.py:141
  8.4 0.0 collective-permute-done.peer_ref
  8.4 0.1 collective-permute-start.8
  8.5 16.7 %all_to_all.25 = bf16[16,16,1280]{2,1,0:T(8,128)(2,1)S(1)} all-to-all(bf16[16,16,1280]{2,1,0:T(8,128)(2,1)S(1)} %get-tuple-element.35), channel_id=1, replica_groups=mesh['x'=4,'core'=2,'tensor'=8,'rep'=4] {'x','rep'}, dimensions={0} | all-to-all | bytes 1310720 | tf_op jit(solution)/shard_map/all_to_all | solution.py:557
  25.2 0.0 copy-done.1
  25.2 0.4 shard_map.149
  25.6 17.2 %all_to_all.26.got_ref = bf16[8,136,128]{2,1,0:T(8,128)(2,1)S(1)} all-to-all(bf16[8,136,128]{2,1,0:T(8,128)(2,1)S(1)} %shard_map.149), channel_id=1, replica_groups=mesh['x'=4,'core'=2,'tensor'=8,'rep'=4] {'tensor'}, dimensions={0} | all-to-all | bytes 557056 | tf_op jit(solution)/shard_map/all_to_all | solution.py:560
  42.9 12.4 %all_to_all.27 = bf16[8,128,128]{2,1,0:T(8,128)(2,1)S(1)} all-to-all(bf16[8,128,128]{2,1,0:T(8,128)(2,1)S(1)} %get-tuple-element.38), channel_id=1, replica_groups=mesh['x'=4,'core'=2,'tensor'=8,'rep'=4] {'tensor'}, dimensions={0} | all-to-all | bytes 524288 | tf_op jit(solution)/shard_map/all_to_all | solution.py:563
  55.2 1.0 collective-permute-start.3
  56.3 1.0 collective-permute-start.2
  57.3 0.9 collective-permute-start.1
  58.1 2.4 %collective-permute-done.3.second_ref = bf16[8,4,32,128]{3,2,1,0:T(8,128)(2,1)S(1)} collective-permute-done((bf16[8,4,32,128]{3,2,1,0:T(8,128)(2,1)S(1)}, bf16[8,4,32,128]{3,2,1,0:T(8,128)(2,1)S(1)}, u32[]{:S(2)}, u32[]{:S(2)}) %collective-permute-start.3) | collective-permute-done | bytes 262176 | tf_op jit(solution)/shard_map/ppermute | solution.py:564
  60.5 2.6 %collective-permute-done.2.second_ref = bf16[8,4,32,128]{3,2,1,0:T(8,128)(2,1)S(1)} collective-permute-done((bf16[8,4,32,128]{3,2,1,0:T(8,128)(2,1)S(1)}, bf16[8,4,32,128]{3,2,1,0:T(8,128)(2,1)S(1)}, u32[]{:S(2)}, u32[]{:S(2)}) %collective-permute-start.2) | collective-permute-done | bytes 262176 | tf_op jit(solution)/shard_map/ppermute | solution.py:564
  63.1 3.0 %collective-permute-done.1.first_ref = bf16[8,4,32,128]{3,2,1,0:T(8,128)(2,1)S(1)} collective-permute-done((bf16[8,4,32,128]{3,2,1,0:T(8,128)(2,1)S(1)}, bf16[8,4,32,128]{3,2,1,0:T(8,128)(2,1)S(1)}, u32[]{:S(2)}, u32[]{:S(2)}) %collective-permute-start.1) | collective-permute-done | bytes 262176 | tf_op jit(solution)/shard_map/ppermute | solution.py:564
  66.1 0.8 collective-permute-start.6
  66.9 0.7 collective-permute-start.4
  67.7 0.0 collective-permute-done.8.refs_4_
  67.7 2.8 %shard_map.153 = (f32[256,1024]{1,0:T(8,128)S(1)}, bf16[4,4,16,128]{3,2,1,0:T(8,128)(2,1)S(1)}, f32[256,128]{1,0:T(8,128)S(1)}, bf16[2,8,4,32,128]{4,3,2,1,0:T(8,128)(2,1)S(1)}, bf16[2,8,4,32,128]{4,3,2,1,0:T(8,128)(2,1)S(1)}) custom-call(bf16[2,8,4,32,128]{4,3,2,1,0:T(8,128)(2,1)S(1)} %shard_map.151.refs_0_, ...), custom_call_target="tpu_custom_call" | custom-call | flops 1073741824 | bytes 7340032 | tf_op jit(solution)/shard_map/pallas_call | solution.py:397
  70.5 0.8 collective-permute-start.9
  71.3 2.0 %collective-permute-start.10 = (bf16[2,8,4,32,128]{4,3,2,1,0:T(8,128)(2,1)S(1)}, bf16[2,8,4,32,128]{4,3,2,1,0:T(8,128)(2,1)S(1)}, u32[]{:S(2)}, u32[]{:S(2)}) collective-permute-start(bf16[2,8,4,32,128]{4,3,2,1,0:T(8,128)(2,1)S(1)} %get-tuple-element.45), channel_id=1, source_target_pairs={{0,192},{1,193},{2,194},{3,195},{32,35},{33,32},{34,33},{35,34},{6... | collective-permute-start | bytes 1572872 | tf_op jit(solution)/shard_map/ppermute | solution.py:565
  73.2 1.0 collective-permute-done.6.refs_1_
  74.2 2.0 %collective-permute-start.7 = (bf16[2,8,4,32,128]{4,3,2,1,0:T(8,128)(2,1)S(1)}, bf16[2,8,4,32,128]{4,3,2,1,0:T(8,128)(2,1)S(1)}, u32[]{:S(2)}, u32[]{:S(2)}) collective-permute-start(bf16[2,8,4,32,128]{4,3,2,1,0:T(8,128)(2,1)S(1)} %collective-permute-done.6.refs_1_), channel_id=1, source_target_pairs={{0,192},{1,193},{2,194},{3,195},{32,35},{33,32},{34,33},{35,34},{6... | collective-permute-start | bytes 1572872 | tf_op jit(solution)/shard_map/ppermute | solution.py:565
  76.2 0.1 collective-permute-done.4.refs_0_
  76.4 0.0 collective-permute-start.5
  76.4 2.9 %shard_map.154 = (f32[256,1024]{1,0:T(8,128)S(1)}, bf16[4,4,16,128]{3,2,1,0:T(8,128)(2,1)S(1)}, f32[256,128]{1,0:T(8,128)S(1)}) custom-call(bf16[2,8,4,32,128]{4,3,2,1,0:T(8,128)(2,1)S(1)} %collective-permute-done.4.refs_0_, bf16[2,8,4,32,128]{4,3,2,1,0:T(8,128)(2,1)S(1)} %collective-permute-done.6.refs_1_, f32[64,128]{1,0:T(8,128)S(1)} %get-tuple-element.42.refs_2_, ...), custom_call_target="tpu_custom_call" | custom-call | flops 1073741824 | bytes 7340032 | tf_op jit(solution)/shard_map/pallas_call | solution.py:397
  79.3 3.0 %collective-permute-done.9.refs_0_ = bf16[2,8,4,32,128]{4,3,2,1,0:T(8,128)(2,1)S(1)} collective-permute-done((bf16[2,8,4,32,128]{4,3,2,1,0:T(8,128)(2,1)S(1)}, bf16[2,8,4,32,128]{4,3,2,1,0:T(8,128)(2,1)S(1)}, u32[]{:S(2)}, u32[]{:S(2)}) %collective-permute-start.9) | collective-permute-done | bytes 524320 | tf_op jit(solution)/shard_map/ppermute | solution.py:565
  82.3 0.0 collective-permute-done.10.refs_1_
  82.3 0.0 copy-start.2
  82.3 0.0 copy-start.3
  82.3 3.3 %shard_map.155 = (f32[256,1024]{1,0:T(8,128)S(1)}, bf16[4,4,16,128]{3,2,1,0:T(8,128)(2,1)S(1)}, f32[256,128]{1,0:T(8,128)S(1)}, bf16[2048,512]{1,0:T(8,128)(2,1)S(1)}) custom-call(bf16[2,8,4,32,128]{4,3,2,1,0:T(8,128)(2,1)S(1)} %collective-permute-done.9.refs_0_, bf16[2,8,4,32,128]{4,3,2,1,0:T(8,128)(2,1)S(1)} %collective-permute-done.10.refs_1_, ...), custom_call_target="tpu_custom_call" | custom-call | flops 1073741824 | bytes 7340032 | tf_op jit(solution)/shard_map/pallas_call | solution.py:397
  85.6 0.2 collective-permute-done.7.refs_1_
  85.8 2.1 %collective-permute-done.5.refs_0_ = bf16[2,8,4,32,128]{4,3,2,1,0:T(8,128)(2,1)S(1)} collective-permute-done((bf16[2,8,4,32,128]{4,3,2,1,0:T(8,128)(2,1)S(1)}, bf16[2,8,4,32,128]{4,3,2,1,0:T(8,128)(2,1)S(1)}, u32[]{:S(2)}, u32[]{:S(2)}) %collective-permute-start.5) | collective-permute-done | bytes 524320 | tf_op jit(solution)/shard_map/ppermute | solution.py:565
  87.9 0.0 copy-done.2
  87.9 0.0 copy-done.3
  87.9 0.0 copy-start
  87.9 1.9 %shard_map.156 = (f32[256,1024]{1,0:T(8,128)S(1)}, bf16[4,4,16,128]{3,2,1,0:T(8,128)(2,1)S(1)}, f32[256,128]{1,0:T(8,128)S(1)}, f32[2,128]{1,0:T(2,128)S(1)}) custom-call(bf16[2,8,4,32,128]{4,3,2,1,0:T(8,128)(2,1)S(1)} %collective-permute-done.5.refs_0_, bf16[2,8,4,32,128]{4,3,2,1,0:T(8,128)(2,1)S(1)} %collective-permute-done.7.refs_1_, ...), custom_call_target="tpu_custom_call" | custom-call | flops 1073741824 | bytes 7340032 | tf_op jit(solution)/shard_map/pallas_call | solution.py:397
  89.8 16.6 %all_to_all.28 = f32[128,2,128]{2,1,0:T(2,128)S(1)} all-to-all(f32[128,2,128]{2,1,0:T(2,128)S(1)} %bitcast.22), channel_id=1, replica_groups=mesh['x'=4,'core'=2,'tensor'=8,'rep'=4] {'x','tensor','rep'}, dimensions={0} | all-to-all | bytes 262144 | tf_op jit(solution)/shard_map/all_to_all | solution.py:583
  106.4 0.0 copy-done
  106.4 1.3 shard_map.157
  107.8 17.4 %all_to_all.29 = f32[128,4,128]{2,1,0:T(4,128)S(1)} all-to-all(f32[128,4,128]{2,1,0:T(4,128)S(1)} %bitcast.21), channel_id=1, replica_groups=mesh['x'=4,'core'=2,'tensor'=8,'rep'=4] {'x','tensor','rep'}, dimensions={0} | all-to-all | bytes 524288 | tf_op jit(solution)/shard_map/all_to_all | solution.py:586
  125.2 0.1 shard_map.158.own_ref
  125.3 10.6 %collective-permute-start.11 = (f32[2,128]{1,0:T(2,128)S(1)}, f32[2,128]{1,0:T(2,128)S(1)}, u32[]{:S(2)}, u32[]{:S(2)}) collective-permute-start(f32[2,128]{1,0:T(2,128)S(1)} %shard_map.158.own_ref), channel_id=1, source_target_pairs={{0,32},{32,0},{1,33},{33,1},{2,34},{34,2},{3,35},{35,3},{4,36},{36... | collective-permute-start | bytes 3080 | tf_op jit(solution)/shard_map/ppermute | solution.py:245
  135.9 0.8 collective-permute-done.11.peer_ref
  136.7 0.7 shard_map.159
  (3 shorter events, 0.1 us)
Async XLA Ops:
  0.6 7.8 %collective-permute-start = (bf16[1024,256]{1,0:T(8,128)(2,1)}, bf16[1024,256]{1,0:T(8,128)(2,1)S(1)}, u32[]{:S(2)}, u32[]{:S(2)}) collective-permute-start(bf16[1024,256]{1,0:T(8,128)(2,1)} %mix.1), channel_id=1, source_target_pairs={{0,32},{32,0},{1,33},{33,1},{2,34},{34,2},{3,35},{35,3},{4,36},{36... | collective-permute-start | bytes 1572872 | tf_op jit(solution)/shard_map/ppermute | solution.py:245
  4.0 21.2 %copy-start.1 = (bf16[1024]{0:T(1024)(128)(2,1)S(1)}, bf16[1024]{0:T(1024)(128)(2,1)}, u32[]{:S(2)}) copy-start(bf16[1024]{0:T(1024)(128)(2,1)} %param.21) | copy-start | bytes 6148
  8.4 59.3 %collective-permute-start.8 = (bf16[8192,512]{1,0:T(8,128)(2,1)}, bf16[8192,512]{1,0:T(8,128)(2,1)S(1)}, u32[]{:S(2)}, u32[]{:S(2)}) collective-permute-start(bf16[8192,512]{1,0:T(8,128)(2,1)} %refs_3_.3), channel_id=1, source_target_pairs={{0,32},{32,0},{1,33},{33,1},{2,34},{34,2},{3,35},{35,3},{4,36},{36... | collective-permute-start | bytes 25165832 | tf_op jit(solution)/shard_map/ppermute | solution.py:245
  55.2 5.2 %collective-permute-start.3 = (bf16[8,4,32,128]{3,2,1,0:T(8,128)(2,1)S(1)}, bf16[8,4,32,128]{3,2,1,0:T(8,128)(2,1)S(1)}, u32[]{:S(2)}, u32[]{:S(2)}) collective-permute-start(bf16[8,4,32,128]{3,2,1,0:T(8,128)(2,1)S(1)} %bitcast.16), channel_id=1, source_target_pairs={{0,3},{1,0},{2,1},{3,2},{32,224},{33,225},{34,226},{35,227},{64,67... | collective-permute-start | bytes 786440 | tf_op jit(solution)/shard_map/ppermute | solution.py:564
  56.3 6.8 %collective-permute-start.2 = (bf16[8,4,32,128]{3,2,1,0:T(8,128)(2,1)S(1)}, bf16[8,4,32,128]{3,2,1,0:T(8,128)(2,1)S(1)}, u32[]{:S(2)}, u32[]{:S(2)}) collective-permute-start(bf16[8,4,32,128]{3,2,1,0:T(8,128)(2,1)S(1)} %bitcast.17), channel_id=1, source_target_pairs={{0,2},{1,3},{2,0},{3,1},{32,160},{33,161},{34,162},{35,163},{64,66... | collective-permute-start | bytes 786440 | tf_op jit(solution)/shard_map/ppermute | solution.py:564
  57.3 8.8 %collective-permute-start.1 = (bf16[8,4,32,128]{3,2,1,0:T(8,128)(2,1)S(1)}, bf16[8,4,32,128]{3,2,1,0:T(8,128)(2,1)S(1)}, u32[]{:S(2)}, u32[]{:S(2)}) collective-permute-start(bf16[8,4,32,128]{3,2,1,0:T(8,128)(2,1)S(1)} %bitcast.18), channel_id=1, source_target_pairs={{0,1},{1,2},{2,3},{3,0},{32,96},{33,97},{34,98},{35,99},{64,65},{6... | collective-permute-start | bytes 786440 | tf_op jit(solution)/shard_map/ppermute | solution.py:564
  66.1 8.1 %collective-permute-start.6 = (bf16[2,8,4,32,128]{4,3,2,1,0:T(8,128)(2,1)S(1)}, bf16[2,8,4,32,128]{4,3,2,1,0:T(8,128)(2,1)S(1)}, u32[]{:S(2)}, u32[]{:S(2)}) collective-permute-start(bf16[2,8,4,32,128]{4,3,2,1,0:T(8,128)(2,1)S(1)} %shard_map.152.refs_1_), channel_id=1, source_target_pairs={{0,192},{1,193},{2,194},{3,195},{32,35},{33,32},{34,33},{35,34},{6... | collective-permute-start | bytes 1572872 | tf_op jit(solution)/shard_map/ppermute | solution.py:565
  66.9 9.5 %collective-permute-start.4 = (bf16[2,8,4,32,128]{4,3,2,1,0:T(8,128)(2,1)S(1)}, bf16[2,8,4,32,128]{4,3,2,1,0:T(8,128)(2,1)S(1)}, u32[]{:S(2)}, u32[]{:S(2)}) collective-permute-start(bf16[2,8,4,32,128]{4,3,2,1,0:T(8,128)(2,1)S(1)} %shard_map.151.refs_0_), channel_id=1, source_target_pairs={{0,64},{1,65},{2,66},{3,67},{32,33},{33,34},{34,35},{35,32},{64,12... | collective-permute-start | bytes 1572872 | tf_op jit(solution)/shard_map/ppermute | solution.py:565
  70.5 11.8 %collective-permute-start.9 = (bf16[2,8,4,32,128]{4,3,2,1,0:T(8,128)(2,1)S(1)}, bf16[2,8,4,32,128]{4,3,2,1,0:T(8,128)(2,1)S(1)}, u32[]{:S(2)}, u32[]{:S(2)}) collective-permute-start(bf16[2,8,4,32,128]{4,3,2,1,0:T(8,128)(2,1)S(1)} %get-tuple-element.44), channel_id=1, source_target_pairs={{0,64},{1,65},{2,66},{3,67},{32,33},{33,34},{34,35},{35,32},{64,12... | collective-permute-start | bytes 1572872 | tf_op jit(solution)/shard_map/ppermute | solution.py:565
  71.3 11.1 %collective-permute-start.10 = (bf16[2,8,4,32,128]{4,3,2,1,0:T(8,128)(2,1)S(1)}, bf16[2,8,4,32,128]{4,3,2,1,0:T(8,128)(2,1)S(1)}, u32[]{:S(2)}, u32[]{:S(2)}) collective-permute-start(bf16[2,8,4,32,128]{4,3,2,1,0:T(8,128)(2,1)S(1)} %get-tuple-element.45), channel_id=1, source_target_pairs={{0,192},{1,193},{2,194},{3,195},{32,35},{33,32},{34,33},{35,34},{6... | collective-permute-start | bytes 1572872 | tf_op jit(solution)/shard_map/ppermute | solution.py:565
  74.2 11.5 %collective-permute-start.7 = (bf16[2,8,4,32,128]{4,3,2,1,0:T(8,128)(2,1)S(1)}, bf16[2,8,4,32,128]{4,3,2,1,0:T(8,128)(2,1)S(1)}, u32[]{:S(2)}, u32[]{:S(2)}) collective-permute-start(bf16[2,8,4,32,128]{4,3,2,1,0:T(8,128)(2,1)S(1)} %collective-permute-done.6.refs_1_), channel_id=1, source_target_pairs={{0,192},{1,193},{2,194},{3,195},{32,35},{33,32},{34,33},{35,34},{6... | collective-permute-start | bytes 1572872 | tf_op jit(solution)/shard_map/ppermute | solution.py:565
  76.4 11.5 %collective-permute-start.5 = (bf16[2,8,4,32,128]{4,3,2,1,0:T(8,128)(2,1)S(1)}, bf16[2,8,4,32,128]{4,3,2,1,0:T(8,128)(2,1)S(1)}, u32[]{:S(2)}, u32[]{:S(2)}) collective-permute-start(bf16[2,8,4,32,128]{4,3,2,1,0:T(8,128)(2,1)S(1)} %collective-permute-done.4.refs_0_), channel_id=1, source_target_pairs={{0,64},{1,65},{2,66},{3,67},{32,33},{33,34},{34,35},{35,32},{64,12... | collective-permute-start | bytes 1572872 | tf_op jit(solution)/shard_map/ppermute | solution.py:565
  82.3 5.6 %copy-start.2 = (f32[512]{0:T(512)S(1)}, f32[512]{0:T(512)}, u32[]{:S(2)}) copy-start(f32[512]{0:T(512)} %param.23) | copy-start | bytes 6148
  82.3 5.6 %copy-start.3 = (s32[512]{0:T(512)S(1)}, s32[512]{0:T(512)}, u32[]{:S(2)}) copy-start(s32[512]{0:T(512)} %param.25) | copy-start | bytes 6148
  87.9 18.5 %copy-start = (f32[512]{0:T(512)S(1)}, f32[512]{0:T(512)}, u32[]{:S(2)}) copy-start(f32[512]{0:T(512)} %param.24) | copy-start | bytes 6148
  125.3 11.5 %collective-permute-start.11 = (f32[2,128]{1,0:T(2,128)S(1)}, f32[2,128]{1,0:T(2,128)S(1)}, u32[]{:S(2)}, u32[]{:S(2)}) collective-permute-start(f32[2,128]{1,0:T(2,128)S(1)} %shard_map.158.own_ref), channel_id=1, source_target_pairs={{0,32},{32,0},{1,33},{33,1},{2,34},{34,2},{3,35},{35,3},{4,36},{36... | collective-permute-start | bytes 3080 | tf_op jit(solution)/shard_map/ppermute | solution.py:245

commit v4 on v3

--- a/solution.py
+++ b/solution.py
@@ -67,7 +67,7 @@
     counts, q_ref, k_hbm, v_hbm, own_k_ref, own_v_ref, skip_ref, mix, out_ref, mix_out, *scratch
 ):
     k_ref, v_ref, own_k, own_v, held, sems, mix_sem = scratch
-    rows = 4
+    rows = 8
     groups = k_ref.shape[0] // rows
     score_scale = 1.0 / math.sqrt(k_ref.shape[3])
     copies = []

time: 138 us -> 137 us (level)
  no operation moved by 1% of the time
where the time goes in v4:
time: 137 us
  blocking collectives  80.3 us (59%)
  starting transfers between devices  23.2 us (17%)
  Pallas kernels  17.3 us (13%)
  waiting for transfers between devices  15.3 us (11%)
    all_to_all x1, blocking collectives, shards(): got = lax.all_to_all(sent.reshape(128, 4, 128), SAME_CORE, 0, 0, tiled=True)  17.4 us
    all_to_all x1, blocking collectives, shards(): got = lax.all_to_all(sent, 'tensor', 0, 0, tiled=True)  17.2 us
    all_to_all x1, blocking collectives, shards(): lax.all_to_all(sent, ('x', 'rep'), 0, 0, tiled=True).reshape(256, 1280)  16.7 us
    all_to_all x1, blocking collectives, shards(): lax.all_to_all(lse.reshape(128, 2, 128), SAME_CORE, 0, 0, tiled=True)  16.6 us
    ppermute x3, starting transfers between devices, swap_core(): return lax.ppermute(value, 'core', [(0, 1), (1, 0)])  14.1 us
    all_to_all x1, blocking collectives, shards(): lax.all_to_all(sent, 'tensor', 0, 0, tiled=True).reshape(8, 4, 32, 128)  12.4 us
    pallas_call x4, Pallas kernels, head_call(): pl.pallas_call(functools.partial(head_body, (sides, at, ready, following,...  10.8 us
    ppermute x3, waiting for transfers between devices, shards(): side = lambda v, s: lax.ppermute(v, PLANE, turn_other(s))  7.94 us
  transfers between devices with their start and end apart: 12, of which 9 were waited for; matrix products, arithmetic and copies ran while one was open for 0% of the time, Pallas kernels for 10%

profile of v4, /device:TPU:1, one launch (start us, length us, event | category | flops | bytes accessed | tf_op | source)
XLA Modules:
  0.0 136.8 jit_solution(17678585932422870485)
XLA Ops:
  0.6 3.3 %collective-permute-start = (bf16[1024,256]{1,0:T(8,128)(2,1)}, bf16[1024,256]{1,0:T(8,128)(2,1)S(1)}, u32[]{:S(2)}, u32[]{:S(2)}) collective-permute-start(bf16[1024,256]{1,0:T(8,128)(2,1)} %mix.1), channel_id=1, source_target_pairs={{0,32},{32,0},{1,33},{33,1},{2,34},{34,2},{3,35},{35,3},{4,36},{36... | collective-permute-start | bytes 1572872 | tf_op jit(solution)/shard_map/ppermute | solution.py:245
  4.0 0.0 copy-start.1
  4.0 3.8 %shard_map.148 = (bf16[16,16,1280]{2,1,0:T(8,128)(2,1)S(1)}, bf16[1024,256]{1,0:T(8,128)(2,1)S(1)}) custom-call(s32[16]{0:T(128)} %counts.1, bf16[16,8,128]{2,1,0:T(8,128)(2,1)} %q_ref.1, bf16[16,1,512,128]{3,2,1,0:T(8,128)(2,1)} %k_hbm.1, bf16[16,1,512,128]{3,2,1,0:T(8,128)(2,1)} %v_hbm.1, bf16[16,128]{1,0:T(8,128)(2,1)} %bitcast.29, ...), custom_call_target="tpu_custom_call" | custom-call | tf_op jit(solution)/shard_map/pallas_call | solution.py:141
  7.8 0.0 collective-permute-done.peer_ref
  7.8 0.1 collective-permute-start.8
  7.9 16.7 %all_to_all.25 = bf16[16,16,1280]{2,1,0:T(8,128)(2,1)S(1)} all-to-all(bf16[16,16,1280]{2,1,0:T(8,128)(2,1)S(1)} %get-tuple-element.35), channel_id=1, replica_groups=mesh['x'=4,'core'=2,'tensor'=8,'rep'=4] {'x','rep'}, dimensions={0} | all-to-all | bytes 1310720 | tf_op jit(solution)/shard_map/all_to_all | solution.py:557
  24.6 0.0 copy-done.1
  24.6 0.4 shard_map.149
  25.0 17.2 %all_to_all.26.got_ref = bf16[8,136,128]{2,1,0:T(8,128)(2,1)S(1)} all-to-all(bf16[8,136,128]{2,1,0:T(8,128)(2,1)S(1)} %shard_map.149), channel_id=1, replica_groups=mesh['x'=4,'core'=2,'tensor'=8,'rep'=4] {'tensor'}, dimensions={0} | all-to-all | bytes 557056 | tf_op jit(solution)/shard_map/all_to_all | solution.py:560
  42.3 12.4 %all_to_all.27 = bf16[8,128,128]{2,1,0:T(8,128)(2,1)S(1)} all-to-all(bf16[8,128,128]{2,1,0:T(8,128)(2,1)S(1)} %get-tuple-element.38), channel_id=1, replica_groups=mesh['x'=4,'core'=2,'tensor'=8,'rep'=4] {'tensor'}, dimensions={0} | all-to-all | bytes 524288 | tf_op jit(solution)/shard_map/all_to_all | solution.py:563
  54.6 1.0 collective-permute-start.3
  55.7 1.0 collective-permute-start.2
  56.6 0.9 collective-permute-start.1
  57.5 2.4 %collective-permute-done.3.second_ref = bf16[8,4,32,128]{3,2,1,0:T(8,128)(2,1)S(1)} collective-permute-done((bf16[8,4,32,128]{3,2,1,0:T(8,128)(2,1)S(1)}, bf16[8,4,32,128]{3,2,1,0:T(8,128)(2,1)S(1)}, u32[]{:S(2)}, u32[]{:S(2)}) %collective-permute-start.3) | collective-permute-done | bytes 262176 | tf_op jit(solution)/shard_map/ppermute | solution.py:564
  59.9 2.6 %collective-permute-done.2.second_ref = bf16[8,4,32,128]{3,2,1,0:T(8,128)(2,1)S(1)} collective-permute-done((bf16[8,4,32,128]{3,2,1,0:T(8,128)(2,1)S(1)}, bf16[8,4,32,128]{3,2,1,0:T(8,128)(2,1)S(1)}, u32[]{:S(2)}, u32[]{:S(2)}) %collective-permute-start.2) | collective-permute-done | bytes 262176 | tf_op jit(solution)/shard_map/ppermute | solution.py:564
  62.5 3.0 %collective-permute-done.1.first_ref = bf16[8,4,32,128]{3,2,1,0:T(8,128)(2,1)S(1)} collective-permute-done((bf16[8,4,32,128]{3,2,1,0:T(8,128)(2,1)S(1)}, bf16[8,4,32,128]{3,2,1,0:T(8,128)(2,1)S(1)}, u32[]{:S(2)}, u32[]{:S(2)}) %collective-permute-start.1) | collective-permute-done | bytes 262176 | tf_op jit(solution)/shard_map/ppermute | solution.py:564
  65.5 0.8 collective-permute-start.6
  66.3 0.7 collective-permute-start.4
  67.1 0.0 collective-permute-done.8.refs_4_
  67.1 2.8 %shard_map.153 = (f32[256,1024]{1,0:T(8,128)S(1)}, bf16[4,4,16,128]{3,2,1,0:T(8,128)(2,1)S(1)}, f32[256,128]{1,0:T(8,128)S(1)}, bf16[2,8,4,32,128]{4,3,2,1,0:T(8,128)(2,1)S(1)}, bf16[2,8,4,32,128]{4,3,2,1,0:T(8,128)(2,1)S(1)}) custom-call(bf16[2,8,4,32,128]{4,3,2,1,0:T(8,128)(2,1)S(1)} %shard_map.151.refs_0_, ...), custom_call_target="tpu_custom_call" | custom-call | flops 1073741824 | bytes 7340032 | tf_op jit(solution)/shard_map/pallas_call | solution.py:397
  69.9 0.8 collective-permute-start.9
  70.6 2.0 %collective-permute-start.10 = (bf16[2,8,4,32,128]{4,3,2,1,0:T(8,128)(2,1)S(1)}, bf16[2,8,4,32,128]{4,3,2,1,0:T(8,128)(2,1)S(1)}, u32[]{:S(2)}, u32[]{:S(2)}) collective-permute-start(bf16[2,8,4,32,128]{4,3,2,1,0:T(8,128)(2,1)S(1)} %get-tuple-element.45), channel_id=1, source_target_pairs={{0,192},{1,193},{2,194},{3,195},{32,35},{33,32},{34,33},{35,34},{6... | collective-permute-start | bytes 1572872 | tf_op jit(solution)/shard_map/ppermute | solution.py:565
  72.6 1.0 collective-permute-done.6.refs_1_
  73.6 2.0 %collective-permute-start.7 = (bf16[2,8,4,32,128]{4,3,2,1,0:T(8,128)(2,1)S(1)}, bf16[2,8,4,32,128]{4,3,2,1,0:T(8,128)(2,1)S(1)}, u32[]{:S(2)}, u32[]{:S(2)}) collective-permute-start(bf16[2,8,4,32,128]{4,3,2,1,0:T(8,128)(2,1)S(1)} %collective-permute-done.6.refs_1_), channel_id=1, source_target_pairs={{0,192},{1,193},{2,194},{3,195},{32,35},{33,32},{34,33},{35,34},{6... | collective-permute-start | bytes 1572872 | tf_op jit(solution)/shard_map/ppermute | solution.py:565
  75.6 0.1 collective-permute-done.4.refs_0_
  75.8 0.0 collective-permute-start.5
  75.8 2.9 %shard_map.154 = (f32[256,1024]{1,0:T(8,128)S(1)}, bf16[4,4,16,128]{3,2,1,0:T(8,128)(2,1)S(1)}, f32[256,128]{1,0:T(8,128)S(1)}) custom-call(bf16[2,8,4,32,128]{4,3,2,1,0:T(8,128)(2,1)S(1)} %collective-permute-done.4.refs_0_, bf16[2,8,4,32,128]{4,3,2,1,0:T(8,128)(2,1)S(1)} %collective-permute-done.6.refs_1_, f32[64,128]{1,0:T(8,128)S(1)} %get-tuple-element.42.refs_2_, ...), custom_call_target="tpu_custom_call" | custom-call | flops 1073741824 | bytes 7340032 | tf_op jit(solution)/shard_map/pallas_call | solution.py:397
  78.7 3.0 %collective-permute-done.9.refs_0_ = bf16[2,8,4,32,128]{4,3,2,1,0:T(8,128)(2,1)S(1)} collective-permute-done((bf16[2,8,4,32,128]{4,3,2,1,0:T(8,128)(2,1)S(1)}, bf16[2,8,4,32,128]{4,3,2,1,0:T(8,128)(2,1)S(1)}, u32[]{:S(2)}, u32[]{:S(2)}) %collective-permute-start.9) | collective-permute-done | bytes 524320 | tf_op jit(solution)/shard_map/ppermute | solution.py:565
  81.7 0.0 collective-permute-done.10.refs_1_
  81.7 0.0 copy-start.2
  81.7 0.0 copy-start.3
  81.7 3.3 %shard_map.155 = (f32[256,1024]{1,0:T(8,128)S(1)}, bf16[4,4,16,128]{3,2,1,0:T(8,128)(2,1)S(1)}, f32[256,128]{1,0:T(8,128)S(1)}, bf16[2048,512]{1,0:T(8,128)(2,1)S(1)}) custom-call(bf16[2,8,4,32,128]{4,3,2,1,0:T(8,128)(2,1)S(1)} %collective-permute-done.9.refs_0_, bf16[2,8,4,32,128]{4,3,2,1,0:T(8,128)(2,1)S(1)} %collective-permute-done.10.refs_1_, ...), custom_call_target="tpu_custom_call" | custom-call | flops 1073741824 | bytes 7340032 | tf_op jit(solution)/shard_map/pallas_call | solution.py:397
  85.0 0.2 collective-permute-done.7.refs_1_
  85.2 2.1 %collective-permute-done.5.refs_0_ = bf16[2,8,4,32,128]{4,3,2,1,0:T(8,128)(2,1)S(1)} collective-permute-done((bf16[2,8,4,32,128]{4,3,2,1,0:T(8,128)(2,1)S(1)}, bf16[2,8,4,32,128]{4,3,2,1,0:T(8,128)(2,1)S(1)}, u32[]{:S(2)}, u32[]{:S(2)}) %collective-permute-start.5) | collective-permute-done | bytes 524320 | tf_op jit(solution)/shard_map/ppermute | solution.py:565
  87.3 0.0 copy-done.2
  87.3 0.0 copy-done.3
  87.3 0.0 copy-start
  87.3 1.9 %shard_map.156 = (f32[256,1024]{1,0:T(8,128)S(1)}, bf16[4,4,16,128]{3,2,1,0:T(8,128)(2,1)S(1)}, f32[256,128]{1,0:T(8,128)S(1)}, f32[2,128]{1,0:T(2,128)S(1)}) custom-call(bf16[2,8,4,32,128]{4,3,2,1,0:T(8,128)(2,1)S(1)} %collective-permute-done.5.refs_0_, bf16[2,8,4,32,128]{4,3,2,1,0:T(8,128)(2,1)S(1)} %collective-permute-done.7.refs_1_, ...), custom_call_target="tpu_custom_call" | custom-call | flops 1073741824 | bytes 7340032 | tf_op jit(solution)/shard_map/pallas_call | solution.py:397
  89.2 16.6 %all_to_all.28 = f32[128,2,128]{2,1,0:T(2,128)S(1)} all-to-all(f32[128,2,128]{2,1,0:T(2,128)S(1)} %bitcast.22), channel_id=1, replica_groups=mesh['x'=4,'core'=2,'tensor'=8,'rep'=4] {'x','tensor','rep'}, dimensions={0} | all-to-all | bytes 262144 | tf_op jit(solution)/shard_map/all_to_all | solution.py:583
  105.8 0.0 copy-done
  105.8 1.3 shard_map.157
  107.2 17.4 %all_to_all.29 = f32[128,4,128]{2,1,0:T(4,128)S(1)} all-to-all(f32[128,4,128]{2,1,0:T(4,128)S(1)} %bitcast.21), channel_id=1, replica_groups=mesh['x'=4,'core'=2,'tensor'=8,'rep'=4] {'x','tensor','rep'}, dimensions={0} | all-to-all | bytes 524288 | tf_op jit(solution)/shard_map/all_to_all | solution.py:586
  124.6 0.1 shard_map.158.own_ref
  124.7 10.6 %collective-permute-start.11 = (f32[2,128]{1,0:T(2,128)S(1)}, f32[2,128]{1,0:T(2,128)S(1)}, u32[]{:S(2)}, u32[]{:S(2)}) collective-permute-start(f32[2,128]{1,0:T(2,128)S(1)} %shard_map.158.own_ref), channel_id=1, source_target_pairs={{0,32},{32,0},{1,33},{33,1},{2,34},{34,2},{3,35},{35,3},{4,36},{36... | collective-permute-start | bytes 3080 | tf_op jit(solution)/shard_map/ppermute | solution.py:245
  135.3 0.8 collective-permute-done.11.peer_ref
  136.1 0.7 shard_map.159
  (3 shorter events, 0.1 us)
Async XLA Ops:
  0.6 7.2 %collective-permute-start = (bf16[1024,256]{1,0:T(8,128)(2,1)}, bf16[1024,256]{1,0:T(8,128)(2,1)S(1)}, u32[]{:S(2)}, u32[]{:S(2)}) collective-permute-start(bf16[1024,256]{1,0:T(8,128)(2,1)} %mix.1), channel_id=1, source_target_pairs={{0,32},{32,0},{1,33},{33,1},{2,34},{34,2},{3,35},{35,3},{4,36},{36... | collective-permute-start | bytes 1572872 | tf_op jit(solution)/shard_map/ppermute | solution.py:245
  4.0 20.6 %copy-start.1 = (bf16[1024]{0:T(1024)(128)(2,1)S(1)}, bf16[1024]{0:T(1024)(128)(2,1)}, u32[]{:S(2)}) copy-start(bf16[1024]{0:T(1024)(128)(2,1)} %param.21) | copy-start | bytes 6148
  7.8 59.3 %collective-permute-start.8 = (bf16[8192,512]{1,0:T(8,128)(2,1)}, bf16[8192,512]{1,0:T(8,128)(2,1)S(1)}, u32[]{:S(2)}, u32[]{:S(2)}) collective-permute-start(bf16[8192,512]{1,0:T(8,128)(2,1)} %refs_3_.3), channel_id=1, source_target_pairs={{0,32},{32,0},{1,33},{33,1},{2,34},{34,2},{3,35},{35,3},{4,36},{36... | collective-permute-start | bytes 25165832 | tf_op jit(solution)/shard_map/ppermute | solution.py:245
  54.6 5.2 %collective-permute-start.3 = (bf16[8,4,32,128]{3,2,1,0:T(8,128)(2,1)S(1)}, bf16[8,4,32,128]{3,2,1,0:T(8,128)(2,1)S(1)}, u32[]{:S(2)}, u32[]{:S(2)}) collective-permute-start(bf16[8,4,32,128]{3,2,1,0:T(8,128)(2,1)S(1)} %bitcast.16), channel_id=1, source_target_pairs={{0,3},{1,0},{2,1},{3,2},{32,224},{33,225},{34,226},{35,227},{64,67... | collective-permute-start | bytes 786440 | tf_op jit(solution)/shard_map/ppermute | solution.py:564
  55.7 6.8 %collective-permute-start.2 = (bf16[8,4,32,128]{3,2,1,0:T(8,128)(2,1)S(1)}, bf16[8,4,32,128]{3,2,1,0:T(8,128)(2,1)S(1)}, u32[]{:S(2)}, u32[]{:S(2)}) collective-permute-start(bf16[8,4,32,128]{3,2,1,0:T(8,128)(2,1)S(1)} %bitcast.17), channel_id=1, source_target_pairs={{0,2},{1,3},{2,0},{3,1},{32,160},{33,161},{34,162},{35,163},{64,66... | collective-permute-start | bytes 786440 | tf_op jit(solution)/shard_map/ppermute | solution.py:564
  56.6 8.8 %collective-permute-start.1 = (bf16[8,4,32,128]{3,2,1,0:T(8,128)(2,1)S(1)}, bf16[8,4,32,128]{3,2,1,0:T(8,128)(2,1)S(1)}, u32[]{:S(2)}, u32[]{:S(2)}) collective-permute-start(bf16[8,4,32,128]{3,2,1,0:T(8,128)(2,1)S(1)} %bitcast.18), channel_id=1, source_target_pairs={{0,1},{1,2},{2,3},{3,0},{32,96},{33,97},{34,98},{35,99},{64,65},{6... | collective-permute-start | bytes 786440 | tf_op jit(solution)/shard_map/ppermute | solution.py:564
  65.5 8.1 %collective-permute-start.6 = (bf16[2,8,4,32,128]{4,3,2,1,0:T(8,128)(2,1)S(1)}, bf16[2,8,4,32,128]{4,3,2,1,0:T(8,128)(2,1)S(1)}, u32[]{:S(2)}, u32[]{:S(2)}) collective-permute-start(bf16[2,8,4,32,128]{4,3,2,1,0:T(8,128)(2,1)S(1)} %shard_map.152.refs_1_), channel_id=1, source_target_pairs={{0,192},{1,193},{2,194},{3,195},{32,35},{33,32},{34,33},{35,34},{6... | collective-permute-start | bytes 1572872 | tf_op jit(solution)/shard_map/ppermute | solution.py:565
  66.3 9.5 %collective-permute-start.4 = (bf16[2,8,4,32,128]{4,3,2,1,0:T(8,128)(2,1)S(1)}, bf16[2,8,4,32,128]{4,3,2,1,0:T(8,128)(2,1)S(1)}, u32[]{:S(2)}, u32[]{:S(2)}) collective-permute-start(bf16[2,8,4,32,128]{4,3,2,1,0:T(8,128)(2,1)S(1)} %shard_map.151.refs_0_), channel_id=1, source_target_pairs={{0,64},{1,65},{2,66},{3,67},{32,33},{33,34},{34,35},{35,32},{64,12... | collective-permute-start | bytes 1572872 | tf_op jit(solution)/shard_map/ppermute | solution.py:565
  69.9 11.8 %collective-permute-start.9 = (bf16[2,8,4,32,128]{4,3,2,1,0:T(8,128)(2,1)S(1)}, bf16[2,8,4,32,128]{4,3,2,1,0:T(8,128)(2,1)S(1)}, u32[]{:S(2)}, u32[]{:S(2)}) collective-permute-start(bf16[2,8,4,32,128]{4,3,2,1,0:T(8,128)(2,1)S(1)} %get-tuple-element.44), channel_id=1, source_target_pairs={{0,64},{1,65},{2,66},{3,67},{32,33},{33,34},{34,35},{35,32},{64,12... | collective-permute-start | bytes 1572872 | tf_op jit(solution)/shard_map/ppermute | solution.py:565
  70.6 11.1 %collective-permute-start.10 = (bf16[2,8,4,32,128]{4,3,2,1,0:T(8,128)(2,1)S(1)}, bf16[2,8,4,32,128]{4,3,2,1,0:T(8,128)(2,1)S(1)}, u32[]{:S(2)}, u32[]{:S(2)}) collective-permute-start(bf16[2,8,4,32,128]{4,3,2,1,0:T(8,128)(2,1)S(1)} %get-tuple-element.45), channel_id=1, source_target_pairs={{0,192},{1,193},{2,194},{3,195},{32,35},{33,32},{34,33},{35,34},{6... | collective-permute-start | bytes 1572872 | tf_op jit(solution)/shard_map/ppermute | solution.py:565
  73.6 11.5 %collective-permute-start.7 = (bf16[2,8,4,32,128]{4,3,2,1,0:T(8,128)(2,1)S(1)}, bf16[2,8,4,32,128]{4,3,2,1,0:T(8,128)(2,1)S(1)}, u32[]{:S(2)}, u32[]{:S(2)}) collective-permute-start(bf16[2,8,4,32,128]{4,3,2,1,0:T(8,128)(2,1)S(1)} %collective-permute-done.6.refs_1_), channel_id=1, source_target_pairs={{0,192},{1,193},{2,194},{3,195},{32,35},{33,32},{34,33},{35,34},{6... | collective-permute-start | bytes 1572872 | tf_op jit(solution)/shard_map/ppermute | solution.py:565
  75.8 11.5 %collective-permute-start.5 = (bf16[2,8,4,32,128]{4,3,2,1,0:T(8,128)(2,1)S(1)}, bf16[2,8,4,32,128]{4,3,2,1,0:T(8,128)(2,1)S(1)}, u32[]{:S(2)}, u32[]{:S(2)}) collective-permute-start(bf16[2,8,4,32,128]{4,3,2,1,0:T(8,128)(2,1)S(1)} %collective-permute-done.4.refs_0_), channel_id=1, source_target_pairs={{0,64},{1,65},{2,66},{3,67},{32,33},{33,34},{34,35},{35,32},{64,12... | collective-permute-start | bytes 1572872 | tf_op jit(solution)/shard_map/ppermute | solution.py:565
  81.7 5.6 %copy-start.2 = (f32[512]{0:T(512)S(1)}, f32[512]{0:T(512)}, u32[]{:S(2)}) copy-start(f32[512]{0:T(512)} %param.23) | copy-start | bytes 6148
  81.7 5.6 %copy-start.3 = (s32[512]{0:T(512)S(1)}, s32[512]{0:T(512)}, u32[]{:S(2)}) copy-start(s32[512]{0:T(512)} %param.25) | copy-start | bytes 6148
  87.3 18.5 %copy-start = (f32[512]{0:T(512)S(1)}, f32[512]{0:T(512)}, u32[]{:S(2)}) copy-start(f32[512]{0:T(512)} %param.24) | copy-start | bytes 6148
  124.7 11.4 %collective-permute-start.11 = (f32[2,128]{1,0:T(2,128)S(1)}, f32[2,128]{1,0:T(2,128)S(1)}, u32[]{:S(2)}, u32[]{:S(2)}) collective-permute-start(f32[2,128]{1,0:T(2,128)S(1)} %shard_map.158.own_ref), channel_id=1, source_target_pairs={{0,32},{32,0},{1,33},{33,1},{2,34},{34,2},{3,35},{35,3},{4,36},{36... | collective-permute-start | bytes 3080 | tf_op jit(solution)/shard_map/ppermute | solution.py:245

commit v5 on v4

--- a/solution.py
+++ b/solution.py
@@ -278,13 +278,14 @@
         z_in, sq_in = take(2)
     if ready:
         (lexs,) = take(1)
+    if last or following:
+        sharp_ref, chosen_ref = take(2)
     if last:
-        sharp_ref, chosen_ref = take(2)
         z_out, pick_out, lse_out, tok_out = take(4)
     else:
         z_out, pick_out, sq_out = take(3)
     if following:
-        (lex_next,) = take(1)
+        lex_next, sharp_out, chosen_out = take(3)
     if first:
         for source, copy_out in zip(sources, take(len(sources))):
             copy_out[...] = source[...]
@@ -337,12 +338,14 @@
     if not last:
         sq_out[...] = squares
     if following:
+        sharp_out[...] = column_of(sharp_ref[...], held)
+        chosen_out[...] = column_of(chosen_ref[...].astype(F32), held)
         for group in next_copies:
             for copy in group:
                 copy.wait()
     if last:
-        sharp = column_of(sharp_ref[...], held)
-        chosen = column_of(chosen_ref[...].astype(F32), held).astype(jnp.int32)
+        sharp = sharp_ref[...]
+        chosen = chosen_ref[...].astype(jnp.int32)
         scale = lax.rsqrt(jnp.sum(squares, axis=1, keepdims=True) / 8192.0 + 1e-05) * sharp
         z = z_out[...] * scale
         z_out[...] = z
@@ -365,7 +368,7 @@
 def head_call(sources, at, following, gain, lex_own, lex_peer, state, lexs, closing):
     sides = [source.shape[0] for source in sources]
     total = sum(sides)
-    first, ready, last = state is None, lexs is not None, closing is not None
+    first, ready, last = state is None, lexs is not None, closing is not None and not following
     vmem, anywhere = pl.BlockSpec(), pl.BlockSpec(memory_space=pl.ANY)
     in_specs = [vmem] * (len(sources) + 1) + [anywhere, vmem]
     operands = [*sources, gain, in_hbm(lex_own), in_vmem(lex_peer)]
@@ -387,6 +390,7 @@
         out_shape += [jax.ShapeDtypeStruct((256, 128), F32)]
     if following:
         out_shape += [pltpu.VMEM((512 * following, 512), BF16)]
+        out_shape += [pltpu.VMEM((256, 1), F32)] * 2
     if first:
         out_shape += [jax.ShapeDtypeStruct(source.shape, source.dtype) for source in sources]
     if not ready:
@@ -574,8 +578,10 @@
     z, pick_0, sq, low, high = head_call([low, high], 0, 0, *fixed, None, None, None)
     left_high, right_low = far(high, 1), far(low, -1)
     z, pick_1, sq = head_call([left_low, right_high], 4, 0, *fixed, (z, sq), None, None)
-    z, pick_2, sq, lexs = head_call([left_high, right_low], 8, 4, *fixed, (z, sq), None, None)
     closing = (sharpening_factor.reshape(4, 128), chosen_symbols.reshape(4, 128))
+    z, pick_2, sq, lexs, *closing = head_call(
+        [left_high, right_low], 8, 4, *fixed, (z, sq), None, closing
+    )
     z, pick_3, lse, tok = head_call(
         [past_low, past_high], 12, 0, *fixed, (z, sq), (lexs,), closing
     )

time: 137 us -> 137 us (level)
  no operation moved by 1% of the time
where the time goes in v5:
time: 137 us
  blocking collectives  80.3 us (59%)
  starting transfers between devices  23.2 us (17%)
  Pallas kernels  17.2 us (13%)
  waiting for transfers between devices  15.3 us (11%)
    all_to_all x1, blocking collectives, shards(): got = lax.all_to_all(sent.reshape(128, 4, 128), SAME_CORE, 0, 0, tiled=True)  17.4 us
    all_to_all x1, blocking collectives, shards(): got = lax.all_to_all(sent, 'tensor', 0, 0, tiled=True)  17.2 us
    all_to_all x1, blocking collectives, shards(): lax.all_to_all(sent, ('x', 'rep'), 0, 0, tiled=True).reshape(256, 1280)  16.7 us
    all_to_all x1, blocking collectives, shards(): lax.all_to_all(lse.reshape(128, 2, 128), SAME_CORE, 0, 0, tiled=True)  16.6 us
    ppermute x3, starting transfers between devices, swap_core(): return lax.ppermute(value, 'core', [(0, 1), (1, 0)])  14 us
    all_to_all x1, blocking collectives, shards(): lax.all_to_all(sent, 'tensor', 0, 0, tiled=True).reshape(8, 4, 32, 128)  12.4 us
    pallas_call x4, Pallas kernels, head_call(): pl.pallas_call(functools.partial(head_body, (sides, at, ready, following,...  10.7 us
    ppermute x3, waiting for transfers between devices, shards(): side = lambda v, s: lax.ppermute(v, PLANE, turn_other(s))  7.94 us
  transfers between devices with their start and end apart: 12, of which 9 were waited for; matrix products, arithmetic and copies ran while one was open for 0% of the time, Pallas kernels for 10%

profile of v5, /device:TPU:1, one launch (start us, length us, event | category | flops | bytes accessed | tf_op | source)
XLA Modules:
  0.0 136.7 jit_solution(15671209773658236067)
XLA Ops:
  0.6 3.3 %collective-permute-start = (bf16[1024,256]{1,0:T(8,128)(2,1)}, bf16[1024,256]{1,0:T(8,128)(2,1)S(1)}, u32[]{:S(2)}, u32[]{:S(2)}) collective-permute-start(bf16[1024,256]{1,0:T(8,128)(2,1)} %mix.1), channel_id=1, source_target_pairs={{0,32},{32,0},{1,33},{33,1},{2,34},{34,2},{3,35},{35,3},{4,36},{36... | collective-permute-start | bytes 1572872 | tf_op jit(solution)/shard_map/ppermute | solution.py:245
  4.0 0.0 copy-start.1
  4.0 3.8 %shard_map.148 = (bf16[16,16,1280]{2,1,0:T(8,128)(2,1)S(1)}, bf16[1024,256]{1,0:T(8,128)(2,1)S(1)}) custom-call(s32[16]{0:T(128)} %counts.1, bf16[16,8,128]{2,1,0:T(8,128)(2,1)} %q_ref.1, bf16[16,1,512,128]{3,2,1,0:T(8,128)(2,1)} %k_hbm.1, bf16[16,1,512,128]{3,2,1,0:T(8,128)(2,1)} %v_hbm.1, bf16[16,128]{1,0:T(8,128)(2,1)} %bitcast.29, ...), custom_call_target="tpu_custom_call" | custom-call | tf_op jit(solution)/shard_map/pallas_call | solution.py:141
  7.8 0.0 collective-permute-done.peer_ref
  7.8 0.1 collective-permute-start.8
  7.9 16.7 %all_to_all.25 = bf16[16,16,1280]{2,1,0:T(8,128)(2,1)S(1)} all-to-all(bf16[16,16,1280]{2,1,0:T(8,128)(2,1)S(1)} %get-tuple-element.37), channel_id=1, replica_groups=mesh['x'=4,'core'=2,'tensor'=8,'rep'=4] {'x','rep'}, dimensions={0} | all-to-all | bytes 1310720 | tf_op jit(solution)/shard_map/all_to_all | solution.py:561
  24.6 0.0 copy-done.1
  24.6 0.4 shard_map.149
  25.0 17.2 %all_to_all.26.got_ref = bf16[8,136,128]{2,1,0:T(8,128)(2,1)S(1)} all-to-all(bf16[8,136,128]{2,1,0:T(8,128)(2,1)S(1)} %shard_map.149), channel_id=1, replica_groups=mesh['x'=4,'core'=2,'tensor'=8,'rep'=4] {'tensor'}, dimensions={0} | all-to-all | bytes 557056 | tf_op jit(solution)/shard_map/all_to_all | solution.py:564
  42.3 12.4 %all_to_all.27 = bf16[8,128,128]{2,1,0:T(8,128)(2,1)S(1)} all-to-all(bf16[8,128,128]{2,1,0:T(8,128)(2,1)S(1)} %get-tuple-element.40), channel_id=1, replica_groups=mesh['x'=4,'core'=2,'tensor'=8,'rep'=4] {'tensor'}, dimensions={0} | all-to-all | bytes 524288 | tf_op jit(solution)/shard_map/all_to_all | solution.py:567
  54.6 1.0 collective-permute-start.3
  55.7 1.0 collective-permute-start.2
  56.6 0.9 collective-permute-start.1
  57.5 2.4 %collective-permute-done.3.second_ref = bf16[8,4,32,128]{3,2,1,0:T(8,128)(2,1)S(1)} collective-permute-done((bf16[8,4,32,128]{3,2,1,0:T(8,128)(2,1)S(1)}, bf16[8,4,32,128]{3,2,1,0:T(8,128)(2,1)S(1)}, u32[]{:S(2)}, u32[]{:S(2)}) %collective-permute-start.3) | collective-permute-done | bytes 262176 | tf_op jit(solution)/shard_map/ppermute | solution.py:568
  59.9 2.6 %collective-permute-done.2.second_ref = bf16[8,4,32,128]{3,2,1,0:T(8,128)(2,1)S(1)} collective-permute-done((bf16[8,4,32,128]{3,2,1,0:T(8,128)(2,1)S(1)}, bf16[8,4,32,128]{3,2,1,0:T(8,128)(2,1)S(1)}, u32[]{:S(2)}, u32[]{:S(2)}) %collective-permute-start.2) | collective-permute-done | bytes 262176 | tf_op jit(solution)/shard_map/ppermute | solution.py:568
  62.5 3.0 %collective-permute-done.1.first_ref = bf16[8,4,32,128]{3,2,1,0:T(8,128)(2,1)S(1)} collective-permute-done((bf16[8,4,32,128]{3,2,1,0:T(8,128)(2,1)S(1)}, bf16[8,4,32,128]{3,2,1,0:T(8,128)(2,1)S(1)}, u32[]{:S(2)}, u32[]{:S(2)}) %collective-permute-start.1) | collective-permute-done | bytes 262176 | tf_op jit(solution)/shard_map/ppermute | solution.py:568
  65.5 0.8 collective-permute-start.6
  66.3 0.7 collective-permute-start.4
  67.1 0.0 collective-permute-done.8.refs_4_
  67.1 2.8 %shard_map.153 = (f32[256,1024]{1,0:T(8,128)S(1)}, bf16[4,4,16,128]{3,2,1,0:T(8,128)(2,1)S(1)}, f32[256,128]{1,0:T(8,128)S(1)}, bf16[2,8,4,32,128]{4,3,2,1,0:T(8,128)(2,1)S(1)}, bf16[2,8,4,32,128]{4,3,2,1,0:T(8,128)(2,1)S(1)}) custom-call(bf16[2,8,4,32,128]{4,3,2,1,0:T(8,128)(2,1)S(1)} %shard_map.151.refs_0_, ...), custom_call_target="tpu_custom_call" | custom-call | flops 1073741824 | bytes 7340032 | tf_op jit(solution)/shard_map/pallas_call | solution.py:401
  69.8 0.8 collective-permute-start.9
  70.6 2.0 %collective-permute-start.10 = (bf16[2,8,4,32,128]{4,3,2,1,0:T(8,128)(2,1)S(1)}, bf16[2,8,4,32,128]{4,3,2,1,0:T(8,128)(2,1)S(1)}, u32[]{:S(2)}, u32[]{:S(2)}) collective-permute-start(bf16[2,8,4,32,128]{4,3,2,1,0:T(8,128)(2,1)S(1)} %get-tuple-element.47), channel_id=1, source_target_pairs={{0,192},{1,193},{2,194},{3,195},{32,35},{33,32},{34,33},{35,34},{6... | collective-permute-start | bytes 1572872 | tf_op jit(solution)/shard_map/ppermute | solution.py:569
  72.6 1.0 collective-permute-done.6.refs_1_
  73.6 2.0 %collective-permute-start.7 = (bf16[2,8,4,32,128]{4,3,2,1,0:T(8,128)(2,1)S(1)}, bf16[2,8,4,32,128]{4,3,2,1,0:T(8,128)(2,1)S(1)}, u32[]{:S(2)}, u32[]{:S(2)}) collective-permute-start(bf16[2,8,4,32,128]{4,3,2,1,0:T(8,128)(2,1)S(1)} %collective-permute-done.6.refs_1_), channel_id=1, source_target_pairs={{0,192},{1,193},{2,194},{3,195},{32,35},{33,32},{34,33},{35,34},{6... | collective-permute-start | bytes 1572872 | tf_op jit(solution)/shard_map/ppermute | solution.py:569
  75.6 0.1 collective-permute-done.4.refs_0_
  75.8 0.0 collective-permute-start.5
  75.8 0.0 copy-start.2
  75.8 0.0 copy-start.3
  75.8 2.9 %shard_map.154 = (f32[256,1024]{1,0:T(8,128)S(1)}, bf16[4,4,16,128]{3,2,1,0:T(8,128)(2,1)S(1)}, f32[256,128]{1,0:T(8,128)S(1)}) custom-call(bf16[2,8,4,32,128]{4,3,2,1,0:T(8,128)(2,1)S(1)} %collective-permute-done.4.refs_0_, bf16[2,8,4,32,128]{4,3,2,1,0:T(8,128)(2,1)S(1)} %collective-permute-done.6.refs_1_, f32[64,128]{1,0:T(8,128)S(1)} %get-tuple-element.44.refs_2_, ...), custom_call_target="tpu_custom_call" | custom-call | flops 1073741824 | bytes 7340032 | tf_op jit(solution)/shard_map/pallas_call | solution.py:401
  78.7 3.0 %collective-permute-done.9.refs_0_ = bf16[2,8,4,32,128]{4,3,2,1,0:T(8,128)(2,1)S(1)} collective-permute-done((bf16[2,8,4,32,128]{4,3,2,1,0:T(8,128)(2,1)S(1)}, bf16[2,8,4,32,128]{4,3,2,1,0:T(8,128)(2,1)S(1)}, u32[]{:S(2)}, u32[]{:S(2)}) %collective-permute-start.9) | collective-permute-done | bytes 524320 | tf_op jit(solution)/shard_map/ppermute | solution.py:569
  81.7 0.0 collective-permute-done.10.refs_1_
  81.7 0.0 copy-done.2
  81.7 0.0 copy-done.3
  81.7 3.2 %shard_map.155 = (f32[256,1024]{1,0:T(8,128)S(1)}, bf16[4,4,16,128]{3,2,1,0:T(8,128)(2,1)S(1)}, f32[256,128]{1,0:T(8,128)S(1)}, bf16[2048,512]{1,0:T(8,128)(2,1)...) custom-call(bf16[2,8,4,32,128]{4,3,2,1,0:T(8,128)(2,1)S(1)} %collective-permute-done.9.refs_0_, ...), custom_call_target="tpu_custom_call" | custom-call | flops 1073741824 | bytes 7340032 | tf_op jit(solution)/shard_map/pallas_call | solution.py:401
  84.9 0.2 collective-permute-done.7.refs_1_
  85.2 2.1 %collective-permute-done.5.refs_0_ = bf16[2,8,4,32,128]{4,3,2,1,0:T(8,128)(2,1)S(1)} collective-permute-done((bf16[2,8,4,32,128]{4,3,2,1,0:T(8,128)(2,1)S(1)}, bf16[2,8,4,32,128]{4,3,2,1,0:T(8,128)(2,1)S(1)}, u32[]{:S(2)}, u32[]{:S(2)}) %collective-permute-start.5) | collective-permute-done | bytes 524320 | tf_op jit(solution)/shard_map/ppermute | solution.py:569
  87.3 0.0 copy-start
  87.3 1.8 %shard_map.156 = (f32[256,1024]{1,0:T(8,128)S(1)}, bf16[4,4,16,128]{3,2,1,0:T(8,128)(2,1)S(1)}, f32[256,128]{1,0:T(8,128)S(1)}, f32[2,128]{1,0:T(2,128)S(1)}) custom-call(bf16[2,8,4,32,128]{4,3,2,1,0:T(8,128)(2,1)S(1)} %collective-permute-done.5.refs_0_, bf16[2,8,4,32,128]{4,3,2,1,0:T(8,128)(2,1)S(1)} %collective-permute-done.7.refs_1_, ...), custom_call_target="tpu_custom_call" | custom-call | flops 1073741824 | bytes 7340032 | tf_op jit(solution)/shard_map/pallas_call | solution.py:401
  89.1 16.6 %all_to_all.28 = f32[128,2,128]{2,1,0:T(2,128)S(1)} all-to-all(f32[128,2,128]{2,1,0:T(2,128)S(1)} %bitcast.22), channel_id=1, replica_groups=mesh['x'=4,'core'=2,'tensor'=8,'rep'=4] {'x','tensor','rep'}, dimensions={0} | all-to-all | bytes 262144 | tf_op jit(solution)/shard_map/all_to_all | solution.py:589
  105.7 0.0 copy-done
  105.8 1.3 shard_map.157
  107.1 17.4 %all_to_all.29 = f32[128,4,128]{2,1,0:T(4,128)S(1)} all-to-all(f32[128,4,128]{2,1,0:T(4,128)S(1)} %bitcast.21), channel_id=1, replica_groups=mesh['x'=4,'core'=2,'tensor'=8,'rep'=4] {'x','tensor','rep'}, dimensions={0} | all-to-all | bytes 524288 | tf_op jit(solution)/shard_map/all_to_all | solution.py:592
  124.5 0.1 shard_map.158.own_ref
  124.6 10.6 %collective-permute-start.11 = (f32[2,128]{1,0:T(2,128)S(1)}, f32[2,128]{1,0:T(2,128)S(1)}, u32[]{:S(2)}, u32[]{:S(2)}) collective-permute-start(f32[2,128]{1,0:T(2,128)S(1)} %shard_map.158.own_ref), channel_id=1, source_target_pairs={{0,32},{32,0},{1,33},{33,1},{2,34},{34,2},{3,35},{35,3},{4,36},{36... | collective-permute-start | bytes 3080 | tf_op jit(solution)/shard_map/ppermute | solution.py:245
  135.2 0.8 collective-permute-done.11.peer_ref
  136.0 0.7 shard_map.159
  (3 shorter events, 0.1 us)
Async XLA Ops:
  0.6 7.2 %collective-permute-start = (bf16[1024,256]{1,0:T(8,128)(2,1)}, bf16[1024,256]{1,0:T(8,128)(2,1)S(1)}, u32[]{:S(2)}, u32[]{:S(2)}) collective-permute-start(bf16[1024,256]{1,0:T(8,128)(2,1)} %mix.1), channel_id=1, source_target_pairs={{0,32},{32,0},{1,33},{33,1},{2,34},{34,2},{3,35},{35,3},{4,36},{36... | collective-permute-start | bytes 1572872 | tf_op jit(solution)/shard_map/ppermute | solution.py:245
  4.0 20.6 %copy-start.1 = (bf16[1024]{0:T(1024)(128)(2,1)S(1)}, bf16[1024]{0:T(1024)(128)(2,1)}, u32[]{:S(2)}) copy-start(bf16[1024]{0:T(1024)(128)(2,1)} %param.21) | copy-start | bytes 6148
  7.8 59.3 %collective-permute-start.8 = (bf16[8192,512]{1,0:T(8,128)(2,1)}, bf16[8192,512]{1,0:T(8,128)(2,1)S(1)}, u32[]{:S(2)}, u32[]{:S(2)}) collective-permute-start(bf16[8192,512]{1,0:T(8,128)(2,1)} %refs_3_.3), channel_id=1, source_target_pairs={{0,32},{32,0},{1,33},{33,1},{2,34},{34,2},{3,35},{35,3},{4,36},{36... | collective-permute-start | bytes 25165832 | tf_op jit(solution)/shard_map/ppermute | solution.py:245
  54.6 5.2 %collective-permute-start.3 = (bf16[8,4,32,128]{3,2,1,0:T(8,128)(2,1)S(1)}, bf16[8,4,32,128]{3,2,1,0:T(8,128)(2,1)S(1)}, u32[]{:S(2)}, u32[]{:S(2)}) collective-permute-start(bf16[8,4,32,128]{3,2,1,0:T(8,128)(2,1)S(1)} %bitcast.16), channel_id=1, source_target_pairs={{0,3},{1,0},{2,1},{3,2},{32,224},{33,225},{34,226},{35,227},{64,67... | collective-permute-start | bytes 786440 | tf_op jit(solution)/shard_map/ppermute | solution.py:568
  55.7 6.8 %collective-permute-start.2 = (bf16[8,4,32,128]{3,2,1,0:T(8,128)(2,1)S(1)}, bf16[8,4,32,128]{3,2,1,0:T(8,128)(2,1)S(1)}, u32[]{:S(2)}, u32[]{:S(2)}) collective-permute-start(bf16[8,4,32,128]{3,2,1,0:T(8,128)(2,1)S(1)} %bitcast.17), channel_id=1, source_target_pairs={{0,2},{1,3},{2,0},{3,1},{32,160},{33,161},{34,162},{35,163},{64,66... | collective-permute-start | bytes 786440 | tf_op jit(solution)/shard_map/ppermute | solution.py:568
  56.6 8.8 %collective-permute-start.1 = (bf16[8,4,32,128]{3,2,1,0:T(8,128)(2,1)S(1)}, bf16[8,4,32,128]{3,2,1,0:T(8,128)(2,1)S(1)}, u32[]{:S(2)}, u32[]{:S(2)}) collective-permute-start(bf16[8,4,32,128]{3,2,1,0:T(8,128)(2,1)S(1)} %bitcast.18), channel_id=1, source_target_pairs={{0,1},{1,2},{2,3},{3,0},{32,96},{33,97},{34,98},{35,99},{64,65},{6... | collective-permute-start | bytes 786440 | tf_op jit(solution)/shard_map/ppermute | solution.py:568
  65.5 8.1 %collective-permute-start.6 = (bf16[2,8,4,32,128]{4,3,2,1,0:T(8,128)(2,1)S(1)}, bf16[2,8,4,32,128]{4,3,2,1,0:T(8,128)(2,1)S(1)}, u32[]{:S(2)}, u32[]{:S(2)}) collective-permute-start(bf16[2,8,4,32,128]{4,3,2,1,0:T(8,128)(2,1)S(1)} %shard_map.152.refs_1_), channel_id=1, source_target_pairs={{0,192},{1,193},{2,194},{3,195},{32,35},{33,32},{34,33},{35,34},{6... | collective-permute-start | bytes 1572872 | tf_op jit(solution)/shard_map/ppermute | solution.py:569
  66.3 9.5 %collective-permute-start.4 = (bf16[2,8,4,32,128]{4,3,2,1,0:T(8,128)(2,1)S(1)}, bf16[2,8,4,32,128]{4,3,2,1,0:T(8,128)(2,1)S(1)}, u32[]{:S(2)}, u32[]{:S(2)}) collective-permute-start(bf16[2,8,4,32,128]{4,3,2,1,0:T(8,128)(2,1)S(1)} %shard_map.151.refs_0_), channel_id=1, source_target_pairs={{0,64},{1,65},{2,66},{3,67},{32,33},{33,34},{34,35},{35,32},{64,12... | collective-permute-start | bytes 1572872 | tf_op jit(solution)/shard_map/ppermute | solution.py:569
  69.8 11.9 %collective-permute-start.9 = (bf16[2,8,4,32,128]{4,3,2,1,0:T(8,128)(2,1)S(1)}, bf16[2,8,4,32,128]{4,3,2,1,0:T(8,128)(2,1)S(1)}, u32[]{:S(2)}, u32[]{:S(2)}) collective-permute-start(bf16[2,8,4,32,128]{4,3,2,1,0:T(8,128)(2,1)S(1)} %get-tuple-element.46), channel_id=1, source_target_pairs={{0,64},{1,65},{2,66},{3,67},{32,33},{33,34},{34,35},{35,32},{64,12... | collective-permute-start | bytes 1572872 | tf_op jit(solution)/shard_map/ppermute | solution.py:569
  70.6 11.1 %collective-permute-start.10 = (bf16[2,8,4,32,128]{4,3,2,1,0:T(8,128)(2,1)S(1)}, bf16[2,8,4,32,128]{4,3,2,1,0:T(8,128)(2,1)S(1)}, u32[]{:S(2)}, u32[]{:S(2)}) collective-permute-start(bf16[2,8,4,32,128]{4,3,2,1,0:T(8,128)(2,1)S(1)} %get-tuple-element.47), channel_id=1, source_target_pairs={{0,192},{1,193},{2,194},{3,195},{32,35},{33,32},{34,33},{35,34},{6... | collective-permute-start | bytes 1572872 | tf_op jit(solution)/shard_map/ppermute | solution.py:569
  73.6 11.5 %collective-permute-start.7 = (bf16[2,8,4,32,128]{4,3,2,1,0:T(8,128)(2,1)S(1)}, bf16[2,8,4,32,128]{4,3,2,1,0:T(8,128)(2,1)S(1)}, u32[]{:S(2)}, u32[]{:S(2)}) collective-permute-start(bf16[2,8,4,32,128]{4,3,2,1,0:T(8,128)(2,1)S(1)} %collective-permute-done.6.refs_1_), channel_id=1, source_target_pairs={{0,192},{1,193},{2,194},{3,195},{32,35},{33,32},{34,33},{35,34},{6... | collective-permute-start | bytes 1572872 | tf_op jit(solution)/shard_map/ppermute | solution.py:569
  75.8 11.5 %collective-permute-start.5 = (bf16[2,8,4,32,128]{4,3,2,1,0:T(8,128)(2,1)S(1)}, bf16[2,8,4,32,128]{4,3,2,1,0:T(8,128)(2,1)S(1)}, u32[]{:S(2)}, u32[]{:S(2)}) collective-permute-start(bf16[2,8,4,32,128]{4,3,2,1,0:T(8,128)(2,1)S(1)} %collective-permute-done.4.refs_0_), channel_id=1, source_target_pairs={{0,64},{1,65},{2,66},{3,67},{32,33},{33,34},{34,35},{35,32},{64,12... | collective-permute-start | bytes 1572872 | tf_op jit(solution)/shard_map/ppermute | solution.py:569
  75.8 5.9 %copy-start.2 = (f32[512]{0:T(512)S(1)}, f32[512]{0:T(512)}, u32[]{:S(2)}) copy-start(f32[512]{0:T(512)} %param.23) | copy-start | bytes 6148
  75.8 5.9 %copy-start.3 = (s32[512]{0:T(512)S(1)}, s32[512]{0:T(512)}, u32[]{:S(2)}) copy-start(s32[512]{0:T(512)} %param.25) | copy-start | bytes 6148
  87.3 18.4 %copy-start = (f32[512]{0:T(512)S(1)}, f32[512]{0:T(512)}, u32[]{:S(2)}) copy-start(f32[512]{0:T(512)} %param.24) | copy-start | bytes 6148
  124.6 11.4 %collective-permute-start.11 = (f32[2,128]{1,0:T(2,128)S(1)}, f32[2,128]{1,0:T(2,128)S(1)}, u32[]{:S(2)}, u32[]{:S(2)}) collective-permute-start(f32[2,128]{1,0:T(2,128)S(1)} %shard_map.158.own_ref), channel_id=1, source_target_pairs={{0,32},{32,0},{1,33},{33,1},{2,34},{34,2},{3,35},{35,3},{4,36},{36... | collective-permute-start | bytes 3080 | tf_op jit(solution)/shard_map/ppermute | solution.py:245

commit v6 on v5

--- a/solution.py
+++ b/solution.py
@@ -454,9 +454,11 @@
         norm = top + jnp.log(total)
         norm_out[h : h + 1, :] = norm
         columns.append(jnp.transpose(jnp.broadcast_to(norm, (128, 128)))[:, :1])
-    logp = z_ref[...] - jnp.concatenate(columns, axis=0)
-    gate = cut_slope * (level + logp * (1.0 / LN2))
-    kept = jnp.sum(jnp.exp(logp) / (1.0 + jnp.exp(-gate)), axis=1, keepdims=True)
+    norms = jnp.concatenate(columns, axis=0)
+    z = z_ref[...]
+    slope = cut_slope / LN2
+    offset = slope * norms - cut_slope * level
+    kept = jnp.sum(jnp.exp(z - norms) / (1.0 + jnp.exp(offset - slope * z)), axis=1, keepdims=True)
     low, high = rows_of(kept, 512)
     which = lax.broadcasted_iota(jnp.int32, (512, 128), 0) % 4
     out_ref[...] = jnp.where(

time: 137 us -> 137 us (level)
  no operation moved by 1% of the time
where the time goes in v6:
time: 137 us
  blocking collectives  80.3 us (59%)
  starting transfers between devices  23.2 us (17%)
  Pallas kernels  17.1 us (12%)
  waiting for transfers between devices  15.3 us (11%)
    all_to_all x1, blocking collectives, shards(): got = lax.all_to_all(sent.reshape(128, 4, 128), SAME_CORE, 0, 0, tiled=True)  17.4 us
    all_to_all x1, blocking collectives, shards(): got = lax.all_to_all(sent, 'tensor', 0, 0, tiled=True)  17.2 us
    all_to_all x1, blocking collectives, shards(): lax.all_to_all(sent, ('x', 'rep'), 0, 0, tiled=True).reshape(256, 1280)  16.7 us
    all_to_all x1, blocking collectives, shards(): lax.all_to_all(lse.reshape(128, 2, 128), SAME_CORE, 0, 0, tiled=True)  16.6 us
    ppermute x3, starting transfers between devices, swap_core(): return lax.ppermute(value, 'core', [(0, 1), (1, 0)])  14 us
    all_to_all x1, blocking collectives, shards(): lax.all_to_all(sent, 'tensor', 0, 0, tiled=True).reshape(8, 4, 32, 128)  12.4 us
    pallas_call x4, Pallas kernels, head_call(): pl.pallas_call(functools.partial(head_body, (sides, at, ready, following,...  10.7 us
    ppermute x3, waiting for transfers between devices, shards(): side = lambda v, s: lax.ppermute(v, PLANE, turn_other(s))  7.94 us
  transfers between devices with their start and end apart: 12, of which 9 were waited for; matrix products, arithmetic and copies ran while one was open for 0% of the time, Pallas kernels for 10%

profile of v6, /device:TPU:1, one launch (start us, length us, event | category | flops | bytes accessed | tf_op | source)
XLA Modules:
  0.0 136.6 jit_solution(14782242164082750375)
XLA Ops:
  0.6 3.3 %collective-permute-start = (bf16[1024,256]{1,0:T(8,128)(2,1)}, bf16[1024,256]{1,0:T(8,128)(2,1)S(1)}, u32[]{:S(2)}, u32[]{:S(2)}) collective-permute-start(bf16[1024,256]{1,0:T(8,128)(2,1)} %mix.1), channel_id=1, source_target_pairs={{0,32},{32,0},{1,33},{33,1},{2,34},{34,2},{3,35},{35,3},{4,36},{36... | collective-permute-start | bytes 1572872 | tf_op jit(solution)/shard_map/ppermute | solution.py:245
  4.0 0.0 copy-start.1
  4.0 3.8 %shard_map.148 = (bf16[16,16,1280]{2,1,0:T(8,128)(2,1)S(1)}, bf16[1024,256]{1,0:T(8,128)(2,1)S(1)}) custom-call(s32[16]{0:T(128)} %counts.1, bf16[16,8,128]{2,1,0:T(8,128)(2,1)} %q_ref.1, bf16[16,1,512,128]{3,2,1,0:T(8,128)(2,1)} %k_hbm.1, bf16[16,1,512,128]{3,2,1,0:T(8,128)(2,1)} %v_hbm.1, bf16[16,128]{1,0:T(8,128)(2,1)} %bitcast.29, ...), custom_call_target="tpu_custom_call" | custom-call | tf_op jit(solution)/shard_map/pallas_call | solution.py:141
  7.8 0.0 collective-permute-done.peer_ref
  7.8 0.1 collective-permute-start.8
  7.9 16.7 %all_to_all.25 = bf16[16,16,1280]{2,1,0:T(8,128)(2,1)S(1)} all-to-all(bf16[16,16,1280]{2,1,0:T(8,128)(2,1)S(1)} %get-tuple-element.37), channel_id=1, replica_groups=mesh['x'=4,'core'=2,'tensor'=8,'rep'=4] {'x','rep'}, dimensions={0} | all-to-all | bytes 1310720 | tf_op jit(solution)/shard_map/all_to_all | solution.py:563
  24.6 0.0 copy-done.1
  24.6 0.4 shard_map.149
  25.0 17.2 %all_to_all.26.got_ref = bf16[8,136,128]{2,1,0:T(8,128)(2,1)S(1)} all-to-all(bf16[8,136,128]{2,1,0:T(8,128)(2,1)S(1)} %shard_map.149), channel_id=1, replica_groups=mesh['x'=4,'core'=2,'tensor'=8,'rep'=4] {'tensor'}, dimensions={0} | all-to-all | bytes 557056 | tf_op jit(solution)/shard_map/all_to_all | solution.py:566
  42.3 12.4 %all_to_all.27 = bf16[8,128,128]{2,1,0:T(8,128)(2,1)S(1)} all-to-all(bf16[8,128,128]{2,1,0:T(8,128)(2,1)S(1)} %get-tuple-element.40), channel_id=1, replica_groups=mesh['x'=4,'core'=2,'tensor'=8,'rep'=4] {'tensor'}, dimensions={0} | all-to-all | bytes 524288 | tf_op jit(solution)/shard_map/all_to_all | solution.py:569
  54.6 1.0 collective-permute-start.3
  55.7 1.0 collective-permute-start.2
  56.6 0.9 collective-permute-start.1
  57.5 2.4 %collective-permute-done.3.second_ref = bf16[8,4,32,128]{3,2,1,0:T(8,128)(2,1)S(1)} collective-permute-done((bf16[8,4,32,128]{3,2,1,0:T(8,128)(2,1)S(1)}, bf16[8,4,32,128]{3,2,1,0:T(8,128)(2,1)S(1)}, u32[]{:S(2)}, u32[]{:S(2)}) %collective-permute-start.3) | collective-permute-done | bytes 262176 | tf_op jit(solution)/shard_map/ppermute | solution.py:570
  59.9 2.6 %collective-permute-done.2.second_ref = bf16[8,4,32,128]{3,2,1,0:T(8,128)(2,1)S(1)} collective-permute-done((bf16[8,4,32,128]{3,2,1,0:T(8,128)(2,1)S(1)}, bf16[8,4,32,128]{3,2,1,0:T(8,128)(2,1)S(1)}, u32[]{:S(2)}, u32[]{:S(2)}) %collective-permute-start.2) | collective-permute-done | bytes 262176 | tf_op jit(solution)/shard_map/ppermute | solution.py:570
  62.5 3.0 %collective-permute-done.1.first_ref = bf16[8,4,32,128]{3,2,1,0:T(8,128)(2,1)S(1)} collective-permute-done((bf16[8,4,32,128]{3,2,1,0:T(8,128)(2,1)S(1)}, bf16[8,4,32,128]{3,2,1,0:T(8,128)(2,1)S(1)}, u32[]{:S(2)}, u32[]{:S(2)}) %collective-permute-start.1) | collective-permute-done | bytes 262176 | tf_op jit(solution)/shard_map/ppermute | solution.py:570
  65.5 0.8 collective-permute-start.6
  66.3 0.7 collective-permute-start.4
  67.1 0.0 collective-permute-done.8.refs_4_
  67.1 2.8 %shard_map.153 = (f32[256,1024]{1,0:T(8,128)S(1)}, bf16[4,4,16,128]{3,2,1,0:T(8,128)(2,1)S(1)}, f32[256,128]{1,0:T(8,128)S(1)}, bf16[2,8,4,32,128]{4,3,2,1,0:T(8,128)(2,1)S(1)}, bf16[2,8,4,32,128]{4,3,2,1,0:T(8,128)(2,1)S(1)}) custom-call(bf16[2,8,4,32,128]{4,3,2,1,0:T(8,128)(2,1)S(1)} %shard_map.151.refs_0_, ...), custom_call_target="tpu_custom_call" | custom-call | flops 1073741824 | bytes 7340032 | tf_op jit(solution)/shard_map/pallas_call | solution.py:401
  69.8 0.8 collective-permute-start.9
  70.6 2.0 %collective-permute-start.10 = (bf16[2,8,4,32,128]{4,3,2,1,0:T(8,128)(2,1)S(1)}, bf16[2,8,4,32,128]{4,3,2,1,0:T(8,128)(2,1)S(1)}, u32[]{:S(2)}, u32[]{:S(2)}) collective-permute-start(bf16[2,8,4,32,128]{4,3,2,1,0:T(8,128)(2,1)S(1)} %get-tuple-element.47), channel_id=1, source_target_pairs={{0,192},{1,193},{2,194},{3,195},{32,35},{33,32},{34,33},{35,34},{6... | collective-permute-start | bytes 1572872 | tf_op jit(solution)/shard_map/ppermute | solution.py:571
  72.6 1.0 collective-permute-done.6.refs_1_
  73.6 2.0 %collective-permute-start.7 = (bf16[2,8,4,32,128]{4,3,2,1,0:T(8,128)(2,1)S(1)}, bf16[2,8,4,32,128]{4,3,2,1,0:T(8,128)(2,1)S(1)}, u32[]{:S(2)}, u32[]{:S(2)}) collective-permute-start(bf16[2,8,4,32,128]{4,3,2,1,0:T(8,128)(2,1)S(1)} %collective-permute-done.6.refs_1_), channel_id=1, source_target_pairs={{0,192},{1,193},{2,194},{3,195},{32,35},{33,32},{34,33},{35,34},{6... | collective-permute-start | bytes 1572872 | tf_op jit(solution)/shard_map/ppermute | solution.py:571
  75.6 0.1 collective-permute-done.4.refs_0_
  75.8 0.0 collective-permute-start.5
  75.8 0.0 copy-start.2
  75.8 0.0 copy-start.3
  75.8 2.9 %shard_map.154 = (f32[256,1024]{1,0:T(8,128)S(1)}, bf16[4,4,16,128]{3,2,1,0:T(8,128)(2,1)S(1)}, f32[256,128]{1,0:T(8,128)S(1)}) custom-call(bf16[2,8,4,32,128]{4,3,2,1,0:T(8,128)(2,1)S(1)} %collective-permute-done.4.refs_0_, bf16[2,8,4,32,128]{4,3,2,1,0:T(8,128)(2,1)S(1)} %collective-permute-done.6.refs_1_, f32[64,128]{1,0:T(8,128)S(1)} %get-tuple-element.44.refs_2_, ...), custom_call_target="tpu_custom_call" | custom-call | flops 1073741824 | bytes 7340032 | tf_op jit(solution)/shard_map/pallas_call | solution.py:401
  78.7 3.0 %collective-permute-done.9.refs_0_ = bf16[2,8,4,32,128]{4,3,2,1,0:T(8,128)(2,1)S(1)} collective-permute-done((bf16[2,8,4,32,128]{4,3,2,1,0:T(8,128)(2,1)S(1)}, bf16[2,8,4,32,128]{4,3,2,1,0:T(8,128)(2,1)S(1)}, u32[]{:S(2)}, u32[]{:S(2)}) %collective-permute-start.9) | collective-permute-done | bytes 524320 | tf_op jit(solution)/shard_map/ppermute | solution.py:571
  81.7 0.0 collective-permute-done.10.refs_1_
  81.7 0.0 copy-done.2
  81.7 0.0 copy-done.3
  81.7 3.2 %shard_map.155 = (f32[256,1024]{1,0:T(8,128)S(1)}, bf16[4,4,16,128]{3,2,1,0:T(8,128)(2,1)S(1)}, f32[256,128]{1,0:T(8,128)S(1)}, bf16[2048,512]{1,0:T(8,128)(2,1)...) custom-call(bf16[2,8,4,32,128]{4,3,2,1,0:T(8,128)(2,1)S(1)} %collective-permute-done.9.refs_0_, ...), custom_call_target="tpu_custom_call" | custom-call | flops 1073741824 | bytes 7340032 | tf_op jit(solution)/shard_map/pallas_call | solution.py:401
  84.9 0.2 collective-permute-done.7.refs_1_
  85.2 2.1 %collective-permute-done.5.refs_0_ = bf16[2,8,4,32,128]{4,3,2,1,0:T(8,128)(2,1)S(1)} collective-permute-done((bf16[2,8,4,32,128]{4,3,2,1,0:T(8,128)(2,1)S(1)}, bf16[2,8,4,32,128]{4,3,2,1,0:T(8,128)(2,1)S(1)}, u32[]{:S(2)}, u32[]{:S(2)}) %collective-permute-start.5) | collective-permute-done | bytes 524320 | tf_op jit(solution)/shard_map/ppermute | solution.py:571
  87.3 0.0 copy-start
  87.3 1.8 %shard_map.156 = (f32[256,1024]{1,0:T(8,128)S(1)}, bf16[4,4,16,128]{3,2,1,0:T(8,128)(2,1)S(1)}, f32[256,128]{1,0:T(8,128)S(1)}, f32[2,128]{1,0:T(2,128)S(1)}) custom-call(bf16[2,8,4,32,128]{4,3,2,1,0:T(8,128)(2,1)S(1)} %collective-permute-done.5.refs_0_, bf16[2,8,4,32,128]{4,3,2,1,0:T(8,128)(2,1)S(1)} %collective-permute-done.7.refs_1_, ...), custom_call_target="tpu_custom_call" | custom-call | flops 1073741824 | bytes 7340032 | tf_op jit(solution)/shard_map/pallas_call | solution.py:401
  89.1 16.6 %all_to_all.28 = f32[128,2,128]{2,1,0:T(2,128)S(1)} all-to-all(f32[128,2,128]{2,1,0:T(2,128)S(1)} %bitcast.22), channel_id=1, replica_groups=mesh['x'=4,'core'=2,'tensor'=8,'rep'=4] {'x','tensor','rep'}, dimensions={0} | all-to-all | bytes 262144 | tf_op jit(solution)/shard_map/all_to_all | solution.py:591
  105.7 0.0 copy-done
  105.8 1.3 shard_map.157
  107.1 17.4 %all_to_all.29 = f32[128,4,128]{2,1,0:T(4,128)S(1)} all-to-all(f32[128,4,128]{2,1,0:T(4,128)S(1)} %bitcast.21), channel_id=1, replica_groups=mesh['x'=4,'core'=2,'tensor'=8,'rep'=4] {'x','tensor','rep'}, dimensions={0} | all-to-all | bytes 524288 | tf_op jit(solution)/shard_map/all_to_all | solution.py:594
  124.5 0.1 shard_map.158.own_ref
  124.6 10.6 %collective-permute-start.11 = (f32[2,128]{1,0:T(2,128)S(1)}, f32[2,128]{1,0:T(2,128)S(1)}, u32[]{:S(2)}, u32[]{:S(2)}) collective-permute-start(f32[2,128]{1,0:T(2,128)S(1)} %shard_map.158.own_ref), channel_id=1, source_target_pairs={{0,32},{32,0},{1,33},{33,1},{2,34},{34,2},{3,35},{35,3},{4,36},{36... | collective-permute-start | bytes 3080 | tf_op jit(solution)/shard_map/ppermute | solution.py:245
  135.2 0.8 collective-permute-done.11.peer_ref
  136.0 0.7 shard_map.159
  (3 shorter events, 0.1 us)
Async XLA Ops:
  0.6 7.2 %collective-permute-start = (bf16[1024,256]{1,0:T(8,128)(2,1)}, bf16[1024,256]{1,0:T(8,128)(2,1)S(1)}, u32[]{:S(2)}, u32[]{:S(2)}) collective-permute-start(bf16[1024,256]{1,0:T(8,128)(2,1)} %mix.1), channel_id=1, source_target_pairs={{0,32},{32,0},{1,33},{33,1},{2,34},{34,2},{3,35},{35,3},{4,36},{36... | collective-permute-start | bytes 1572872 | tf_op jit(solution)/shard_map/ppermute | solution.py:245
  4.0 20.6 %copy-start.1 = (bf16[1024]{0:T(1024)(128)(2,1)S(1)}, bf16[1024]{0:T(1024)(128)(2,1)}, u32[]{:S(2)}) copy-start(bf16[1024]{0:T(1024)(128)(2,1)} %param.21) | copy-start | bytes 6148
  7.8 59.3 %collective-permute-start.8 = (bf16[8192,512]{1,0:T(8,128)(2,1)}, bf16[8192,512]{1,0:T(8,128)(2,1)S(1)}, u32[]{:S(2)}, u32[]{:S(2)}) collective-permute-start(bf16[8192,512]{1,0:T(8,128)(2,1)} %refs_3_.3), channel_id=1, source_target_pairs={{0,32},{32,0},{1,33},{33,1},{2,34},{34,2},{3,35},{35,3},{4,36},{36... | collective-permute-start | bytes 25165832 | tf_op jit(solution)/shard_map/ppermute | solution.py:245
  54.6 5.2 %collective-permute-start.3 = (bf16[8,4,32,128]{3,2,1,0:T(8,128)(2,1)S(1)}, bf16[8,4,32,128]{3,2,1,0:T(8,128)(2,1)S(1)}, u32[]{:S(2)}, u32[]{:S(2)}) collective-permute-start(bf16[8,4,32,128]{3,2,1,0:T(8,128)(2,1)S(1)} %bitcast.16), channel_id=1, source_target_pairs={{0,3},{1,0},{2,1},{3,2},{32,224},{33,225},{34,226},{35,227},{64,67... | collective-permute-start | bytes 786440 | tf_op jit(solution)/shard_map/ppermute | solution.py:570
  55.7 6.8 %collective-permute-start.2 = (bf16[8,4,32,128]{3,2,1,0:T(8,128)(2,1)S(1)}, bf16[8,4,32,128]{3,2,1,0:T(8,128)(2,1)S(1)}, u32[]{:S(2)}, u32[]{:S(2)}) collective-permute-start(bf16[8,4,32,128]{3,2,1,0:T(8,128)(2,1)S(1)} %bitcast.17), channel_id=1, source_target_pairs={{0,2},{1,3},{2,0},{3,1},{32,160},{33,161},{34,162},{35,163},{64,66... | collective-permute-start | bytes 786440 | tf_op jit(solution)/shard_map/ppermute | solution.py:570
  56.6 8.8 %collective-permute-start.1 = (bf16[8,4,32,128]{3,2,1,0:T(8,128)(2,1)S(1)}, bf16[8,4,32,128]{3,2,1,0:T(8,128)(2,1)S(1)}, u32[]{:S(2)}, u32[]{:S(2)}) collective-permute-start(bf16[8,4,32,128]{3,2,1,0:T(8,128)(2,1)S(1)} %bitcast.18), channel_id=1, source_target_pairs={{0,1},{1,2},{2,3},{3,0},{32,96},{33,97},{34,98},{35,99},{64,65},{6... | collective-permute-start | bytes 786440 | tf_op jit(solution)/shard_map/ppermute | solution.py:570
  65.5 8.1 %collective-permute-start.6 = (bf16[2,8,4,32,128]{4,3,2,1,0:T(8,128)(2,1)S(1)}, bf16[2,8,4,32,128]{4,3,2,1,0:T(8,128)(2,1)S(1)}, u32[]{:S(2)}, u32[]{:S(2)}) collective-permute-start(bf16[2,8,4,32,128]{4,3,2,1,0:T(8,128)(2,1)S(1)} %shard_map.152.refs_1_), channel_id=1, source_target_pairs={{0,192},{1,193},{2,194},{3,195},{32,35},{33,32},{34,33},{35,34},{6... | collective-permute-start | bytes 1572872 | tf_op jit(solution)/shard_map/ppermute | solution.py:571
  66.3 9.5 %collective-permute-start.4 = (bf16[2,8,4,32,128]{4,3,2,1,0:T(8,128)(2,1)S(1)}, bf16[2,8,4,32,128]{4,3,2,1,0:T(8,128)(2,1)S(1)}, u32[]{:S(2)}, u32[]{:S(2)}) collective-permute-start(bf16[2,8,4,32,128]{4,3,2,1,0:T(8,128)(2,1)S(1)} %shard_map.151.refs_0_), channel_id=1, source_target_pairs={{0,64},{1,65},{2,66},{3,67},{32,33},{33,34},{34,35},{35,32},{64,12... | collective-permute-start | bytes 1572872 | tf_op jit(solution)/shard_map/ppermute | solution.py:571
  69.8 11.9 %collective-permute-start.9 = (bf16[2,8,4,32,128]{4,3,2,1,0:T(8,128)(2,1)S(1)}, bf16[2,8,4,32,128]{4,3,2,1,0:T(8,128)(2,1)S(1)}, u32[]{:S(2)}, u32[]{:S(2)}) collective-permute-start(bf16[2,8,4,32,128]{4,3,2,1,0:T(8,128)(2,1)S(1)} %get-tuple-element.46), channel_id=1, source_target_pairs={{0,64},{1,65},{2,66},{3,67},{32,33},{33,34},{34,35},{35,32},{64,12... | collective-permute-start | bytes 1572872 | tf_op jit(solution)/shard_map/ppermute | solution.py:571
  70.6 11.1 %collective-permute-start.10 = (bf16[2,8,4,32,128]{4,3,2,1,0:T(8,128)(2,1)S(1)}, bf16[2,8,4,32,128]{4,3,2,1,0:T(8,128)(2,1)S(1)}, u32[]{:S(2)}, u32[]{:S(2)}) collective-permute-start(bf16[2,8,4,32,128]{4,3,2,1,0:T(8,128)(2,1)S(1)} %get-tuple-element.47), channel_id=1, source_target_pairs={{0,192},{1,193},{2,194},{3,195},{32,35},{33,32},{34,33},{35,34},{6... | collective-permute-start | bytes 1572872 | tf_op jit(solution)/shard_map/ppermute | solution.py:571
  73.6 11.5 %collective-permute-start.7 = (bf16[2,8,4,32,128]{4,3,2,1,0:T(8,128)(2,1)S(1)}, bf16[2,8,4,32,128]{4,3,2,1,0:T(8,128)(2,1)S(1)}, u32[]{:S(2)}, u32[]{:S(2)}) collective-permute-start(bf16[2,8,4,32,128]{4,3,2,1,0:T(8,128)(2,1)S(1)} %collective-permute-done.6.refs_1_), channel_id=1, source_target_pairs={{0,192},{1,193},{2,194},{3,195},{32,35},{33,32},{34,33},{35,34},{6... | collective-permute-start | bytes 1572872 | tf_op jit(solution)/shard_map/ppermute | solution.py:571
  75.8 11.5 %collective-permute-start.5 = (bf16[2,8,4,32,128]{4,3,2,1,0:T(8,128)(2,1)S(1)}, bf16[2,8,4,32,128]{4,3,2,1,0:T(8,128)(2,1)S(1)}, u32[]{:S(2)}, u32[]{:S(2)}) collective-permute-start(bf16[2,8,4,32,128]{4,3,2,1,0:T(8,128)(2,1)S(1)} %collective-permute-done.4.refs_0_), channel_id=1, source_target_pairs={{0,64},{1,65},{2,66},{3,67},{32,33},{33,34},{34,35},{35,32},{64,12... | collective-permute-start | bytes 1572872 | tf_op jit(solution)/shard_map/ppermute | solution.py:571
  75.8 5.9 %copy-start.2 = (f32[512]{0:T(512)S(1)}, f32[512]{0:T(512)}, u32[]{:S(2)}) copy-start(f32[512]{0:T(512)} %param.23) | copy-start | bytes 6148
  75.8 5.9 %copy-start.3 = (s32[512]{0:T(512)S(1)}, s32[512]{0:T(512)}, u32[]{:S(2)}) copy-start(s32[512]{0:T(512)} %param.25) | copy-start | bytes 6148
  87.3 18.4 %copy-start = (f32[512]{0:T(512)S(1)}, f32[512]{0:T(512)}, u32[]{:S(2)}) copy-start(f32[512]{0:T(512)} %param.24) | copy-start | bytes 6148
  124.6 11.4 %collective-permute-start.11 = (f32[2,128]{1,0:T(2,128)S(1)}, f32[2,128]{1,0:T(2,128)S(1)}, u32[]{:S(2)}, u32[]{:S(2)}) collective-permute-start(f32[2,128]{1,0:T(2,128)S(1)} %shard_map.158.own_ref), channel_id=1, source_target_pairs={{0,32},{32,0},{1,33},{33,1},{2,34},{34,2},{3,35},{35,3},{4,36},{36... | collective-permute-start | bytes 3080 | tf_op jit(solution)/shard_map/ppermute | solution.py:245
